TPU v7x, 32 devices: a whole 2x2x4 slice. The times are simulated.
32 devices in a mesh: dp: 4 (over y, x), seq: 4 (over z), tensor: 2 (over core).
Axes of the slice: x: 2, y: 2, z: 4, core: 2. Of those that a mesh axis runs over, the one named last changes fastest.
Arguments:
- tokens: bfloat16 [4, 2048, 2048], P('dp', ('seq', 'tensor')), may hold values from -6 to 6
- lengths: int32 [4, 6], P('dp'), may hold values from 1 to 2043, as said below
- ln1_gain: float32 [2048], replicated, may hold values from 0.5 to 1.5
- ln1_bias: float32 [2048], replicated, may hold values from -4 to 4
- w_query: bfloat16 [2048, 2048], P(None, 'tensor'), may hold values from -0.1875 to 0.1875
- b_query: float32 [16, 128], P('tensor'), may hold values from -6 to 6
- w_key: bfloat16 [2048, 128], replicated, may hold values from -0.1875 to 0.1875
- w_value: bfloat16 [2048, 128], replicated, may hold values from -0.125 to 0.125
- b_value: float32 [128], replicated, may hold values from -6 to 6
- w_out: bfloat16 [2048, 2048], P('tensor'), may hold values from -1 to 1
- b_out: float32 [2048], replicated, may hold values from -4 to 4
- ln2_gain: float32 [2048], replicated, may hold values from 0.5 to 1.5
- ln2_bias: float32 [2048], replicated, may hold values from -4 to 4
- w_up: bfloat16 [2048, 8192], P(None, 'tensor'), may hold values from -0.125 to 0.125
- b_up: float32 [64, 128], P('tensor'), may hold values from -6 to 6
- w_down: bfloat16 [8192, 2048], P('tensor'), may hold values from -0.0625 to 0.0625
- b_down: float32 [2048], replicated, may hold values from -4 to 4
- cotangent: bfloat16 [4, 2048, 2048], P('dp', ('seq', 'tensor')), may hold values from -6 to 6
Outputs:
- output: bfloat16 [4, 2048, 2048], P('dp', ('seq', 'tensor'))
- grad_input: bfloat16 [4, 2048, 2048], P('dp', ('seq', 'tensor'))
- grad_ln1_gain: float32 [2048], P(('dp', 'seq', 'tensor'))
- grad_ln1_bias: float32 [2048], P(('dp', 'seq', 'tensor'))
- grad_w_query: float32 [2048, 2048], P(('dp', 'seq'), 'tensor')
- grad_b_query: float32 [16, 128], P('tensor', ('dp', 'seq'))
- grad_w_key: float32 [2048, 128], P(('dp', 'seq', 'tensor'))
- grad_w_value: float32 [2048, 128], P(('dp', 'seq', 'tensor'))
- grad_b_value: float32 [128], P(('dp', 'seq', 'tensor'))
- grad_w_out: float32 [2048, 2048], P('tensor', ('dp', 'seq'))
- grad_b_out: float32 [2048], P(('dp', 'seq', 'tensor'))
- grad_ln2_gain: float32 [2048], P(('dp', 'seq', 'tensor'))
- grad_ln2_bias: float32 [2048], P(('dp', 'seq', 'tensor'))
- grad_w_up: float32 [2048, 8192], P(('dp', 'seq'), 'tensor')
- grad_b_up: float32 [64, 128], P('tensor', ('dp', 'seq'))
- grad_w_down: float32 [8192, 2048], P('tensor', ('dp', 'seq'))
- grad_b_down: float32 [2048], P(('dp', 'seq', 'tensor'))
Inputs may be any that keep to these rules, and one draw needn't show every extreme that they name: Each window's lengths are positive and sum to 2048; one of them, at a position drawn for each window, is larger than 1536, and each other one is at most (511) // 5. In one window, drawn from the seed, every other length is 1.
All inputs are finite; a program needn't handle non-finite values.
Results may differ from a plain program's by a relative error of at most 0.017.
Values may be sent and summed in bfloat16 or wider, within the bound.
No kernel may reach another device: no remote copies, remote signals or barrier semaphores. Data moves between devices by JAX's collectives and lax.ppermute only.
A program may use at most 256 MiB of HBM per device.

v0:
```python
import jax
import jax.numpy as jnp
from jax import lax
from jax.sharding import PartitionSpec as P

epsilon = 1e-05
negative = -1e30


def norm_rows(rows, gain, shift):
    centre = rows - jnp.mean(rows, axis=-1, keepdims=True)
    spread = jnp.mean(centre * centre, axis=-1, keepdims=True)
    return centre * lax.rsqrt(spread + epsilon) * gain + shift


def gelu_tanh(value):
    return jax.nn.gelu(value, approximate=True)


def contract_rows(left, right):
    return lax.dot_general(
        left, right, (((0,), (0,)), ((), ())), preferred_element_type=jnp.float32
    )


def contract_cols(left, right):
    return lax.dot_general(
        left, right, (((1,), (1,)), ((), ())), preferred_element_type=jnp.float32
    )


def on_device(
    tokens,
    lengths,
    ln1_gain,
    ln1_bias,
    w_query,
    b_query,
    w_key,
    w_value,
    b_value,
    w_out,
    b_out,
    ln2_gain,
    ln2_bias,
    w_up,
    b_up,
    w_down,
    b_down,
    cotangent,
):
    shard = tokens[0].astype(jnp.float32)
    rows_own = shard.shape[0]
    rows_span = rows_own * lax.axis_size("tensor")
    window = rows_span * lax.axis_size("seq")
    heads_local = b_query.shape[0]
    head_dim = b_query.shape[1]
    scale = head_dim ** (-0.5)
    block = min(512, window)
    span_start = lax.axis_index("seq") * rows_span
    ends = jnp.cumsum(lengths[0], dtype=jnp.int32)
    positions = jnp.arange(window, dtype=jnp.int32)
    segment = jnp.sum((positions[:, None] >= ends[None, :]).astype(jnp.int32), axis=1)
    query_pos = span_start + jnp.arange(rows_span, dtype=jnp.int32)
    query_seg = lax.dynamic_slice_in_dim(segment, span_start, rows_span)
    block_count = (span_start + rows_span + block - 1) // block
    normed_low = norm_rows(shard, ln1_gain, ln1_bias).astype(jnp.bfloat16)
    key_own = jnp.dot(normed_low, w_key, preferred_element_type=jnp.float32).astype(jnp.bfloat16)
    value_own = (jnp.dot(normed_low, w_value, preferred_element_type=jnp.float32) + b_value).astype(
        jnp.bfloat16
    )
    keys, values = (
        lax.all_gather(key_own, ("seq", "tensor"), axis=0, tiled=True),
        lax.all_gather(value_own, ("seq", "tensor"), axis=0, tiled=True),
    )
    normed_all = lax.all_gather(normed_low, "tensor", axis=0, tiled=True)
    query = (
        jnp.dot(normed_all, w_query, preferred_element_type=jnp.float32) + b_query.reshape(-1)
    ).astype(jnp.bfloat16)
    query3 = query.reshape(rows_span, heads_local, head_dim)

    def block_scores(index):
        start = index * block
        key_block = lax.dynamic_slice_in_dim(keys, start, block)
        value_block = lax.dynamic_slice_in_dim(values, start, block)
        key_pos = start + jnp.arange(block, dtype=jnp.int32)
        key_seg = lax.dynamic_slice_in_dim(segment, start, block)
        allowed = (key_pos[None, :] <= query_pos[:, None]) & (
            key_seg[None, :] == query_seg[:, None]
        )
        scores = (
            jnp.einsum("rhd,kd->rhk", query3, key_block, preferred_element_type=jnp.float32) * scale
        )
        return (scores, allowed[:, None, :], start, key_block, value_block)

    def max_step(index, carry):
        highest, total = carry
        scores, allowed, start, key_block, value_block = block_scores(index)
        scores = jnp.where(allowed, scores, negative)
        new_high = jnp.maximum(highest, jnp.max(scores, axis=2))
        weights = jnp.where(allowed, jnp.exp(scores - new_high[..., None]), 0.0)
        total = total * jnp.exp(highest - new_high) + jnp.sum(weights, axis=2)
        return (new_high, total)

    start_state = (
        jnp.full((rows_span, heads_local), negative, jnp.float32),
        jnp.zeros((rows_span, heads_local), jnp.float32),
    )
    highest, total = lax.fori_loop(0, block_count, max_step, start_state)
    log_total = highest + jnp.log(total)

    def block_probs(index):
        scores, allowed, start, key_block, value_block = block_scores(index)
        probs = jnp.where(allowed, jnp.exp(scores - log_total[..., None]), 0.0)
        return (probs, start, key_block, value_block)

    def out_step(index, running):
        probs, start, key_block, value_block = block_probs(index)
        return running + jnp.einsum(
            "rhk,kd->rhd",
            probs.astype(jnp.bfloat16),
            value_block,
            preferred_element_type=jnp.float32,
        )

    attended = lax.fori_loop(
        0, block_count, out_step, jnp.zeros((rows_span, heads_local, head_dim), jnp.float32)
    )
    attended_low = attended.reshape(rows_span, heads_local * head_dim).astype(jnp.bfloat16)
    middle = shard + (
        lax.psum_scatter(
            jnp.dot(attended_low, w_out, preferred_element_type=jnp.float32).astype(jnp.bfloat16),
            "tensor",
            scatter_dimension=0,
            tiled=True,
        ).astype(jnp.float32)
        + b_out
    )
    normed_two = norm_rows(middle, ln2_gain, ln2_bias).astype(jnp.bfloat16)
    normed_two_all = lax.all_gather(normed_two, "tensor", axis=0, tiled=True)
    hidden = jnp.dot(normed_two_all, w_up, preferred_element_type=jnp.float32) + b_up.reshape(-1)
    activated, gelu_pull = jax.vjp(gelu_tanh, hidden)
    activated_low = activated.astype(jnp.bfloat16)
    result = middle + (
        lax.psum_scatter(
            jnp.dot(activated_low, w_down, preferred_element_type=jnp.float32).astype(jnp.bfloat16),
            "tensor",
            scatter_dimension=0,
            tiled=True,
        ).astype(jnp.float32)
        + b_down
    )
    output = result.astype(jnp.bfloat16)[None]
    grad_out = cotangent[0].astype(jnp.float32)
    grad_out_low = cotangent[0]
    grad_out_all = lax.all_gather(grad_out_low, "tensor", axis=0, tiled=True)
    grad_w_down = contract_rows(activated_low, grad_out_all)
    grad_b_down = jnp.sum(grad_out, axis=0)
    grad_act = contract_cols(grad_out_all, w_down)
    grad_hidden = gelu_pull(grad_act)[0].astype(jnp.bfloat16)
    grad_w_up = contract_rows(normed_two_all, grad_hidden)
    grad_b_up = jnp.sum(grad_hidden.astype(jnp.float32), axis=0).reshape(b_up.shape)
    grad_normed_two = lax.psum_scatter(
        contract_cols(grad_hidden, w_up).astype(jnp.bfloat16),
        "tensor",
        scatter_dimension=0,
        tiled=True,
    ).astype(jnp.float32)
    norm_two_unused, norm_two_pull = jax.vjp(norm_rows, middle, ln2_gain, ln2_bias)
    grad_from_norm, grad_ln2_gain, grad_ln2_bias = norm_two_pull(grad_normed_two)
    grad_middle = grad_out + grad_from_norm
    grad_branch = grad_middle.astype(jnp.bfloat16)
    grad_b_out = jnp.sum(grad_branch.astype(jnp.float32), axis=0)
    grad_branch_all = lax.all_gather(grad_branch, "tensor", axis=0, tiled=True)
    grad_w_out = contract_rows(attended_low, grad_branch_all)
    grad_attended = (
        contract_cols(grad_branch_all, w_out)
        .astype(jnp.bfloat16)
        .reshape(rows_span, heads_local, head_dim)
    )

    def inner_step(index, running):
        probs, start, key_block, value_block = block_probs(index)
        grad_probs = jnp.einsum(
            "rhd,kd->rhk", grad_attended, value_block, preferred_element_type=jnp.float32
        )
        return running + jnp.sum(grad_probs * probs, axis=2)

    inner = lax.fori_loop(
        0, block_count, inner_step, jnp.zeros((rows_span, heads_local), jnp.float32)
    )

    def grad_step(index, carry):
        grad_query, grad_keys, grad_values = carry
        probs, start, key_block, value_block = block_probs(index)
        grad_probs = jnp.einsum(
            "rhd,kd->rhk", grad_attended, value_block, preferred_element_type=jnp.float32
        )
        grad_scores = (probs * (grad_probs - inner[..., None])).astype(jnp.bfloat16)
        grad_query = (
            grad_query
            + jnp.einsum("rhk,kd->rhd", grad_scores, key_block, preferred_element_type=jnp.float32)
            * scale
        )
        key_part = (
            jnp.einsum("rhk,rhd->kd", grad_scores, query3, preferred_element_type=jnp.float32)
            * scale
        )
        value_part = jnp.einsum(
            "rhk,rhd->kd",
            probs.astype(jnp.bfloat16),
            grad_attended,
            preferred_element_type=jnp.float32,
        )
        grad_keys = lax.dynamic_update_slice_in_dim(
            grad_keys, lax.dynamic_slice_in_dim(grad_keys, start, block) + key_part, start, 0
        )
        grad_values = lax.dynamic_update_slice_in_dim(
            grad_values, lax.dynamic_slice_in_dim(grad_values, start, block) + value_part, start, 0
        )
        return (grad_query, grad_keys, grad_values)

    empty_kv = jnp.zeros((window, head_dim), jnp.float32)
    grad_query, grad_keys, grad_values = lax.fori_loop(
        0,
        block_count,
        grad_step,
        (jnp.zeros((rows_span, heads_local, head_dim), jnp.float32), empty_kv, empty_kv),
    )
    key_sum, value_sum = (
        lax.psum_scatter(
            grad_keys.astype(jnp.bfloat16), ("seq", "tensor"), scatter_dimension=0, tiled=True
        ).astype(jnp.float32),
        lax.psum_scatter(
            grad_values.astype(jnp.bfloat16), ("seq", "tensor"), scatter_dimension=0, tiled=True
        ).astype(jnp.float32),
    )
    key_low = key_sum.astype(jnp.bfloat16)
    value_low = value_sum.astype(jnp.bfloat16)
    query_low = grad_query.reshape(rows_span, heads_local * head_dim).astype(jnp.bfloat16)
    grad_w_query = contract_rows(normed_all, query_low)
    grad_b_query = jnp.sum(query_low.astype(jnp.float32), axis=0).reshape(b_query.shape)
    grad_w_key = contract_rows(normed_low, key_low)
    grad_w_value = contract_rows(normed_low, value_low)
    grad_b_value = jnp.sum(value_low.astype(jnp.float32), axis=0)
    grad_normed = (
        lax.psum_scatter(
            contract_cols(query_low, w_query).astype(jnp.bfloat16),
            "tensor",
            scatter_dimension=0,
            tiled=True,
        ).astype(jnp.float32)
        + contract_cols(key_low, w_key)
        + contract_cols(value_low, w_value)
    )
    norm_one_unused, norm_one_pull = jax.vjp(norm_rows, shard, ln1_gain, ln1_bias)
    grad_shard, grad_ln1_gain, grad_ln1_bias = norm_one_pull(grad_normed)
    grad_input = (grad_middle + grad_shard).astype(jnp.bfloat16)[None]
    small = (
        lax.psum_scatter(grad_w_key, ("dp", "seq", "tensor"), scatter_dimension=0, tiled=True),
        lax.psum_scatter(grad_w_value, ("dp", "seq", "tensor"), scatter_dimension=0, tiled=True),
        lax.psum_scatter(grad_b_value, ("dp", "seq", "tensor"), scatter_dimension=0, tiled=True),
        lax.psum_scatter(grad_ln1_gain, ("dp", "seq", "tensor"), scatter_dimension=0, tiled=True),
        lax.psum_scatter(grad_ln1_bias, ("dp", "seq", "tensor"), scatter_dimension=0, tiled=True),
        lax.psum_scatter(grad_b_out, ("dp", "seq", "tensor"), scatter_dimension=0, tiled=True),
        lax.psum_scatter(grad_ln2_gain, ("dp", "seq", "tensor"), scatter_dimension=0, tiled=True),
        lax.psum_scatter(grad_ln2_bias, ("dp", "seq", "tensor"), scatter_dimension=0, tiled=True),
        lax.psum_scatter(grad_b_down, ("dp", "seq", "tensor"), scatter_dimension=0, tiled=True),
    )
    sum_w_query, sum_b_query, sum_w_out, sum_w_up, sum_b_up, sum_w_down = (
        lax.psum_scatter(grad_w_query, ("dp", "seq"), scatter_dimension=0, tiled=True),
        lax.psum_scatter(grad_b_query, ("dp", "seq"), scatter_dimension=1, tiled=True),
        lax.psum_scatter(grad_w_out, ("dp", "seq"), scatter_dimension=1, tiled=True),
        lax.psum_scatter(grad_w_up, ("dp", "seq"), scatter_dimension=0, tiled=True),
        lax.psum_scatter(grad_b_up, ("dp", "seq"), scatter_dimension=1, tiled=True),
        lax.psum_scatter(grad_w_down, ("dp", "seq"), scatter_dimension=1, tiled=True),
    )
    return (
        output,
        grad_input,
        small[3],
        small[4],
        sum_w_query,
        sum_b_query,
        small[0],
        small[1],
        small[2],
        sum_w_out,
        small[5],
        small[6],
        small[7],
        sum_w_up,
        sum_b_up,
        sum_w_down,
        small[8],
    )


def solution(mesh):
    in_specs = (
        P("dp", ("seq", "tensor"), None),
        P("dp", None),
        P(),
        P(),
        P(None, "tensor"),
        P("tensor", None),
        P(),
        P(),
        P(),
        P("tensor", None),
        P(),
        P(),
        P(),
        P(None, "tensor"),
        P("tensor", None),
        P("tensor", None),
        P(),
        P("dp", ("seq", "tensor"), None),
    )
    out_specs = (
        P("dp", ("seq", "tensor"), None),
        P("dp", ("seq", "tensor"), None),
        P(("dp", "seq", "tensor")),
        P(("dp", "seq", "tensor")),
        P(("dp", "seq"), "tensor"),
        P("tensor", ("dp", "seq")),
        P(("dp", "seq", "tensor"), None),
        P(("dp", "seq", "tensor"), None),
        P(("dp", "seq", "tensor")),
        P("tensor", ("dp", "seq")),
        P(("dp", "seq", "tensor")),
        P(("dp", "seq", "tensor")),
        P(("dp", "seq", "tensor")),
        P(("dp", "seq"), "tensor"),
        P("tensor", ("dp", "seq")),
        P("tensor", ("dp", "seq")),
        P(("dp", "seq", "tensor")),
    )
    return jax.shard_map(
        on_device, mesh=mesh, in_specs=in_specs, out_specs=out_specs, check_vma=False
    )
```

profile of v0, /device:TPU:0, one launch (start us, length us, event | category | flops | bytes accessed | tf_op | source)
XLA Modules:
  0.0 2414.5 jit_solution(3729939861865298722)
XLA Ops:
  7.3 1.5 convert_reduce_fusion.3
  8.9 1.7 fusion.91
  11.7 1.4 fusion.88
  13.6 1.7 convolution_convert_fusion.5
  15.3 16.6 all_gather.18
  32.3 15.8 all_gather.20
  48.1 5.2 fusion.104
  53.5 4.0 while.50
  53.9 1.5 fusion.191
  55.4 2.0 select_reduce_fusion.2
  57.5 1.5 broadcast.267.clone
  59.0 5.8 while.51
  59.3 5.2 fusion.196
  64.8 2.6 copy.65
  67.4 6.2 convolution_convert_fusion.1
  73.7 39.6 %reduce-scatter.15.cloned.1.call-done = bf16[256,2048]{1,0:T(8,128)(2,1)} async-done(((bf16[512,2048]{1,0:T(8,128)(2,1)}), bf16[256,2048]{1,0:T(8,128)(2,1)}) %reduce-scatter.15.cloned.1.call-update) | async-done | bytes 1048592 | tf_op jit(solution)/shard_map/reduce_scatter | solution.py:131
  113.3 1.7 fusion.102
  115.7 1.7 add_convert_fusion.2
  118.0 11.3 all-gather.8.cloned.1.call-done
  129.2 15.0 fusion.115
  144.2 21.1 convert_reduce_fusion
  165.3 15.1 convolution_convert_fusion.2
  180.5 17.7 convolution_convert_fusion.3
  198.2 3.2 fusion.94
  201.4 7.7 reduce-scatter.17.cloned.1.call-done
  209.1 4.0 fusion.114
  213.1 2.2 convert_reduce_fusion.4
  215.6 11.7 all-gather.10.cloned.1.call-done
  227.3 5.2 fusion.103
  232.7 5.4 while.52
  233.1 2.2 fusion.201
  235.3 2.8 fusion.202
  238.1 1.1 broadcast_in_dim.114.clone
  239.2 1.0 broadcast_in_dim.114
  240.2 1.5 broadcast.267
  241.7 13.7 while.53
  242.1 1.3 fusion.213
  243.4 1.9 fusion.216
  245.3 4.0 fusion.214
  249.3 3.1 fusion.215
  252.4 1.6 multiply_add_fusion.7
  253.9 1.3 copy-done.4
  255.5 2.2 convert_element_type.141
  258.6 1.8 copy.70
  260.4 6.3 convolution_convert_fusion
  266.8 79.9 %reduce-scatter.25.cloned.1.call-done = bf16[256,128]{1,0:T(8,128)(2,1)} async-done(((bf16[2048,128]{1,0:T(8,128)(2,1)}), bf16[256,128]{1,0:T(8,128)(2,1)}) %reduce-scatter.25.cloned.1.call-update) | async-done | bytes 65552 | tf_op jit(solution)/shard_map/reduce_scatter | solution.py:234
  346.7 2.4 fusion.118
  349.1 29.5 %reduce-scatter.23.cloned.1.call-done = bf16[256,128]{1,0:T(8,128)(2,1)} async-done(((bf16[2048,128]{1,0:T(8,128)(2,1)}), bf16[256,128]{1,0:T(8,128)(2,1)}) %reduce-scatter.23.cloned.1.call-update) | async-done | bytes 65552 | tf_op jit(solution)/shard_map/reduce_scatter | solution.py:231
  378.6 2.3 fusion.117
  381.0 7.2 fusion.116
  388.3 1.2 copy-done.19
  389.4 7.2 fusion.119
  397.4 19.5 fusion.95
  416.9 17.9 fusion.120
  437.1 74.5 %all-reduce.10 = (f32[8,128]{1,0:T(8,128)S(1)}, f32[32,128]{1,0:T(8,128)S(1)}) all-reduce(f32[8,128]{1,0:T(8,128)S(1)} %convert_reduce_fusion.5, f32[32,128]{1,0:T(8,128)S(1)} %bitcast.281), channel_id=12, replica_groups=mesh['dp'=4,'seq'=4,'tensor'=2] {'dp','seq'}, use_global_device_ids=true, to_apply=%region_33.34.clone | all-reduce | flops 5120 | bytes 40960
  513.1 1.7 convolution_add_fusion.1
  515.7 1.3 copy-done.9
  517.9 37.9 %all-reduce.9 = (f32[2048]{0:T(1024)S(1)}, f32[2048]{0:T(1024)S(1)}, f32[128]{0:T(128)S(1)}, f32[2048]{0:T(1024)S(1)}, f32[2048]{0:T(1024)S(1)}, /*index=5*/f32[2048]{0:T(1024)S(1)}, f32[2048]{0:T(1024)S(1)}) all-reduce(f32[2048]{0:T(1024)S(1)} %get-tuple-element.572, ...), channel_id=9, replica_groups=mesh['dp'=4,'seq'=4,'tensor'=2] {'dp','seq','tensor'}, use_global_device_ids=true, to_apply=%region_28.29.clone | all-reduce | flops 12416 | bytes 99328
  559.9 4.1 fusion.108
  564.0 98.0 %reduce-scatter.29.cloned.1.call-done = f32[64,128]{1,0:T(8,128)} async-done(((f32[2048,128]{1,0:T(8,128)}), f32[64,128]{1,0:T(8,128)}) %reduce-scatter.29.cloned.1.call-update) | async-done | bytes 32784 | tf_op jit(solution)/shard_map/reduce_scatter | solution.py:260
  662.1 181.3 %reduce-scatter.27.cloned.1.call-done = f32[128,1024]{1,0:T(8,128)} async-done(((f32[2048,1024]{1,0:T(8,128)}), f32[128,1024]{1,0:T(8,128)}) %reduce-scatter.27.cloned.1.call-update) | async-done | bytes 524304 | tf_op jit(solution)/shard_map/reduce_scatter | solution.py:271
  843.4 182.6 %reduce-scatter.33.cloned.1.call-done = f32[1024,128]{1,0:T(8,128)} async-done(((f32[1024,2048]{1,0:T(8,128)}), f32[1024,128]{1,0:T(8,128)}) %reduce-scatter.33.cloned.1.call-update) | async-done | bytes 524304 | tf_op jit(solution)/shard_map/reduce_scatter | solution.py:273
  1025.9 690.0 %reduce-scatter.37.cloned.1.call-done = f32[4096,128]{1,0:T(8,128)} async-done(((f32[4096,2048]{1,0:T(8,128)}), f32[4096,128]{1,0:T(8,128)}) %reduce-scatter.37.cloned.1.call-update) | async-done | bytes 2097168 | tf_op jit(solution)/shard_map/reduce_scatter | solution.py:276
  1716.0 691.5 %reduce-scatter.35.cloned.1.call-done = f32[128,4096]{1,0:T(8,128)} async-done(((f32[2048,4096]{1,0:T(8,128)}), f32[128,4096]{1,0:T(8,128)}) %reduce-scatter.35.cloned.1.call-update) | async-done | bytes 2097168 | tf_op jit(solution)/shard_map/reduce_scatter | solution.py:274
  (180 shorter events, 16.5 us)
Async XLA Ops:
  7.2 24.6 %copy-start = (bf16[2048,128]{1,0:T(8,128)(2,1)S(1)}, bf16[2048,128]{1,0:T(8,128)(2,1)}, u32[]{:S(2)}) copy-start(bf16[2048,128]{1,0:T(8,128)(2,1)} %param.33) | copy-start | bytes 1572868
  7.2 4.5 copy-start.1
  7.2 4.5 copy-start.23
  7.2 4.5 copy-start.38
  7.2 40.9 %all-gather.6.cloned.1.call-start = ((), (), s32[]{:S(2)}) async-start(), calls=%async_computation.12 | async-start | bytes 3145728 | tf_op jit(solution)/shard_map/all_gather | solution.py:76
  8.8 1.8 copy-start.26
  8.8 4.4 copy-start.45
  8.9 4.7 copy-start.17
  10.6 0.6 copy-start.36
  11.2 0.5 copy-start.31
  13.1 18.7 copy-start.5
  13.1 18.7 copy-start.41
  13.2 100.1 %reduce-scatter.15.cloned.1.call-start = ((), (), s32[]{:S(2)}) async-start(), calls=%async_computation.13 | async-start | bytes 3145728 | tf_op jit(solution)/shard_map/reduce_scatter | solution.py:131
  13.6 34.5 %copy-start.44 = (f32[8,128]{1,0:T(8,128)S(1)}, f32[8,128]{1,0:T(8,128)}, u32[]{:S(2)}) copy-start(f32[8,128]{1,0:T(8,128)} %param.31) | copy-start | bytes 12292
  73.6 39.7 %copy-start.22 = (f32[2048]{0:T(1024)S(1)}, f32[2048]{0:T(1024)}, u32[]{:S(2)}) copy-start(f32[2048]{0:T(1024)} %param.36) | copy-start | bytes 24580
  73.6 42.0 %copy-start.25 = (f32[2048]{0:T(1024)S(1)}, f32[2048]{0:T(1024)}, u32[]{:S(2)}) copy-start(f32[2048]{0:T(1024)} %param.37) | copy-start | bytes 24580
  73.6 42.0 %copy-start.39 = (f32[2048]{0:T(1024)S(1)}, f32[2048]{0:T(1024)}, u32[]{:S(2)}) copy-start(f32[2048]{0:T(1024)} %param.38) | copy-start | bytes 24580
  73.6 55.6 %all-gather.8.cloned.1.call-start = ((), (), s32[]{:S(2)}) async-start(), calls=%async_computation.14 | async-start | bytes 3145728 | tf_op jit(solution)/shard_map/all_gather | solution.py:140
  113.3 1.7 copy-start.7
  117.3 26.9 %all-gather.12.cloned.1.call-start = ((), (), s32[]{:S(2)}) async-start(), calls=%async_computation.27 | async-start | bytes 3145728 | tf_op jit(solution)/shard_map/all_gather | solution.py:156
  117.9 26.3 %copy-start.42 = (f32[32,128]{1,0:T(8,128)S(1)}, f32[32,128]{1,0:T(8,128)}, u32[]{:S(2)}) copy-start(f32[32,128]{1,0:T(8,128)} %param.40) | copy-start | bytes 49156
  117.9 80.3 %reduce-scatter.19.cloned.1.call-start = ((), (), s32[]{:S(2)}) async-start(), calls=%async_computation.16 | async-start | bytes 3145728 | tf_op jit(solution)/shard_map/reduce_scatter | solution.py:163
  180.4 28.7 %reduce-scatter.17.cloned.1.call-start = ((), (), s32[]{:S(2)}) async-start(), calls=%async_computation.15 | async-start | bytes 3145728 | tf_op jit(solution)/shard_map/reduce_scatter | solution.py:145
  198.1 10.9 copy-start.40
  198.2 29.2 %all-gather.10.cloned.1.call-start = ((), (), s32[]{:S(2)}) async-start(), calls=%async_computation.17 | async-start | bytes 3145728 | tf_op jit(solution)/shard_map/all_gather | solution.py:174
  209.1 4.0 copy-start.10
  213.1 2.3 copy-start.8
  213.1 2.3 copy-start.34
  215.4 131.3 %reduce-scatter.25.cloned.1.call-start = ((), (), s32[]{:S(2)}) async-start(), calls=%async_computation.20 | async-start | bytes 589824 | tf_op jit(solution)/shard_map/reduce_scatter | solution.py:234
  242.1 1.3 copy-start.15
  245.3 4.0 copy-start.16
  249.3 3.1 copy-start.3
  253.9 1.3 copy-start.4
  255.5 2.2 copy-start.12
  257.6 120.9 %reduce-scatter.23.cloned.1.call-start = ((), (), s32[]{:S(2)}) async-start(), calls=%async_computation.19 | async-start | bytes 589824 | tf_op jit(solution)/shard_map/reduce_scatter | solution.py:231
  258.6 254.5 %reduce-scatter.21.cloned.1.call-start = ((), (), s32[]{:S(2)}) async-start(), calls=%async_computation.18 | async-start | bytes 3145728 | tf_op jit(solution)/shard_map/reduce_scatter | solution.py:247
  260.4 120.6 %copy-start.13 = (bf16[512,8,128]{0,2,1:T(8,128)(2,1)}, bf16[512,8,128]{0,2,1:T(8,128)(2,1)S(1)}, u32[]{:S(2)}) copy-start(bf16[512,8,128]{0,2,1:T(8,128)(2,1)S(1)} %copy.70) | copy-start | bytes 3145732
  266.7 80.0 %copy-start.6 = (bf16[256,2048]{1,0:T(8,128)(2,1)S(1)}, bf16[256,2048]{1,0:T(8,128)(2,1)}, u32[]{:S(2)}) copy-start(bf16[256,2048]{1,0:T(8,128)(2,1)} %fusion.88) | copy-start | bytes 3145732
  266.7 297.3 %reduce-scatter.31.cloned.1.call-start = ((), (), s32[]{:S(2)}) async-start(), calls=%async_computation.23 | async-start | bytes 1081344 | tf_op jit(solution)/shard_map/reduce_scatter | solution.py:261
  349.1 313.0 %reduce-scatter.29.cloned.1.call-start = ((), (), s32[]{:S(2)}) async-start(), calls=%async_computation.22 | async-start | bytes 1081344 | tf_op jit(solution)/shard_map/reduce_scatter | solution.py:260
  380.9 462.5 %reduce-scatter.27.cloned.1.call-start = ((), (), s32[]{:S(2)}) async-start(), calls=%async_computation.21 | async-start | bytes 8912896 | tf_op jit(solution)/shard_map/reduce_scatter | solution.py:271
  388.2 1.2 copy-start.19
  388.2 637.7 %reduce-scatter.33.cloned.1.call-start = ((), (), s32[]{:S(2)}) async-start(), calls=%async_computation.24 | async-start | bytes 8912896 | tf_op jit(solution)/shard_map/reduce_scatter | solution.py:273
  396.6 0.7 copy-start.43
  396.7 1319.3 %reduce-scatter.37.cloned.1.call-start = ((), (), s32[]{:S(2)}) async-start(), calls=%async_computation.26 | async-start | bytes 35651584 | tf_op jit(solution)/shard_map/reduce_scatter | solution.py:276
  416.9 1990.6 %reduce-scatter.35.cloned.1.call-start = ((), (), s32[]{:S(2)}) async-start(), calls=%async_computation.25 | async-start | bytes 35651584 | tf_op jit(solution)/shard_map/reduce_scatter | solution.py:274
  434.8 0.7 copy-start.46
  434.8 1.9 copy-start.11
  434.8 2.1 copy-start.14
  434.8 2.3 copy-start.33
  434.8 78.2 %copy-start.20 = (bf16[256,128]{1,0:T(8,128)(2,1)S(1)}, bf16[256,128]{1,0:T(8,128)(2,1)}, u32[]{:S(2)}) copy-start(bf16[256,128]{1,0:T(8,128)(2,1)} %reduce-scatter.25.cloned.1.call-done) | copy-start | bytes 196612
  434.8 78.2 %copy-start.18 = (bf16[2048,128]{1,0:T(8,128)(2,1)S(1)}, bf16[2048,128]{1,0:T(8,128)(2,1)}, u32[]{:S(2)}) copy-start(bf16[2048,128]{1,0:T(8,128)(2,1)} %param.32) | copy-start | bytes 1572868
  434.9 78.2 %copy-start.21 = (bf16[256,128]{1,0:T(8,128)(2,1)S(1)}, bf16[256,128]{1,0:T(8,128)(2,1)}, u32[]{:S(2)}) copy-start(bf16[256,128]{1,0:T(8,128)(2,1)} %reduce-scatter.23.cloned.1.call-done) | copy-start | bytes 196612
  437.1 77.7 %copy-start.2 = (bf16[1,256,2048]{2,1,0:T(8,128)(2,1)S(1)}, bf16[1,256,2048]{2,1,0:T(8,128)(2,1)}, u32[]{:S(2)}) copy-start(bf16[1,256,2048]{2,1,0:T(8,128)(2,1)} %param.26) | copy-start | bytes 3145732
  437.1 77.7 %copy-start.24 = (f32[2048]{0:T(1024)S(1)}, f32[2048]{0:T(1024)}, u32[]{:S(2)}) copy-start(f32[2048]{0:T(1024)} %param.28) | copy-start | bytes 24580
  437.1 77.7 %copy-start.27 = (f32[256]{0:T(256)S(1)}, f32[256]{0:T(256)}, u32[]{:S(2)}) copy-start(f32[256]{0:T(256)} %copy-done.26) | copy-start | bytes 3076
  514.8 0.8 copy-start.37
  514.8 2.1 copy-start.32
  515.6 1.3 copy-start.9
  515.6 2.3 copy-start.28
  515.6 2.3 copy-start.29
  515.6 2.3 copy-start.30
  515.6 44.3 %copy-start.35 = (f32[256]{0:T(256)S(1)}, f32[256]{0:T(256)}, u32[]{:S(2)}) copy-start(f32[256]{0:T(256)} %copy-done.34) | copy-start | bytes 3076
Sparse Core Ops, SparseCore 0:
  13.3 13.2 all-gather.5
  73.7 39.5 reduce-scatter.14
  117.5 11.7 all-gather.7
  130.7 11.7 all-gather.11
  180.5 10.7 reduce-scatter.18
  198.3 10.7 reduce-scatter.16
  215.5 11.7 all-gather.9
  257.8 88.8 reduce-scatter.24
  349.5 29.0 reduce-scatter.22
  380.8 7.6 reduce-scatter.20
  391.3 136.6 reduce-scatter.30
  530.8 131.1 reduce-scatter.28
  664.9 178.4 reduce-scatter.26
  846.1 179.7 reduce-scatter.32
  1028.7 687.2 reduce-scatter.36
  1718.7 688.6 reduce-scatter.34
where the time goes:
time: 2420 us; the launch traced here: 2410 us
  waiting for transfers between devices  2020 us (83%)
  matrix products  176 us (7%)
  blocking collectives  145 us (6%)
  other arithmetic  30.1 us (1%)
    reduce_scatter x1, waiting for transfers between devices, on_device(): lax.psum_scatter(grad_w_up, ('dp', 'seq'), scatter_dimension=0, tiled=True)  691 us
    reduce_scatter x1, waiting for transfers between devices, on_device(): lax.psum_scatter(grad_w_down, ('dp', 'seq'), scatter_dimension=1, tiled=T...  690 us
    reduce_scatter x1, waiting for transfers between devices, on_device(): lax.psum_scatter(grad_w_out, ('dp', 'seq'), scatter_dimension=1, tiled=True)  183 us
    reduce_scatter x1, waiting for transfers between devices, on_device(): lax.psum_scatter(grad_w_query, ('dp', 'seq'), scatter_dimension=0, tiled=...  181 us
    unnamed x2, blocking collectives  112 us
    reduce_scatter x1, waiting for transfers between devices, on_device(): lax.psum_scatter(grad_w_key, ('dp', 'seq', 'tensor'), scatter_dimension=0...  98 us
    reduce_scatter x1, waiting for transfers between devices, on_device(): lax.psum_scatter(grad_values.astype(jnp.bfloat16), ('seq', 'tensor'), sca...  79.9 us
    dot_general x6, matrix products, contract_rows(): lax.dot_general(left, right, (((0,), (0,)), ((), ())), preferred_element_...  56.4 us
  transfers between devices with their start and end apart: 16, of which 11 were waited for; matrix products, arithmetic and copies ran while one was open for 5% of the time, Pallas kernels for 0%

commit v1 on v0

v1 whole, which is shorter than its diff:
```python
import functools

import jax
import jax.numpy as jnp
from jax import lax
from jax.experimental import pallas as pl
from jax.experimental.pallas import tpu as pltpu
from jax.sharding import PartitionSpec as P

epsilon = 1e-05
negative = -1e30
log2e = 1.4426950408889634
f32 = jnp.float32
low = jnp.bfloat16
vmem_bytes = 48 * 1024 * 1024


def dot(left, right):
    return jnp.dot(left, right, preferred_element_type=f32)


def contract_rows(left, right):
    return lax.dot_general(left, right, (((0,), (0,)), ((), ())), preferred_element_type=f32)


def contract_cols(left, right):
    return lax.dot_general(left, right, (((1,), (1,)), ((), ())), preferred_element_type=f32)


def allowed_mask(start, base, flip, pos_ref):
    offset = lax.broadcasted_iota(jnp.int32, (start, 1), 0)
    key_pos = base + (offset ^ flip)
    return (key_pos <= pos_ref[0:1, :]) & (key_pos >= pos_ref[1:2, :])


def over_blocks(info, body):
    body(0, True)
    lax.fori_loop(1, info[0], lambda s, c: (body(s, False), c)[1], 0)
    lax.fori_loop(info[0], info[1], lambda s, c: (body(s, True), c)[1], 0)


def attend_kernel(
    scale, info, q_ref, k_ref, vt_ref, pos_ref, o_ref, lse_ref, m_ref, l_ref, acc_ref
):
    span = q_ref.shape[0]
    head = k_ref.shape[1]
    pair = q_ref.shape[1] // head
    step = pl.program_id(0)
    turned = [q_ref[:, h * head : (h + 1) * head].T for h in range(pair)]
    m_ref[...] = jnp.full_like(m_ref, negative)
    l_ref[...] = jnp.zeros_like(l_ref)
    acc_ref[...] = jnp.zeros_like(acc_ref)

    def body(s, masked):
        where = pl.multiple_of(s * span, span)
        key_block = k_ref[pl.ds(where, span), :]
        value_block = vt_ref[:, pl.ds(where, span)]
        if masked:
            allowed = allowed_mask(span, (info[2] - s) * span, info[3], pos_ref)
        for h in range(pair):
            scores = dot(key_block, turned[h]) * scale
            if masked:
                scores = jnp.where(allowed, scores, negative)
            before = m_ref[h]
            after = jnp.maximum(before, jnp.max(scores, axis=0, keepdims=True))
            weights = jnp.exp2(scores - after)
            shrink = jnp.exp2(before - after)
            m_ref[h] = after
            l_ref[h] = l_ref[h] * shrink + jnp.sum(weights, axis=0, keepdims=True)
            acc_ref[h] = acc_ref[h] * shrink + dot(value_block, weights.astype(low))

    over_blocks(info, body)
    for h in range(pair):
        total = l_ref[h]
        lse_ref[pl.ds(step * pair + h, 1), :] = m_ref[h] + jnp.log2(total)
        o_ref[:, h * head : (h + 1) * head] = (acc_ref[h] / total).T.astype(low)


def attend_back_kernel(
    scale,
    unit,
    info,
    q_ref,
    do_ref,
    o_ref,
    lse_ref,
    k_ref,
    kt_ref,
    v_ref,
    pos_ref,
    dq_ref,
    dkv_ref,
    dk_ref,
    dv_ref,
    dqt_ref,
):
    span = q_ref.shape[0]
    head = k_ref.shape[1]
    pair = q_ref.shape[1] // head
    step = pl.program_id(0)

    @pl.when(step == 0)
    def _():
        dk_ref[...] = jnp.zeros_like(dk_ref)
        dv_ref[...] = jnp.zeros_like(dv_ref)

    dqt_ref[...] = jnp.zeros_like(dqt_ref)
    queries = [q_ref[:, h * head : (h + 1) * head] for h in range(pair)]
    grads = [do_ref[:, h * head : (h + 1) * head] for h in range(pair)]
    queries_t = [item.T for item in queries]
    grads_t = [item.T for item in grads]
    inner = [
        jnp.sum(
            grads_t[h].astype(f32) * o_ref[:, h * head : (h + 1) * head].T.astype(f32),
            axis=0,
            keepdims=True,
        )
        for h in range(pair)
    ]
    totals = [lse_ref[pl.ds(step * pair + h, 1), :] for h in range(pair)]

    def body(s, masked):
        where = pl.multiple_of(s * span, span)
        key_block = k_ref[pl.ds(where, span), :]
        key_turned = kt_ref[:, pl.ds(where, span)]
        value_block = v_ref[pl.ds(where, span), :]
        if masked:
            allowed = allowed_mask(span, (info[2] - s) * span, info[3], pos_ref)
        key_part = jnp.zeros((span, head), f32)
        value_part = jnp.zeros((span, head), f32)
        for h in range(pair):
            scores = dot(key_block, queries_t[h]) * scale - totals[h]
            if masked:
                scores = jnp.where(allowed, scores, negative)
            probs = jnp.exp2(scores)
            grad_probs = dot(value_block, grads_t[h])
            grad_scores = (probs * (grad_probs - inner[h])).astype(low)
            key_part += dot(grad_scores, queries[h])
            value_part += dot(probs.astype(low), grads[h])
            dqt_ref[h] += dot(key_turned, grad_scores)
        dk_ref[pl.ds(where, span), :] += key_part
        dv_ref[pl.ds(where, span), :] += value_part

    over_blocks(info, body)
    for h in range(pair):
        dq_ref[:, h * head : (h + 1) * head] = (dqt_ref[h] * unit).T.astype(low)

    @pl.when(step == pl.num_programs(0) - 1)
    def _():
        dkv_ref[0] = (dk_ref[...] * unit).astype(low)
        dkv_ref[1] = dv_ref[...].astype(low)


def attend(info, query, keys, values_t, pos, heads, head):
    span = query.shape[0]
    window = keys.shape[0]
    pair = 2
    scale = head**-0.5 * log2e
    work = heads * span * window * head
    spec = pltpu.PrefetchScalarGridSpec(
        num_scalar_prefetch=1,
        grid=(heads // pair,),
        in_specs=[
            pl.BlockSpec((span, pair * head), lambda i, s: (0, i)),
            pl.BlockSpec((window, head), lambda i, s: (0, 0)),
            pl.BlockSpec((head, window), lambda i, s: (0, 0)),
            pl.BlockSpec(pos.shape, lambda i, s: (0, 0)),
        ],
        out_specs=[
            pl.BlockSpec((span, pair * head), lambda i, s: (0, i)),
            pl.BlockSpec((heads, span), lambda i, s: (0, 0)),
        ],
        scratch_shapes=[
            pltpu.VMEM((pair, 1, span), f32),
            pltpu.VMEM((pair, 1, span), f32),
            pltpu.VMEM((pair, head, span), f32),
        ],
    )
    return pl.pallas_call(
        functools.partial(attend_kernel, scale),
        grid_spec=spec,
        out_shape=(
            jax.ShapeDtypeStruct(query.shape, low),
            jax.ShapeDtypeStruct((heads, span), f32),
        ),
        compiler_params=pltpu.CompilerParams(vmem_limit_bytes=vmem_bytes),
        cost_estimate=pl.CostEstimate(
            flops=8 * work, bytes_accessed=4 * query.size, transcendentals=work // head
        ),
        name="attend",
    )(info, query, keys, values_t, pos)


def attend_back(info, query, grad, attended, lse, keys, keys_t, values, pos, heads, head):
    span = query.shape[0]
    window = keys.shape[0]
    pair = 2
    scale = head**-0.5 * log2e
    work = heads * span * window * head
    wide = pl.BlockSpec((span, pair * head), lambda i, s: (0, i))
    tall = pl.BlockSpec((window, head), lambda i, s: (0, 0))
    spec = pltpu.PrefetchScalarGridSpec(
        num_scalar_prefetch=1,
        grid=(heads // pair,),
        in_specs=[
            wide,
            wide,
            wide,
            pl.BlockSpec((heads, span), lambda i, s: (0, 0)),
            tall,
            pl.BlockSpec((head, window), lambda i, s: (0, 0)),
            tall,
            pl.BlockSpec(pos.shape, lambda i, s: (0, 0)),
        ],
        out_specs=[wide, pl.BlockSpec((2, window, head), lambda i, s: (0, 0, 0))],
        scratch_shapes=[
            pltpu.VMEM((window, head), f32),
            pltpu.VMEM((window, head), f32),
            pltpu.VMEM((pair, head, span), f32),
        ],
    )
    return pl.pallas_call(
        functools.partial(attend_back_kernel, scale, head**-0.5),
        grid_spec=spec,
        out_shape=(
            jax.ShapeDtypeStruct(query.shape, low),
            jax.ShapeDtypeStruct((2, window, head), low),
        ),
        compiler_params=pltpu.CompilerParams(vmem_limit_bytes=vmem_bytes),
        cost_estimate=pl.CostEstimate(
            flops=20 * work, bytes_accessed=8 * query.size, transcendentals=work // head
        ),
        name="attend_back",
    )(info, query, grad, attended, lse, keys, keys_t, values, pos)


def swap(item):
    return lax.ppermute(item, "tensor", [(0, 1), (1, 0)])


def cross(item, bits):
    size = lax.axis_size("dp")
    return lax.ppermute(item, "dp", [(i, i ^ bits) for i in range(size)])


def shift(item, by):
    size = lax.axis_size("seq")
    return lax.ppermute(item, "seq", [(i, (i + by) % size) for i in range(size)])


def shift_up(item, by):
    size = lax.axis_size("seq")
    return lax.ppermute(item, "seq", [(i, i + by) for i in range(size - by)])


def shift_down(item, by):
    size = lax.axis_size("seq")
    return lax.ppermute(item, "seq", [(i + by, i) for i in range(size - by)])


def pair_gather(item):
    return jnp.concatenate([item, swap(item)], axis=0)


def pair_sum(left, right_of):
    half = left.shape[0] // 2
    mine = right_of(left[:half])
    theirs = right_of(left[half:]).astype(low)
    return mine + swap(theirs).astype(f32)


def ring_gather(own):
    size = lax.axis_size("seq")
    held, blocks = own, []
    for step in range(size):
        if step:
            held = shift(held, 1)
        blocks.append(pair_gather(held))
    return blocks


def dp_scatter(piece):
    far = piece(3).astype(low)
    half = far.shape[0] // 2
    near_x = piece(1).astype(low)
    near_y = piece(2).astype(low)
    far_a = cross(far[:half], 1)
    far_b = cross(far[half:], 2)
    own_a = cross(near_x[:half], 1)
    own_b = cross(near_y[half:], 2)
    own = piece(0)
    second_a = (near_y[:half].astype(f32) + far_a.astype(f32)).astype(low)
    second_b = (near_x[half:].astype(f32) + far_b.astype(f32)).astype(low)
    got_a = cross(second_a, 2)
    got_b = cross(second_b, 1)
    return jnp.concatenate(
        [
            own[:half] + own_a.astype(f32) + got_a.astype(f32),
            own[half:] + own_b.astype(f32) + got_b.astype(f32),
        ],
        axis=0,
    )


def norm_parts(rows):
    centre = rows - jnp.mean(rows, axis=-1, keepdims=True)
    inverse = lax.rsqrt(jnp.mean(centre * centre, axis=-1, keepdims=True) + epsilon)
    return centre * inverse, inverse


def norm_back(grad, unit, inverse, gain):
    scaled = grad * gain
    part = (
        scaled
        - jnp.mean(scaled, axis=-1, keepdims=True)
        - unit * jnp.mean(scaled * unit, axis=-1, keepdims=True)
    )
    return part * inverse, jnp.sum(grad * unit, axis=0), jnp.sum(grad, axis=0)


def gelu_both(value, grad):
    inside = 0.7978845608028654 * (value + 0.044715 * value * value * value)
    bend = jnp.tanh(inside)
    half = 0.5 * (1.0 + bend)
    slope = half + 0.5 * value * (1.0 - bend * bend) * 0.7978845608028654 * (
        1.0 + 3.0 * 0.044715 * value * value
    )
    return (value * half).astype(low), (grad.astype(f32) * slope).astype(low)


def on_device(
    tokens,
    lengths,
    ln1_gain,
    ln1_bias,
    w_query,
    b_query,
    w_key,
    w_value,
    b_value,
    w_out,
    b_out,
    ln2_gain,
    ln2_bias,
    w_up,
    b_up,
    w_down,
    b_down,
    cotangent,
):
    shard = tokens[0].astype(f32)
    rows_own, width = shard.shape
    seqs = lax.axis_size("seq")
    dps = lax.axis_size("dp")
    span = 2 * rows_own
    heads, head = b_query.shape
    at_dp, at_seq, at_core = (lax.axis_index(name) for name in ("dp", "seq", "tensor"))
    flip = at_core * rows_own
    span_start = at_seq * span
    hidden_local = w_up.shape[1]
    hidden_part = hidden_local // seqs
    dp_part = width // dps
    out_part = dp_part // seqs

    ends = jnp.cumsum(lengths[0], dtype=jnp.int32)
    row_pos = span_start + (jnp.arange(span, dtype=jnp.int32) ^ flip)
    row_start = jnp.max(
        jnp.where(row_pos[:, None] >= ends[None, :], ends[None, :], 0), axis=1
    ).astype(jnp.int32)
    pos = jnp.zeros((8, span), jnp.int32).at[0].set(row_pos).at[1].set(row_start)
    first, last = jnp.min(row_start), jnp.max(row_start)
    whole_to = jnp.clip(at_seq + 1 - (last + span - 1) // span, 1, at_seq + 1)
    some_to = jnp.clip(at_seq + 1 - first // span, whole_to, at_seq + 1)
    info = jnp.stack([whole_to, some_to, at_seq, flip]).astype(jnp.int32)

    grad_own = cotangent[0]
    grad_blocks = ring_gather(grad_own)
    up_part = lax.dynamic_slice_in_dim(w_up, at_seq * hidden_part, hidden_part, 1)
    down_part = lax.dynamic_slice_in_dim(w_down, at_seq * hidden_part, hidden_part, 0)
    bias_part = lax.dynamic_slice_in_dim(
        b_up.reshape(-1), at_seq * hidden_part, hidden_part, 0
    )
    grad_act = contract_cols(grad_blocks[0], w_down).astype(low)
    grad_act_parts = [
        contract_cols(block, down_part).astype(low) for block in grad_blocks[1:]
    ]

    unit_one, inverse_one = norm_parts(shard)
    normed = (unit_one * ln1_gain + ln1_bias).astype(low)
    key_own = dot(normed, w_key).astype(low)
    value_own = (dot(normed, w_value) + b_value).astype(low)
    both_own = jnp.concatenate([key_own, value_own], axis=1)
    both = [both_own] + [shift_up(both_own, by) for by in range(1, seqs)]
    both = jnp.stack(both)
    both = jnp.stack([both, swap(both)], axis=1).reshape(seqs * span, 2 * head)
    keys, values = both[:, :head], both[:, head:]
    normed_all = pair_gather(normed)
    query = (dot(normed_all, w_query) + b_query.reshape(-1)).astype(low)
    attended, lse = attend(info, query, keys, values.T, pos, heads, head)
    middle = shard + (pair_sum(attended, lambda part: dot(part, w_out)) + b_out)
    unit_two, inverse_two = norm_parts(middle)
    normed_two = (unit_two * ln2_gain + ln2_bias).astype(low)

    normed_blocks = ring_gather(normed_two)
    hidden = dot(normed_blocks[0], w_up) + b_up.reshape(-1)
    activated, grad_hidden = gelu_both(hidden, grad_act)
    result = middle + (pair_sum(activated, lambda part: dot(part, w_down)) + b_down)
    output = result.astype(low)[None]
    grad_normed_two = pair_sum(grad_hidden, lambda part: contract_cols(part, w_up))
    grad_b_up = jnp.sum(grad_hidden.astype(f32), axis=0)

    back, grad_ln2_gain, grad_ln2_bias = norm_back(
        grad_normed_two, unit_two, inverse_two, ln2_gain
    )
    grad_out = grad_own.astype(f32)
    grad_b_down = jnp.sum(grad_out, axis=0)
    grad_middle = grad_out + back
    grad_branch = grad_middle.astype(low)
    grad_b_out = jnp.sum(grad_branch.astype(f32), axis=0)
    grad_branch_all = pair_gather(grad_branch)
    grad_attended = contract_cols(grad_branch_all, w_out).astype(low)

    grad_query, grad_both = attend_back(
        info, query, grad_attended, attended, lse, keys, keys.T, values, pos, heads, head
    )
    grad_both = grad_both.reshape(2, seqs, 2, rows_own, head)
    kept = lax.dynamic_index_in_dim(grad_both, at_core, 0, False)
    given = lax.dynamic_index_in_dim(grad_both, 1 - at_core, 0, False)
    grad_kv = (kept.astype(f32) + swap(given)[:, ::-1].astype(f32)).astype(low)
    grad_kv = grad_kv.reshape(seqs, span, head)
    total = grad_kv[0].astype(f32)
    for by in range(1, seqs):
        total = total + shift_down(grad_kv[by], by).astype(f32)
    grad_kv = total.astype(low)
    grad_qkv = jnp.concatenate([grad_query, grad_kv], axis=1)
    w_qkv = jnp.concatenate([w_query, jnp.where(at_core == 0, w_key, w_value)], axis=1)
    grad_normed = pair_sum(grad_qkv, lambda part: contract_cols(part, w_qkv))
    back, grad_ln1_gain, grad_ln1_bias = norm_back(
        grad_normed, unit_one, inverse_one, ln1_gain
    )
    grad_input = (grad_middle + back).astype(low)[None]

    acts, grads = [], []
    for step in range(seqs):
        if step:
            value = dot(normed_blocks[step], up_part) + bias_part
            act, grad = gelu_both(value, grad_act_parts[step - 1])
        else:
            act = lax.dynamic_slice_in_dim(activated, at_seq * hidden_part, hidden_part, 1)
            grad = lax.dynamic_slice_in_dim(grad_hidden, at_seq * hidden_part, hidden_part, 1)
        acts.append(act)
        grads.append(grad)
    acts = jnp.concatenate(acts, axis=0)
    grads = jnp.concatenate(grads, axis=0)
    grad_tokens = jnp.concatenate(grad_blocks, axis=0)
    normed_tokens = jnp.concatenate(normed_blocks, axis=0)

    def columns(item, r):
        return lax.dynamic_slice_in_dim(item, (at_dp ^ r) * dp_part, dp_part, 1)

    sum_down = dp_scatter(lambda r: contract_rows(acts, columns(grad_tokens, r)))
    sum_up = dp_scatter(lambda r: contract_rows(columns(normed_tokens, r), grads))
    sum_out = dp_scatter(lambda r: contract_rows(attended, columns(grad_branch_all, r)))
    sum_qkv = dp_scatter(lambda r: contract_rows(columns(normed_all, r), grad_qkv))

    def to_seq(item, by, axis):
        at = lax.rem(at_seq + by, seqs)
        return lax.dynamic_slice_in_dim(item, at * out_part, out_part, axis)

    def spread(item, axis):
        narrow = item.astype(low)
        other = 1 - axis
        shape = [out_part, out_part]
        shape[other] = hidden_local
        whole = jnp.zeros(shape, f32)
        for by in range(seqs):
            if by:
                got = shift(to_seq(narrow, by, axis), by).astype(f32)
            else:
                got = to_seq(item, 0, axis)
            at = lax.rem(at_seq + seqs - by, seqs)
            whole = lax.dynamic_update_slice_in_dim(whole, got, at * hidden_part, other)
        return whole

    def seq_sum(item, axis):
        narrow = item.astype(low)
        total = to_seq(item, 0, axis)
        for by in range(1, seqs):
            total = total + shift(to_seq(narrow, by, axis), by).astype(f32)
        return total

    out_w_down = spread(sum_down, 1)
    out_w_up = spread(sum_up, 0)
    out_w_out = seq_sum(sum_out, 1)
    out_qkv = seq_sum(sum_qkv, 0)
    out_w_query = out_qkv[:, : heads * head]
    half = out_part // 2
    last_kv = out_qkv[:, heads * head :]
    mine = lax.dynamic_slice_in_dim(last_kv, at_core * half, half, 0)
    other = swap(lax.dynamic_slice_in_dim(last_kv, (1 - at_core) * half, half, 0))
    out_w_key = jnp.where(at_core == 0, mine, other)
    out_w_value = jnp.where(at_core == 0, other, mine)

    grad_b_value = jnp.where(at_core == 1, jnp.sum(grad_kv.astype(f32), axis=0), 0.0)
    grad_b_query = jnp.sum(grad_query.astype(f32), axis=0)
    shared = [
        item.reshape(dps, seqs, 2, -1)
        for item in (
            grad_ln1_gain,
            grad_ln1_bias,
            grad_b_out,
            grad_ln2_gain,
            grad_ln2_bias,
            grad_b_down,
            grad_b_value,
        )
    ]
    sizes = [item.shape[-1] for item in shared]
    shared = jnp.concatenate(shared, axis=-1)
    shared = lax.dynamic_index_in_dim(shared, at_core, 2, False) + swap(
        lax.dynamic_index_in_dim(shared, 1 - at_core, 2, False)
    )

    def by_device(item, rows):
        item = item.reshape(rows, dps, seqs, -1)
        return jnp.transpose(item, (1, 2, 0, 3)).reshape(dps, seqs, -1)

    local_up = by_device(grad_b_up, b_up.shape[0])
    local_query = by_device(grad_b_query, heads)
    sizes = sizes + [local_up.shape[-1], local_query.shape[-1]]
    packed = jnp.concatenate([shared, local_up, local_query], axis=-1)
    total = lax.dynamic_index_in_dim(packed, at_dp, 0, False)
    for r in (1, 2, 3):
        total = total + cross(lax.dynamic_index_in_dim(packed, at_dp ^ r, 0, False), r)
    packed = total
    total = lax.dynamic_index_in_dim(packed, at_seq, 0, False)
    for by in range(1, seqs):
        at = lax.rem(at_seq + by, seqs)
        total = total + shift(lax.dynamic_index_in_dim(packed, at, 0, False), by)
    parts, at = [], 0
    for size in sizes:
        parts.append(total[at : at + size])
        at += size
    return (
        output,
        grad_input,
        parts[0],
        parts[1],
        out_w_query,
        parts[8].reshape(heads, -1),
        out_w_key,
        out_w_value,
        parts[6],
        out_w_out,
        parts[2],
        parts[3],
        parts[4],
        out_w_up,
        parts[7].reshape(b_up.shape[0], -1),
        out_w_down,
        parts[5],
    )


def solution(mesh):
    in_specs = (
        P("dp", ("seq", "tensor"), None),
        P("dp", None),
        P(),
        P(),
        P(None, "tensor"),
        P("tensor", None),
        P(),
        P(),
        P(),
        P("tensor", None),
        P(),
        P(),
        P(),
        P(None, "tensor"),
        P("tensor", None),
        P("tensor", None),
        P(),
        P("dp", ("seq", "tensor"), None),
    )
    out_specs = (
        P("dp", ("seq", "tensor"), None),
        P("dp", ("seq", "tensor"), None),
        P(("dp", "seq", "tensor")),
        P(("dp", "seq", "tensor")),
        P(("dp", "seq"), "tensor"),
        P("tensor", ("dp", "seq")),
        P(("dp", "seq", "tensor"), None),
        P(("dp", "seq", "tensor"), None),
        P(("dp", "seq", "tensor")),
        P("tensor", ("dp", "seq")),
        P(("dp", "seq", "tensor")),
        P(("dp", "seq", "tensor")),
        P(("dp", "seq", "tensor")),
        P(("dp", "seq"), "tensor"),
        P("tensor", ("dp", "seq")),
        P("tensor", ("dp", "seq")),
        P(("dp", "seq", "tensor")),
    )
    return jax.shard_map(
        on_device, mesh=mesh, in_specs=in_specs, out_specs=out_specs, check_vma=False
    )
```

time: 2420 us -> 570 us (0.24)
  waiting for transfers between devices: 2020 us -> 144 us
  blocking collectives: 145 us -> 0 us
  starting transfers between devices: 1.09 us -> 90.1 us
  local copies, waits for them, and re-layouts: 22.3 us -> 68.6 us
    reduce_scatter x12 -> x0, waiting for transfers between devices: 2000 us -> none  [the longest x1 691 us: on_device(): lax.psum_scatter(grad_w_up, ('dp', 'seq'), scatter_dimension=0, tiled=True)]
    ppermute x0 -> x72, waiting for transfers between devices: none -> 144 us  [the longest x21 65.7 us: shift(): lax.ppermute(item, 'seq', [(i, (i + by) % size) for i in range(size)])]
    unnamed x2 -> x0, blocking collectives: 112 us -> none
    ppermute x0 -> x72, starting transfers between devices: none -> 90.1 us  [the longest x21 43.6 us: shift(): lax.ppermute(item, 'seq', [(i, (i + by) % size) for i in range(size)])]
    all_gather x2 -> x0, blocking collectives: 32.4 us -> none  [the longest x1 16.6 us: on_device(): lax.all_gather(key_own, ('seq', 'tensor'), axis=0, tiled=True)]
    dot_general x6 -> x9, matrix products: 50.1 us -> 75.9 us  [contract_cols(): lax.dot_general(left, right, (((1,), (1,)), ((), ())), preferred_element_...]
    dot_general x6 -> x16, matrix products: 56.4 us -> 50.3 us  [contract_rows(): lax.dot_general(left, right, (((0,), (0,)), ((), ())), preferred_element_...]
    dot_general x15 -> x11, matrix products: 69.6 us -> 69.1 us  [dot(): return jnp.dot(left, right, preferred_element_type=f32)]
  transfers between devices with their start and end apart: 16 -> 72, of which waited for: 11 -> 22; matrix products, arithmetic and copies ran while one was open for 5% -> 53% of each run, Pallas kernels for 0% -> 3%
where the time goes in v1:
time: 570 us; the launch traced here: 559 us
  matrix products  195 us (34%)
  waiting for transfers between devices  144 us (25%)
  starting transfers between devices  90.1 us (16%)
  local copies, waits for them, and re-layouts  68.6 us (12%)
  other arithmetic  38.9 us (7%)
  Pallas kernels  16.4 us (3%)
  between operations  5.95 us (1%)
    dot_general x9, matrix products, contract_cols(): lax.dot_general(left, right, (((1,), (1,)), ((), ())), preferred_element_...  75.9 us
    dot_general x11, matrix products, dot(): return jnp.dot(left, right, preferred_element_type=f32)  69.1 us
    ppermute x21, waiting for transfers between devices, shift(): lax.ppermute(item, 'seq', [(i, (i + by) % size) for i in range(size)])  65.7 us
    ppermute x27, waiting for transfers between devices, cross(): return lax.ppermute(item, 'dp', [(i, i ^ bits) for i in range(size)])  54.6 us
    dot_general x16, matrix products, contract_rows(): lax.dot_general(left, right, (((0,), (0,)), ((), ())), preferred_element_...  50.3 us
    ppermute x21, starting transfers between devices, shift(): lax.ppermute(item, 'seq', [(i, (i + by) % size) for i in range(size)])  43.6 us
    unnamed x171, local copies, waits for them, and re-layouts  33.8 us
    ppermute x27, starting transfers between devices, cross(): return lax.ppermute(item, 'dp', [(i, i ^ bits) for i in range(size)])  27.9 us
  transfers between devices with their start and end apart: 72, of which 22 were waited for; matrix products, arithmetic and copies ran while one was open for 53% of the time, Pallas kernels for 3%

profile of v1, /device:TPU:0, one launch (start us, length us, event | category | flops | bytes accessed | tf_op | source)
XLA Modules:
  0.0 559.2 jit_solution(15595520842949437288)
XLA Ops:
  5.6 7.0 %collective-permute-start.3 = (bf16[256,256]{0,1:T(8,128)(2,1)S(1)}, bf16[256,256]{0,1:T(8,128)(2,1)S(1)}, u32[]{:S(2)}, u32[]{:S(2)}) collective-permute-start(bf16[256,256]{0,1:T(8,128)(2,1)S(1)} %get-tuple-element.162), channel_id=1, source_target_pairs={{0,6},{1,7},{8,14},{9,15},{16,22},{17,23},{24,30},{25,31}} | collective-permute-start | bytes 393224 | tf_op jit(solution)/shard_map/ppermute | solution.py:253
  13.8 2.5 collective-permute-start.1
  16.5 2.8 collective-permute-done.2
  21.6 4.2 collective-permute-start.48
  34.1 2.4 fusion.276
  38.0 4.8 add_convert_fusion.2.q_ref
  42.9 6.6 %attend.1 = (bf16[512,1024]{1,0:T(8,128)(2,1)S(1)}, f32[8,512]{1,0:T(8,128)S(1)}) custom-call(s32[4]{0:T(128)S(1)} %pad_add_fusion.info, bf16[512,1024]{1,0:T(8,128)(2,1)S(1)} %add_convert_fusion.2.q_ref, bf16[2048,128]{1,0:T(8,128)(2,1)S(1)} %get-tuple-element.154.k_ref, bf16[128,2048]{1,0:T(8,128)(2,1)S(1)} %copy.50.vt_ref, s32[8,512]{1,0:T(8,128)S(1)} %scatter.9.pos_ref), custom_call_target="tpu_custom_call" | custom-call | flops 8589934592 | bytes 2097152 | tf_op jit(solution)/shard_map/attend/pallas_call | solution.py:179
  54.5 7.8 %collective-permute-start.50 = (bf16[256,2048]{1,0:T(8,128)(2,1)}, bf16[256,2048]{1,0:T(8,128)(2,1)}, u32[]{:S(2)}, u32[]{:S(2)}) collective-permute-start(bf16[256,2048]{1,0:T(8,128)(2,1)} %collective-permute-done.48), channel_id=1, source_target_pairs={{0,2},{2,4},{4,6},{6,0},{1,3},{3,5},{5,7},{7,1},{8,10},{10,12},{12... | collective-permute-start | bytes 3145736 | tf_op jit(solution)/shard_map/ppermute | solution.py:248
  62.4 4.0 fusion.279
  73.0 2.4 constant_dynamic-update-slice_fusion.13
  75.3 4.9 collective-permute-start.42
  80.2 14.4 %collective-permute-done.50 = bf16[256,2048]{1,0:T(8,128)(2,1)} collective-permute-done((bf16[256,2048]{1,0:T(8,128)(2,1)}, bf16[256,2048]{1,0:T(8,128)(2,1)}, u32[]{:S(2)}, u32[]{:S(2)}) %collective-permute-start.50) | collective-permute-done | bytes 1048608 | tf_op jit(solution)/shard_map/ppermute | solution.py:248
  94.7 2.3 constant_dynamic-update-slice_fusion.12
  99.3 17.0 %multiply_convert_fusion = (bf16[512,4096]{1,0:T(8,128)(2,1)}, f32[512,4096]{1,0:T(8,128)}) fusion(f32[4096]{0:T(1024)S(1)} %bitcast.144, bf16[2048,4096]{1,0:T(8,128)(2,1)} %param.35, bf16[256,2048]{1,0:T(8,128)(2,1)S(1)} %collective-permute-done.6, bf16[256,2048]{1,0:T(8,128)(2,1)} %get-tuple-element.115), kind=kOutput, calls=%fused_computation.10 | convolution fusion | flops 8615100416 | bytes 31473664 | tf_op jit(solution)/shard_map/dot_general | solution.py:19
  116.3 20.2 %convert_reduce_fusion = (f32[4096]{0:T(1024)S(1)}, bf16[512,4096]{1,0:T(8,128)(2,1)}) fusion(f32[512,4096]{1,0:T(8,128)} %get-tuple-element.184, f32[4096]{0:T(1024)S(1)} %bitcast.145, bf16[4096,2048]{1,0:T(8,128)(2,1)} %param.37, bf16[256,2048]{1,0:T(8,128)(2,1)} %collective-permute-done.8, bf16[256,2048]{1,0:T(8,128)(2,1)} %bitcast.19), kind=kOutput, calls=%fused_computation.9 | convolution fusion | flops 8644456448 | bytes 31490048 | tf_op jit(solution)/shard_map/dot_general | solution.py:27
  136.5 11.9 %convolution_convert_fusion.4 = bf16[256,2048]{1,0:T(8,128)(2,1)} fusion(bf16[2048,4096]{1,0:T(8,128)(2,1)} %param.35, bf16[512,4096]{1,0:T(8,128)(2,1)} %get-tuple-element.186), kind=kOutput, calls=%fused_computation.67 | convolution fusion | flops 4295491584 | bytes 19922944 | tf_op jit(solution)/shard_map/dot_general | solution.py:27
  149.0 11.9 %convolution_convert_fusion.5 = bf16[256,2048]{1,0:T(8,128)(2,1)} fusion(bf16[4096,2048]{1,0:T(8,128)(2,1)} %param.37, bf16[512,4096]{1,0:T(8,128)(2,1)} %get-tuple-element.183), kind=kOutput, calls=%fused_computation.68 | convolution fusion | flops 4295491584 | bytes 19922944 | tf_op jit(solution)/shard_map/dot_general | solution.py:19
  164.7 2.9 constant_dynamic-update-slice_fusion.5
  168.3 2.4 constant_dynamic-update-slice_fusion.10
  170.6 9.7 %fusion.70 = f32[256,2048]{1,0:T(8,128)} fusion(bf16[4096,2048]{1,0:T(8,128)(2,1)} %param.37, bf16[512,4096]{1,0:T(8,128)(2,1)S(1)} %copy-done.40), kind=kOutput, calls=%fused_computation.125 | convolution fusion | flops 4294967296 | bytes 20971520 | tf_op jit(solution)/shard_map/dot_general | solution.py:19
  180.4 13.0 %multiply_reduce_fusion = (f32[2048]{0:T(1024)S(1)}, f32[256]{0:T(256)S(1)}, f32[256]{0:T(256)S(1)}, f32[2048]{0:T(1024)S(1)}, f32[256,2048]{1,0:T(8,128)}) fusion(f32[256,2048]{1,0:T(8,128)S(1)} %copy-done.7, f32[256]{0:T(256)S(1)} %add_rsqrt_fusion, f32[256]{0:T(256)S(1)} %broadcast_multiply_fusion.4, bf16[256,2048]{1,0:T(8,128)(2,1)} %collective-permute-done.9, ...), kind=kOutput, calls=%fused_computation.175 | convolution fusion | flops 4300730368 | bytes 24145920 | tf_op jit(solution)/shard_map/dot_general | solution.py:27
  193.4 5.4 convert_reduce_fusion.4
  207.8 2.5 collective-permute-start.46
  210.3 2.5 constant_dynamic-update-slice_fusion.4
  215.1 2.3 constant_dynamic-update-slice_fusion.8
  217.5 4.0 fusion.131.do_ref
  221.6 9.8 %attend_back.1 = (bf16[512,1024]{1,0:T(8,128)(2,1)S(1)}, bf16[2,2048,128]{2,1,0:T(8,128)(2,1)S(1)}) custom-call(s32[4]{0:T(128)S(1)} %pad_add_fusion.info, bf16[512,1024]{1,0:T(8,128)(2,1)S(1)} %copy-done.5, bf16[512,1024]{1,0:T(8,128)(2,1)S(1)} %fusion.131.do_ref, bf16[512,1024]{1,0:T(8,128)(2,1)} %copy-done, f32[8,512]{1,0:T(8,128)S(1)} %get-tuple-element.46.lse_ref, ...), custom_call_target="tpu_custom_call" | custom-call | flops 21474836480 | bytes 4194304 | tf_op jit(solution)/shard_map/attend_back/pallas_call | solution.py:222
  239.8 2.7 convolution_convert_fusion.9
  242.4 3.0 fusion.190
  247.0 4.8 fusion.9
  251.8 8.0 %fusion.56 = bf16[512,1024]{1,0:T(8,128)(2,1)} fusion(f32[512,1024]{1,0:T(8,128)S(1)} %fusion.9, f32[1024]{0:T(1024)S(1)} %dynamic_slice.191, bf16[4096,2048]{1,0:T(8,128)(2,1)} %param.37, s32[]{:T(128)S(6)} %select_n.188, bf16[256,2048]{1,0:T(8,128)(2,1)} %collective-permute-done.51, bf16[256,2048]{1,0:T(8,128)(2,1)} %collective-permute-done.50), kind=kOutput, calls=%fused_computation.111 | convolution fusion | flops 2163212288 | bytes 9441284 | tf_op jit(solution)/shard_map/dot_general | solution.py:27
  264.9 2.4 constant_dynamic-update-slice_fusion.1
  276.9 18.9 %collective-permute-done.14 = bf16[512,128]{1,0:T(8,128)(2,1)S(1)} collective-permute-done((bf16[512,128]{1,0:T(8,128)(2,1)S(1)}, bf16[512,128]{1,0:T(8,128)(2,1)S(1)}, u32[]{:S(2)}, u32[]{:S(2)}) %collective-permute-start.14) | collective-permute-done | bytes 131104 | tf_op jit(solution)/shard_map/ppermute | solution.py:258
  300.8 2.9 convolution_convert_fusion.3
  308.4 3.4 fusion.199
  311.8 2.5 fusion.23
  318.8 3.1 collective-permute-start.41
  325.1 5.2 fusion.7
  330.3 6.3 %fusion.63 = bf16[512,1024]{1,0:T(8,128)(2,1)S(1)} fusion(f32[512,1024]{1,0:T(8,128)S(1)} %fusion.7, f32[1024]{0:T(1024)S(1)} %dynamic_slice.191, bf16[4096,2048]{1,0:T(8,128)(2,1)} %param.37, s32[]{:T(128)S(6)} %select_n.188, bf16[256,2048]{1,0:T(8,128)(2,1)} %collective-permute-done.53, bf16[256,2048]{1,0:T(8,128)(2,1)} %collective-permute-done.52), kind=kOutput, calls=%fused_computation.118 | convolution fusion | flops 2163212288 | bytes 9441284 | tf_op jit(solution)/shard_map/dot_general | solution.py:27
  336.6 8.5 %multiply_convert_fusion.3 = (bf16[512,1024]{1,0:T(8,128)(2,1)}, bf16[512,1024]{1,0:T(8,128)(2,1)}, bf16[512,1024]{1,0:T(8,128)(2,1)}, f32[512,1024]{1,0:T(8,128)S(1)}) fusion(f32[1024]{0:T(1024)S(1)} %dynamic_slice.191, f32[512,1024]{1,0:T(8,128)S(1)} %fusion.7, f32[512,1024]{1,0:T(8,128)S(1)} %copy-done.67, bf16[2048,4096]{1,0:T(8,128)(2,1)} %param.35, ...), kind=kOutput, calls=%fused_computation.162 | convolution fusion | flops 2167406592 | bytes 15732740 | tf_op jit(solution)/shard_map/dot_general | solution.py:19
  346.4 6.3 %fusion.49 = bf16[512,1024]{1,0:T(8,128)(2,1)S(1)} fusion(f32[512,1024]{1,0:T(8,128)S(1)} %get-tuple-element.188, f32[1024]{0:T(1024)S(1)} %dynamic_slice.191, bf16[4096,2048]{1,0:T(8,128)(2,1)} %param.37, s32[]{:T(128)S(6)} %select_n.188, bf16[256,2048]{1,0:T(8,128)(2,1)} %collective-permute-done.49, bf16[256,2048]{1,0:T(8,128)(2,1)} %collective-permute-done.48), kind=kOutput, calls=%fused_computation.104 | convolution fusion | flops 2163212288 | bytes 9441284 | tf_op jit(solution)/shard_map/dot_general | solution.py:27
  352.8 2.8 fusion.119
  355.7 2.6 fusion.113
  358.3 4.4 fusion.116
  362.8 3.6 fusion.103
  366.4 3.6 fusion.128
  370.0 3.9 fusion.122
  374.0 4.3 fusion.125
  378.3 6.0 %fusion.111 = f32[512,1024]{1,0:T(8,128)} fusion(bf16[2048,2048]{1,0:T(8,128)(2,1)S(1)} %constant_dynamic-update-slice_fusion, s32[]{:T(128)S(6)} %select_n.175, bf16[512,1024]{1,0:T(8,128)(2,1)} %copy-done.72, bf16[512,1024]{1,0:T(8,128)(2,1)} %fusion.56, bf16[512,1024]{1,0:T(8,128)(2,1)} %copy-done.73, bf16[512,1024]{1,0:T(8,128)(2,1)S(1)} %copy-done.24), kind=kOutput, calls=%fused_computation.172 | convolution fusion | flops 2164260864 | bytes 8388612 | tf_op jit(solution)/shard_map/dot_general | solution.py:23
  395.6 7.9 %collective-permute-done.58 = bf16[256,1024]{1,0:T(8,128)(2,1)S(1)} collective-permute-done((bf16[256,1024]{1,0:T(8,128)(2,1)S(1)}, bf16[256,1024]{1,0:T(8,128)(2,1)S(1)}, u32[]{:S(2)}, u32[]{:S(2)}) %collective-permute-start.58) | collective-permute-done | bytes 524320 | tf_op jit(solution)/shard_map/ppermute | solution.py:243
  407.5 16.3 %collective-permute-done.67 = bf16[512,512]{1,0:T(8,128)(2,1)S(1)} collective-permute-done((bf16[512,512]{1,0:T(8,128)(2,1)S(1)}, bf16[512,512]{1,0:T(8,128)(2,1)S(1)}, u32[]{:S(2)}, u32[]{:S(2)}) %collective-permute-start.67) | collective-permute-done | bytes 524320 | tf_op jit(solution)/shard_map/ppermute | solution.py:243
  424.9 3.6 fusion.41
  437.1 2.7 collective-permute-start.22
  444.3 3.5 fusion.151
  461.4 7.4 %collective-permute-done.57 = bf16[256,1024]{1,0:T(8,128)(2,1)S(1)} collective-permute-done((bf16[256,1024]{1,0:T(8,128)(2,1)}, bf16[256,1024]{1,0:T(8,128)(2,1)S(1)}, u32[]{:S(2)}, u32[]{:S(2)}) %collective-permute-start.57) | collective-permute-done | bytes 524320 | tf_op jit(solution)/shard_map/ppermute | solution.py:243
  470.9 8.9 %collective-permute-done.59 = bf16[256,1024]{1,0:T(8,128)(2,1)S(1)} collective-permute-done((bf16[256,1024]{1,0:T(8,128)(2,1)S(1)}, bf16[256,1024]{1,0:T(8,128)(2,1)S(1)}, u32[]{:S(2)}, u32[]{:S(2)}) %collective-permute-start.59) | collective-permute-done | bytes 524320 | tf_op jit(solution)/shard_map/ppermute | solution.py:243
  480.7 10.6 %collective-permute-done.56 = bf16[256,1024]{1,0:T(8,128)(2,1)S(1)} collective-permute-done((bf16[256,1024]{1,0:T(8,128)(2,1)}, bf16[256,1024]{1,0:T(8,128)(2,1)S(1)}, u32[]{:S(2)}, u32[]{:S(2)}) %collective-permute-start.56) | collective-permute-done | bytes 524320 | tf_op jit(solution)/shard_map/ppermute | solution.py:243
  491.3 4.1 collective-permute-start.31
  497.3 2.4 collective-permute-start.60
  502.5 3.6 collective-permute-done.31
  507.2 22.1 %collective-permute-done.30 = bf16[128,1152]{1,0:T(8,128)(2,1)S(1)} collective-permute-done((bf16[128,1152]{1,0:T(8,128)(2,1)S(1)}, bf16[128,1152]{1,0:T(8,128)(2,1)S(1)}, u32[]{:S(2)}, u32[]{:S(2)}) %collective-permute-start.30) | collective-permute-done | bytes 294944 | tf_op jit(solution)/shard_map/ppermute | solution.py:248
  532.3 3.0 collective-permute-start.71
  535.4 5.6 %collective-permute-done.69 = bf16[1024,128]{1,0:T(8,128)(2,1)S(1)} collective-permute-done((bf16[1024,128]{1,0:T(8,128)(2,1)S(1)}, bf16[1024,128]{1,0:T(8,128)(2,1)S(1)}, u32[]{:S(2)}, u32[]{:S(2)}) %collective-permute-start.69) | collective-permute-done | bytes 262176 | tf_op jit(solution)/shard_map/ppermute | solution.py:248
  541.1 15.5 %collective-permute-done.70 = bf16[1024,128]{1,0:T(8,128)(2,1)S(1)} collective-permute-done((bf16[1024,128]{1,0:T(8,128)(2,1)S(1)}, bf16[1024,128]{1,0:T(8,128)(2,1)S(1)}, u32[]{:S(2)}, u32[]{:S(2)}) %collective-permute-start.70) | collective-permute-done | bytes 262176 | tf_op jit(solution)/shard_map/ppermute | solution.py:248
  (406 shorter events, 144.9 us)
Async XLA Ops:
  5.6 10.9 %collective-permute-start.3 = (bf16[256,256]{0,1:T(8,128)(2,1)S(1)}, bf16[256,256]{0,1:T(8,128)(2,1)S(1)}, u32[]{:S(2)}, u32[]{:S(2)}) collective-permute-start(bf16[256,256]{0,1:T(8,128)(2,1)S(1)} %get-tuple-element.162), channel_id=1, source_target_pairs={{0,6},{1,7},{8,14},{9,15},{16,22},{17,23},{24,30},{25,31}} | collective-permute-start | bytes 393224 | tf_op jit(solution)/shard_map/ppermute | solution.py:253
  12.5 6.7 %collective-permute-start.2 = (bf16[256,256]{0,1:T(8,128)(2,1)S(1)}, bf16[256,256]{0,1:T(8,128)(2,1)S(1)}, u32[]{:S(2)}, u32[]{:S(2)}) collective-permute-start(bf16[256,256]{0,1:T(8,128)(2,1)S(1)} %get-tuple-element.162), channel_id=1, source_target_pairs={{0,4},{2,6},{1,5},{3,7},{8,12},{10,14},{9,13},{11,15},{16,20},{18,... | collective-permute-start | bytes 393224 | tf_op jit(solution)/shard_map/ppermute | solution.py:253
  13.8 7.1 %collective-permute-start.1 = (bf16[256,256]{0,1:T(8,128)(2,1)S(1)}, bf16[256,256]{0,1:T(8,128)(2,1)S(1)}, u32[]{:S(2)}, u32[]{:S(2)}) collective-permute-start(bf16[256,256]{0,1:T(8,128)(2,1)S(1)} %get-tuple-element.162), channel_id=1, source_target_pairs={{0,2},{2,4},{4,6},{1,3},{3,5},{5,7},{8,10},{10,12},{12,14},{9,11},... | collective-permute-start | bytes 393224 | tf_op jit(solution)/shard_map/ppermute | solution.py:253
  21.0 9.8 %collective-permute-start.4 = (bf16[4,256,256]{1,2,0:T(8,128)(2,1)S(1)}, bf16[4,256,256]{1,2,0:T(8,128)(2,1)S(1)}, u32[]{:S(2)}, u32[]{:S(2)}) collective-permute-start(bf16[4,256,256]{1,2,0:T(8,128)(2,1)S(1)} %get-tuple-element.160), channel_id=1, source_target_pairs={{0,1},{1,0},{2,3},{3,2},{4,5},{5,4},{6,7},{7,6},{8,9},{9,8},{10,11... | collective-permute-start | bytes 1572872 | tf_op jit(solution)/shard_map/ppermute | solution.py:238
  21.1 16.9 %collective-permute-start = (bf16[256,2048]{1,0:T(8,128)(2,1)S(1)}, bf16[256,2048]{1,0:T(8,128)(2,1)}, u32[]{:S(2)}, u32[]{:S(2)}) collective-permute-start(bf16[256,2048]{1,0:T(8,128)(2,1)S(1)} %fusion.35), channel_id=1, source_target_pairs={{0,1},{1,0},{2,3},{3,2},{4,5},{5,4},{6,7},{7,6},{8,9},{9,8},{10,11... | collective-permute-start | bytes 3145736 | tf_op jit(solution)/shard_map/ppermute | solution.py:238
  21.6 32.9 %collective-permute-start.48 = (bf16[256,2048]{1,0:T(8,128)(2,1)}, bf16[256,2048]{1,0:T(8,128)(2,1)}, u32[]{:S(2)}, u32[]{:S(2)}) collective-permute-start(bf16[256,2048]{1,0:T(8,128)(2,1)} %bitcast.19), channel_id=1, source_target_pairs={{0,2},{2,4},{4,6},{6,0},{1,3},{3,5},{5,7},{7,1},{8,10},{10,12},{12... | collective-permute-start | bytes 3145736 | tf_op jit(solution)/shard_map/ppermute | solution.py:248
  51.7 10.7 %collective-permute-start.5 = (bf16[256,2048]{1,0:T(8,128)(2,1)}, bf16[256,2048]{1,0:T(8,128)(2,1)}, u32[]{:S(2)}, u32[]{:S(2)}) collective-permute-start(bf16[256,2048]{1,0:T(8,128)(2,1)} %convolution_convert_fusion.6), channel_id=1, source_target_pairs={{0,1},{1,0},{2,3},{3,2},{4,5},{5,4},{6,7},{7,6},{8,9},{9,8},{10,11... | collective-permute-start | bytes 3145736 | tf_op jit(solution)/shard_map/ppermute | solution.py:238
  51.7 18.9 %collective-permute-start.8 = (bf16[256,2048]{1,0:T(8,128)(2,1)}, bf16[256,2048]{1,0:T(8,128)(2,1)}, u32[]{:S(2)}, u32[]{:S(2)}) collective-permute-start(bf16[256,2048]{1,0:T(8,128)(2,1)} %bitcast.19), channel_id=1, source_target_pairs={{0,1},{1,0},{2,3},{3,2},{4,5},{5,4},{6,7},{7,6},{8,9},{9,8},{10,11... | collective-permute-start | bytes 3145736 | tf_op jit(solution)/shard_map/ppermute | solution.py:238
  54.5 40.1 %collective-permute-start.50 = (bf16[256,2048]{1,0:T(8,128)(2,1)}, bf16[256,2048]{1,0:T(8,128)(2,1)}, u32[]{:S(2)}, u32[]{:S(2)}) collective-permute-start(bf16[256,2048]{1,0:T(8,128)(2,1)} %collective-permute-done.48), channel_id=1, source_target_pairs={{0,2},{2,4},{4,6},{6,0},{1,3},{3,5},{5,7},{7,1},{8,10},{10,12},{12... | collective-permute-start | bytes 3145736 | tf_op jit(solution)/shard_map/ppermute | solution.py:248
  62.4 32.3 %collective-permute-start.49 = (bf16[256,2048]{1,0:T(8,128)(2,1)}, bf16[256,2048]{1,0:T(8,128)(2,1)}, u32[]{:S(2)}, u32[]{:S(2)}) collective-permute-start(bf16[256,2048]{1,0:T(8,128)(2,1)} %collective-permute-done.48), channel_id=1, source_target_pairs={{0,1},{1,0},{2,3},{3,2},{4,5},{5,4},{6,7},{7,6},{8,9},{9,8},{10,11... | collective-permute-start | bytes 3145736 | tf_op jit(solution)/shard_map/ppermute | solution.py:238
  69.0 30.2 %collective-permute-start.6 = (bf16[256,2048]{1,0:T(8,128)(2,1)}, bf16[256,2048]{1,0:T(8,128)(2,1)S(1)}, u32[]{:S(2)}, u32[]{:S(2)}) collective-permute-start(bf16[256,2048]{1,0:T(8,128)(2,1)} %get-tuple-element.115), channel_id=1, source_target_pairs={{0,1},{1,0},{2,3},{3,2},{4,5},{5,4},{6,7},{7,6},{8,9},{9,8},{10,11... | collective-permute-start | bytes 3145736 | tf_op jit(solution)/shard_map/ppermute | solution.py:238
  75.3 85.5 %collective-permute-start.42 = (bf16[256,2048]{1,0:T(8,128)(2,1)}, bf16[256,2048]{1,0:T(8,128)(2,1)}, u32[]{:S(2)}, u32[]{:S(2)}) collective-permute-start(bf16[256,2048]{1,0:T(8,128)(2,1)} %get-tuple-element.115), channel_id=1, source_target_pairs={{0,2},{2,4},{4,6},{6,0},{1,3},{3,5},{5,7},{7,1},{8,10},{10,12},{12... | collective-permute-start | bytes 3145736 | tf_op jit(solution)/shard_map/ppermute | solution.py:248
  94.6 72.9 %collective-permute-start.52 = (bf16[256,2048]{1,0:T(8,128)(2,1)}, bf16[256,2048]{1,0:T(8,128)(2,1)}, u32[]{:S(2)}, u32[]{:S(2)}) collective-permute-start(bf16[256,2048]{1,0:T(8,128)(2,1)} %collective-permute-done.50), channel_id=1, source_target_pairs={{0,2},{2,4},{4,6},{6,0},{1,3},{3,5},{5,7},{7,1},{8,10},{10,12},{12... | collective-permute-start | bytes 3145736 | tf_op jit(solution)/shard_map/ppermute | solution.py:248
  94.6 73.6 %collective-permute-start.51 = (bf16[256,2048]{1,0:T(8,128)(2,1)}, bf16[256,2048]{1,0:T(8,128)(2,1)}, u32[]{:S(2)}, u32[]{:S(2)}) collective-permute-start(bf16[256,2048]{1,0:T(8,128)(2,1)} %collective-permute-done.50), channel_id=1, source_target_pairs={{0,1},{1,0},{2,3},{3,2},{4,5},{5,4},{6,7},{7,6},{8,9},{9,8},{10,11... | collective-permute-start | bytes 3145736 | tf_op jit(solution)/shard_map/ppermute | solution.py:238
  148.4 31.9 %collective-permute-start.9 = (bf16[256,2048]{1,0:T(8,128)(2,1)}, bf16[256,2048]{1,0:T(8,128)(2,1)}, u32[]{:S(2)}, u32[]{:S(2)}) collective-permute-start(bf16[256,2048]{1,0:T(8,128)(2,1)} %convolution_convert_fusion.4), channel_id=1, source_target_pairs={{0,1},{1,0},{2,3},{3,2},{4,5},{5,4},{6,7},{7,6},{8,9},{9,8},{10,11... | collective-permute-start | bytes 3145736 | tf_op jit(solution)/shard_map/ppermute | solution.py:238
  160.8 32.6 %collective-permute-start.7 = (bf16[256,2048]{1,0:T(8,128)(2,1)}, bf16[256,2048]{1,0:T(8,128)(2,1)}, u32[]{:S(2)}, u32[]{:S(2)}) collective-permute-start(bf16[256,2048]{1,0:T(8,128)(2,1)} %convolution_convert_fusion.5), channel_id=1, source_target_pairs={{0,1},{1,0},{2,3},{3,2},{4,5},{5,4},{6,7},{7,6},{8,9},{9,8},{10,11... | collective-permute-start | bytes 3145736 | tf_op jit(solution)/shard_map/ppermute | solution.py:238
  160.8 49.5 %collective-permute-start.43 = (bf16[256,2048]{1,0:T(8,128)(2,1)}, bf16[256,2048]{1,0:T(8,128)(2,1)}, u32[]{:S(2)}, u32[]{:S(2)}) collective-permute-start(bf16[256,2048]{1,0:T(8,128)(2,1)} %collective-permute-done.42), channel_id=1, source_target_pairs={{0,1},{1,0},{2,3},{3,2},{4,5},{5,4},{6,7},{7,6},{8,9},{9,8},{10,11... | collective-permute-start | bytes 3145736 | tf_op jit(solution)/shard_map/ppermute | solution.py:238
  167.6 40.2 %collective-permute-start.44 = (bf16[256,2048]{1,0:T(8,128)(2,1)}, bf16[256,2048]{1,0:T(8,128)(2,1)}, u32[]{:S(2)}, u32[]{:S(2)}) collective-permute-start(bf16[256,2048]{1,0:T(8,128)(2,1)} %collective-permute-done.42), channel_id=1, source_target_pairs={{0,2},{2,4},{4,6},{6,0},{1,3},{3,5},{5,7},{7,1},{8,10},{10,12},{12... | collective-permute-start | bytes 3145736 | tf_op jit(solution)/shard_map/ppermute | solution.py:248
  168.3 46.8 %collective-permute-start.53 = (bf16[256,2048]{1,0:T(8,128)(2,1)}, bf16[256,2048]{1,0:T(8,128)(2,1)}, u32[]{:S(2)}, u32[]{:S(2)}) collective-permute-start(bf16[256,2048]{1,0:T(8,128)(2,1)} %collective-permute-done.52), channel_id=1, source_target_pairs={{0,1},{1,0},{2,3},{3,2},{4,5},{5,4},{6,7},{7,6},{8,9},{9,8},{10,11... | collective-permute-start | bytes 3145736 | tf_op jit(solution)/shard_map/ppermute | solution.py:238
  198.8 18.6 %collective-permute-start.10 = (bf16[256,2048]{1,0:T(8,128)(2,1)}, bf16[256,2048]{1,0:T(8,128)(2,1)S(1)}, u32[]{:S(2)}, u32[]{:S(2)}) collective-permute-start(bf16[256,2048]{1,0:T(8,128)(2,1)} %get-tuple-element.119), channel_id=1, source_target_pairs={{0,1},{1,0},{2,3},{3,2},{4,5},{5,4},{6,7},{7,6},{8,9},{9,8},{10,11... | collective-permute-start | bytes 3145736 | tf_op jit(solution)/shard_map/ppermute | solution.py:238
  207.8 37.6 %collective-permute-start.45 = (bf16[256,2048]{1,0:T(8,128)(2,1)}, bf16[256,2048]{1,0:T(8,128)(2,1)S(1)}, u32[]{:S(2)}, u32[]{:S(2)}) collective-permute-start(bf16[256,2048]{1,0:T(8,128)(2,1)} %collective-permute-done.44), channel_id=1, source_target_pairs={{0,1},{1,0},{2,3},{3,2},{4,5},{5,4},{6,7},{7,6},{8,9},{9,8},{10,11... | collective-permute-start | bytes 3145736 | tf_op jit(solution)/shard_map/ppermute | solution.py:238
  207.8 56.6 %collective-permute-start.46 = (bf16[256,2048]{1,0:T(8,128)(2,1)}, bf16[256,2048]{1,0:T(8,128)(2,1)}, u32[]{:S(2)}, u32[]{:S(2)}) collective-permute-start(bf16[256,2048]{1,0:T(8,128)(2,1)} %collective-permute-done.44), channel_id=1, source_target_pairs={{0,2},{2,4},{4,6},{6,0},{1,3},{3,5},{5,7},{7,1},{8,10},{10,12},{12... | collective-permute-start | bytes 3145736 | tf_op jit(solution)/shard_map/ppermute | solution.py:248
  232.2 35.1 %collective-permute-start.11 = (bf16[4,2,256,128]{3,2,1,0:T(8,128)(2,1)}, bf16[4,2,256,128]{3,2,1,0:T(8,128)(2,1)}, u32[]{:S(2)}, u32[]{:S(2)}) collective-permute-start(bf16[4,2,256,128]{3,2,1,0:T(8,128)(2,1)} %dynamic-slice_bitcast_fusion), channel_id=1, source_target_pairs={{0,1},{1,0},{2,3},{3,2},{4,5},{5,4},{6,7},{7,6},{8,9},{9,8},{10,11... | collective-permute-start | bytes 1572872 | tf_op jit(solution)/shard_map/ppermute | solution.py:238
  235.2 34.8 %collective-permute-start.37 = (bf16[512,512]{1,0:T(8,128)(2,1)}, bf16[512,512]{1,0:T(8,128)(2,1)}, u32[]{:S(2)}, u32[]{:S(2)}) collective-permute-start(bf16[512,512]{1,0:T(8,128)(2,1)} %get-tuple-element.148), channel_id=1, source_target_pairs={{0,16},{8,24},{16,0},{24,8},{1,17},{9,25},{17,1},{25,9},{2,18},{10... | collective-permute-start | bytes 1572872 | tf_op jit(solution)/shard_map/ppermute | solution.py:243
  239.3 75.1 %collective-permute-start.36 = (bf16[512,512]{1,0:T(8,128)(2,1)}, bf16[512,512]{1,0:T(8,128)(2,1)}, u32[]{:S(2)}, u32[]{:S(2)}) collective-permute-start(bf16[512,512]{1,0:T(8,128)(2,1)} %slice.290), channel_id=1, source_target_pairs={{0,16},{8,24},{16,0},{24,8},{1,17},{9,25},{17,1},{25,9},{2,18},{10... | collective-permute-start | bytes 1572872 | tf_op jit(solution)/shard_map/ppermute | solution.py:243
  245.5 27.8 %collective-permute-start.34 = (bf16[512,512]{1,0:T(8,128)(2,1)}, bf16[512,512]{1,0:T(8,128)(2,1)}, u32[]{:S(2)}, u32[]{:S(2)}) collective-permute-start(bf16[512,512]{1,0:T(8,128)(2,1)} %get-tuple-element.149), channel_id=1, source_target_pairs={{0,8},{8,0},{16,24},{24,16},{1,9},{9,1},{17,25},{25,17},{2,10},{10... | collective-permute-start | bytes 1572872 | tf_op jit(solution)/shard_map/ppermute | solution.py:243
  264.4 51.5 %collective-permute-start.33 = (bf16[512,512]{1,0:T(8,128)(2,1)}, bf16[512,512]{1,0:T(8,128)(2,1)}, u32[]{:S(2)}, u32[]{:S(2)}) collective-permute-start(bf16[512,512]{1,0:T(8,128)(2,1)} %slice.286), channel_id=1, source_target_pairs={{0,8},{8,0},{16,24},{24,16},{1,9},{9,1},{17,25},{25,17},{2,10},{10... | collective-permute-start | bytes 1572872 | tf_op jit(solution)/shard_map/ppermute | solution.py:243
  268.5 27.3 %collective-permute-start.14 = (bf16[512,128]{1,0:T(8,128)(2,1)S(1)}, bf16[512,128]{1,0:T(8,128)(2,1)S(1)}, u32[]{:S(2)}, u32[]{:S(2)}) collective-permute-start(bf16[512,128]{1,0:T(8,128)(2,1)S(1)} %bitcast.140), channel_id=1, source_target_pairs={{6,0},{7,1},{14,8},{15,9},{22,16},{23,17},{30,24},{31,25}} | collective-permute-start | bytes 393224 | tf_op jit(solution)/shard_map/ppermute | solution.py:258
  270.0 25.8 %collective-permute-start.13 = (bf16[512,128]{1,0:T(8,128)(2,1)S(1)}, bf16[512,128]{1,0:T(8,128)(2,1)S(1)}, u32[]{:S(2)}, u32[]{:S(2)}) collective-permute-start(bf16[512,128]{1,0:T(8,128)(2,1)S(1)} %bitcast.139), channel_id=1, source_target_pairs={{4,0},{6,2},{5,1},{7,3},{12,8},{14,10},{13,9},{15,11},{20,16},{22,... | collective-permute-start | bytes 393224 | tf_op jit(solution)/shard_map/ppermute | solution.py:258
  273.3 23.9 %collective-permute-start.12 = (bf16[512,128]{1,0:T(8,128)(2,1)S(1)}, bf16[512,128]{1,0:T(8,128)(2,1)S(1)}, u32[]{:S(2)}, u32[]{:S(2)}) collective-permute-start(bf16[512,128]{1,0:T(8,128)(2,1)S(1)} %bitcast.138), channel_id=1, source_target_pairs={{2,0},{4,2},{6,4},{3,1},{5,3},{7,5},{10,8},{12,10},{14,12},{11,9},... | collective-permute-start | bytes 393224 | tf_op jit(solution)/shard_map/ppermute | solution.py:258
  295.8 27.4 %collective-permute-start.47 = (bf16[256,2048]{1,0:T(8,128)(2,1)}, bf16[256,2048]{1,0:T(8,128)(2,1)}, u32[]{:S(2)}, u32[]{:S(2)}) collective-permute-start(bf16[256,2048]{1,0:T(8,128)(2,1)} %collective-permute-done.46), channel_id=1, source_target_pairs={{0,1},{1,0},{2,3},{3,2},{4,5},{5,4},{6,7},{7,6},{8,9},{9,8},{10,11... | collective-permute-start | bytes 3145736 | tf_op jit(solution)/shard_map/ppermute | solution.py:238
  295.8 20.7 %collective-permute-start.38 = (bf16[512,512]{1,0:T(8,128)(2,1)}, bf16[512,512]{1,0:T(8,128)(2,1)}, u32[]{:S(2)}, u32[]{:S(2)}) collective-permute-start(bf16[512,512]{1,0:T(8,128)(2,1)} %add_convert_fusion.9), channel_id=1, source_target_pairs={{0,8},{8,0},{16,24},{24,16},{1,9},{9,1},{17,25},{25,17},{2,10},{10... | collective-permute-start | bytes 1572872 | tf_op jit(solution)/shard_map/ppermute | solution.py:243
  297.2 19.3 %collective-permute-start.35 = (bf16[512,512]{1,0:T(8,128)(2,1)}, bf16[512,512]{1,0:T(8,128)(2,1)}, u32[]{:S(2)}, u32[]{:S(2)}) collective-permute-start(bf16[512,512]{1,0:T(8,128)(2,1)} %add_convert_fusion.10), channel_id=1, source_target_pairs={{0,16},{8,24},{16,0},{24,8},{1,17},{9,25},{17,1},{25,9},{2,18},{10... | collective-permute-start | bytes 1572872 | tf_op jit(solution)/shard_map/ppermute | solution.py:243
  314.4 74.3 %collective-permute-start.27 = (bf16[256,1152]{1,0:T(8,128)(2,1)S(1)}, bf16[256,1152]{1,0:T(8,128)(2,1)S(1)}, u32[]{:S(2)}, u32[]{:S(2)}) collective-permute-start(bf16[256,1152]{1,0:T(8,128)(2,1)S(1)} %copy-done.33), channel_id=1, source_target_pairs={{0,16},{8,24},{16,0},{24,8},{1,17},{9,25},{17,1},{25,9},{2,18},{10... | collective-permute-start | bytes 1769480 | tf_op jit(solution)/shard_map/ppermute | solution.py:243
  315.9 74.5 %collective-permute-start.24 = (bf16[256,1152]{1,0:T(8,128)(2,1)S(1)}, bf16[256,1152]{1,0:T(8,128)(2,1)S(1)}, u32[]{:S(2)}, u32[]{:S(2)}) collective-permute-start(bf16[256,1152]{1,0:T(8,128)(2,1)S(1)} %copy-done.32), channel_id=1, source_target_pairs={{0,8},{8,0},{16,24},{24,16},{1,9},{9,1},{17,25},{25,17},{2,10},{10... | collective-permute-start | bytes 1769480 | tf_op jit(solution)/shard_map/ppermute | solution.py:243
  318.8 73.8 %collective-permute-start.41 = (bf16[1024,128]{1,0:T(8,128)(2,1)S(1)}, bf16[1024,128]{1,0:T(8,128)(2,1)S(1)}, u32[]{:S(2)}, u32[]{:S(2)}) collective-permute-start(bf16[1024,128]{1,0:T(8,128)(2,1)S(1)} %get-tuple-element.146), channel_id=1, source_target_pairs={{0,6},{2,0},{4,2},{6,4},{1,7},{3,1},{5,3},{7,5},{8,14},{10,8},{12,... | collective-permute-start | bytes 786440 | tf_op jit(solution)/shard_map/ppermute | solution.py:248
  321.9 70.7 %collective-permute-start.40 = (bf16[1024,128]{1,0:T(8,128)(2,1)S(1)}, bf16[1024,128]{1,0:T(8,128)(2,1)S(1)}, u32[]{:S(2)}, u32[]{:S(2)}) collective-permute-start(bf16[1024,128]{1,0:T(8,128)(2,1)S(1)} %get-tuple-element.147), channel_id=1, source_target_pairs={{0,4},{2,6},{4,0},{6,2},{1,5},{3,7},{5,1},{7,3},{8,12},{10,14},{12... | collective-permute-start | bytes 786440 | tf_op jit(solution)/shard_map/ppermute | solution.py:248
  323.2 70.0 %collective-permute-start.39 = (bf16[1024,128]{1,0:T(8,128)(2,1)S(1)}, bf16[1024,128]{1,0:T(8,128)(2,1)S(1)}, u32[]{:S(2)}, u32[]{:S(2)}) collective-permute-start(bf16[1024,128]{1,0:T(8,128)(2,1)S(1)} %get-tuple-element.145), channel_id=1, source_target_pairs={{0,2},{2,4},{4,6},{6,0},{1,3},{3,5},{5,7},{7,1},{8,10},{10,12},{12... | collective-permute-start | bytes 786440 | tf_op jit(solution)/shard_map/ppermute | solution.py:248
  388.6 14.9 %collective-permute-start.58 = (bf16[256,1024]{1,0:T(8,128)(2,1)S(1)}, bf16[256,1024]{1,0:T(8,128)(2,1)S(1)}, u32[]{:S(2)}, u32[]{:S(2)}) collective-permute-start(bf16[256,1024]{1,0:T(8,128)(2,1)S(1)} %get-tuple-element.143), channel_id=1, source_target_pairs={{0,16},{8,24},{16,0},{24,8},{1,17},{9,25},{17,1},{25,9},{2,18},{10... | collective-permute-start | bytes 1572872 | tf_op jit(solution)/shard_map/ppermute | solution.py:243
  390.3 15.0 %collective-permute-start.55 = (bf16[256,1024]{1,0:T(8,128)(2,1)S(1)}, bf16[256,1024]{1,0:T(8,128)(2,1)S(1)}, u32[]{:S(2)}, u32[]{:S(2)}) collective-permute-start(bf16[256,1024]{1,0:T(8,128)(2,1)S(1)} %get-tuple-element.144), channel_id=1, source_target_pairs={{0,8},{8,0},{16,24},{24,16},{1,9},{9,1},{17,25},{25,17},{2,10},{10... | collective-permute-start | bytes 1572872 | tf_op jit(solution)/shard_map/ppermute | solution.py:243
  392.6 32.3 %collective-permute-start.15 = (bf16[256,2048]{1,0:T(8,128)(2,1)S(1)}, bf16[256,2048]{1,0:T(8,128)(2,1)S(1)}, u32[]{:S(2)}, u32[]{:S(2)}) collective-permute-start(bf16[256,2048]{1,0:T(8,128)(2,1)S(1)} %copy-done.62), channel_id=1, source_target_pairs={{0,1},{1,0},{2,3},{3,2},{4,5},{5,4},{6,7},{7,6},{8,9},{9,8},{10,11... | collective-permute-start | bytes 3145736 | tf_op jit(solution)/shard_map/ppermute | solution.py:238
  392.6 60.9 %collective-permute-start.26 = (bf16[256,1152]{1,0:T(8,128)(2,1)}, bf16[256,1152]{1,0:T(8,128)(2,1)}, u32[]{:S(2)}, u32[]{:S(2)}) collective-permute-start(bf16[256,1152]{1,0:T(8,128)(2,1)} %slice.280), channel_id=1, source_target_pairs={{0,16},{8,24},{16,0},{24,8},{1,17},{9,25},{17,1},{25,9},{2,18},{10... | collective-permute-start | bytes 1769480 | tf_op jit(solution)/shard_map/ppermute | solution.py:243
  393.3 61.3 %collective-permute-start.23 = (bf16[256,1152]{1,0:T(8,128)(2,1)}, bf16[256,1152]{1,0:T(8,128)(2,1)}, u32[]{:S(2)}, u32[]{:S(2)}) collective-permute-start(bf16[256,1152]{1,0:T(8,128)(2,1)} %slice.276), channel_id=1, source_target_pairs={{0,8},{8,0},{16,24},{24,16},{1,9},{9,1},{17,25},{25,17},{2,10},{10... | collective-permute-start | bytes 1769480 | tf_op jit(solution)/shard_map/ppermute | solution.py:243
  403.5 20.4 %collective-permute-start.67 = (bf16[512,512]{1,0:T(8,128)(2,1)S(1)}, bf16[512,512]{1,0:T(8,128)(2,1)S(1)}, u32[]{:S(2)}, u32[]{:S(2)}) collective-permute-start(bf16[512,512]{1,0:T(8,128)(2,1)S(1)} %get-tuple-element.138), channel_id=1, source_target_pairs={{0,16},{8,24},{16,0},{24,8},{1,17},{9,25},{17,1},{25,9},{2,18},{10... | collective-permute-start | bytes 1572872 | tf_op jit(solution)/shard_map/ppermute | solution.py:243
  405.3 23.7 %collective-permute-start.64 = (bf16[512,512]{1,0:T(8,128)(2,1)}, bf16[512,512]{1,0:T(8,128)(2,1)}, u32[]{:S(2)}, u32[]{:S(2)}) collective-permute-start(bf16[512,512]{1,0:T(8,128)(2,1)} %get-tuple-element.139), channel_id=1, source_target_pairs={{0,8},{8,0},{16,24},{24,16},{1,9},{9,1},{17,25},{25,17},{2,10},{10... | collective-permute-start | bytes 1572872 | tf_op jit(solution)/shard_map/ppermute | solution.py:243
  435.9 19.7 %collective-permute-start.28 = (bf16[256,1152]{1,0:T(8,128)(2,1)}, bf16[256,1152]{1,0:T(8,128)(2,1)S(1)}, u32[]{:S(2)}, u32[]{:S(2)}) collective-permute-start(bf16[256,1152]{1,0:T(8,128)(2,1)} %add_convert_fusion.3), channel_id=1, source_target_pairs={{0,8},{8,0},{16,24},{24,16},{1,9},{9,1},{17,25},{25,17},{2,10},{10... | collective-permute-start | bytes 1769480 | tf_op jit(solution)/shard_map/ppermute | solution.py:243
  441.2 16.5 %collective-permute-start.25 = (bf16[256,1152]{1,0:T(8,128)(2,1)}, bf16[256,1152]{1,0:T(8,128)(2,1)S(1)}, u32[]{:S(2)}, u32[]{:S(2)}) collective-permute-start(bf16[256,1152]{1,0:T(8,128)(2,1)} %add_convert_fusion.4), channel_id=1, source_target_pairs={{0,16},{8,24},{16,0},{24,8},{1,17},{9,25},{17,1},{25,9},{2,18},{10... | collective-permute-start | bytes 1769480 | tf_op jit(solution)/shard_map/ppermute | solution.py:243
  449.7 19.1 %collective-permute-start.57 = (bf16[256,1024]{1,0:T(8,128)(2,1)}, bf16[256,1024]{1,0:T(8,128)(2,1)S(1)}, u32[]{:S(2)}, u32[]{:S(2)}) collective-permute-start(bf16[256,1024]{1,0:T(8,128)(2,1)} %slice.298), channel_id=1, source_target_pairs={{0,16},{8,24},{16,0},{24,8},{1,17},{9,25},{17,1},{25,9},{2,18},{10... | collective-permute-start | bytes 1572872 | tf_op jit(solution)/shard_map/ppermute | solution.py:243
  453.5 16.7 %collective-permute-start.54 = (bf16[256,1024]{1,0:T(8,128)(2,1)}, bf16[256,1024]{1,0:T(8,128)(2,1)S(1)}, u32[]{:S(2)}, u32[]{:S(2)}) collective-permute-start(bf16[256,1024]{1,0:T(8,128)(2,1)} %slice.294), channel_id=1, source_target_pairs={{0,8},{8,0},{16,24},{24,16},{1,9},{9,1},{17,25},{25,17},{2,10},{10... | collective-permute-start | bytes 1572872 | tf_op jit(solution)/shard_map/ppermute | solution.py:243
  454.5 41.7 %collective-permute-start.66 = (bf16[512,512]{1,0:T(8,128)(2,1)}, bf16[512,512]{1,0:T(8,128)(2,1)S(1)}, u32[]{:S(2)}, u32[]{:S(2)}) collective-permute-start(bf16[512,512]{1,0:T(8,128)(2,1)} %slice.306), channel_id=1, source_target_pairs={{0,16},{8,24},{16,0},{24,8},{1,17},{9,25},{17,1},{25,9},{2,18},{10... | collective-permute-start | bytes 1572872 | tf_op jit(solution)/shard_map/ppermute | solution.py:243
  455.6 24.2 %collective-permute-start.59 = (bf16[256,1024]{1,0:T(8,128)(2,1)S(1)}, bf16[256,1024]{1,0:T(8,128)(2,1)S(1)}, u32[]{:S(2)}, u32[]{:S(2)}) collective-permute-start(bf16[256,1024]{1,0:T(8,128)(2,1)S(1)} %copy-done.35), channel_id=1, source_target_pairs={{0,8},{8,0},{16,24},{24,16},{1,9},{9,1},{17,25},{25,17},{2,10},{10... | collective-permute-start | bytes 1572872 | tf_op jit(solution)/shard_map/ppermute | solution.py:243
  457.6 33.7 %collective-permute-start.56 = (bf16[256,1024]{1,0:T(8,128)(2,1)}, bf16[256,1024]{1,0:T(8,128)(2,1)S(1)}, u32[]{:S(2)}, u32[]{:S(2)}) collective-permute-start(bf16[256,1024]{1,0:T(8,128)(2,1)} %add_convert_fusion.8), channel_id=1, source_target_pairs={{0,16},{8,24},{16,0},{24,8},{1,17},{9,25},{17,1},{25,9},{2,18},{10... | collective-permute-start | bytes 1572872 | tf_op jit(solution)/shard_map/ppermute | solution.py:243
  468.9 27.4 %collective-permute-start.63 = (bf16[512,512]{1,0:T(8,128)(2,1)S(1)}, bf16[512,512]{1,0:T(8,128)(2,1)S(1)}, u32[]{:S(2)}, u32[]{:S(2)}) collective-permute-start(bf16[512,512]{1,0:T(8,128)(2,1)S(1)} %copy-done.38), channel_id=1, source_target_pairs={{0,8},{8,0},{16,24},{24,16},{1,9},{9,1},{17,25},{25,17},{2,10},{10... | collective-permute-start | bytes 1572872 | tf_op jit(solution)/shard_map/ppermute | solution.py:243
  470.2 27.1 %collective-permute-start.68 = (bf16[512,512]{1,0:T(8,128)(2,1)S(1)}, bf16[512,512]{1,0:T(8,128)(2,1)S(1)}, u32[]{:S(2)}, u32[]{:S(2)}) collective-permute-start(bf16[512,512]{1,0:T(8,128)(2,1)S(1)} %copy-done.34), channel_id=1, source_target_pairs={{0,8},{8,0},{16,24},{24,16},{1,9},{9,1},{17,25},{25,17},{2,10},{10... | collective-permute-start | bytes 1572872 | tf_op jit(solution)/shard_map/ppermute | solution.py:243
  479.8 20.0 %collective-permute-start.65 = (bf16[512,512]{1,0:T(8,128)(2,1)S(1)}, bf16[512,512]{1,0:T(8,128)(2,1)S(1)}, u32[]{:S(2)}, u32[]{:S(2)}) collective-permute-start(bf16[512,512]{1,0:T(8,128)(2,1)S(1)} %copy-done.36), channel_id=1, source_target_pairs={{0,16},{8,24},{16,0},{24,8},{1,17},{9,25},{17,1},{25,9},{2,18},{10... | collective-permute-start | bytes 1572872 | tf_op jit(solution)/shard_map/ppermute | solution.py:243
  491.3 14.7 %collective-permute-start.31 = (bf16[128,1152]{1,0:T(8,128)(2,1)S(1)}, bf16[128,1152]{1,0:T(8,128)(2,1)S(1)}, u32[]{:S(2)}, u32[]{:S(2)}) collective-permute-start(bf16[128,1152]{1,0:T(8,128)(2,1)S(1)} %get-tuple-element.131), channel_id=1, source_target_pairs={{0,6},{2,0},{4,2},{6,4},{1,7},{3,1},{5,3},{7,5},{8,14},{10,8},{12,... | collective-permute-start | bytes 884744 | tf_op jit(solution)/shard_map/ppermute | solution.py:248
  496.2 33.1 %collective-permute-start.30 = (bf16[128,1152]{1,0:T(8,128)(2,1)S(1)}, bf16[128,1152]{1,0:T(8,128)(2,1)S(1)}, u32[]{:S(2)}, u32[]{:S(2)}) collective-permute-start(bf16[128,1152]{1,0:T(8,128)(2,1)S(1)} %get-tuple-element.132), channel_id=1, source_target_pairs={{0,4},{2,6},{4,0},{6,2},{1,5},{3,7},{5,1},{7,3},{8,12},{10,14},{12... | collective-permute-start | bytes 884744 | tf_op jit(solution)/shard_map/ppermute | solution.py:248
  496.3 33.0 %collective-permute-start.29 = (bf16[128,1152]{1,0:T(8,128)(2,1)S(1)}, bf16[128,1152]{1,0:T(8,128)(2,1)S(1)}, u32[]{:S(2)}, u32[]{:S(2)}) collective-permute-start(bf16[128,1152]{1,0:T(8,128)(2,1)S(1)} %get-tuple-element.130), channel_id=1, source_target_pairs={{0,2},{2,4},{4,6},{6,0},{1,3},{3,5},{5,7},{7,1},{8,10},{10,12},{12... | collective-permute-start | bytes 884744 | tf_op jit(solution)/shard_map/ppermute | solution.py:248
  497.3 35.0 %collective-permute-start.60 = (bf16[128,1024]{1,0:T(8,128)(2,1)S(1)}, bf16[128,1024]{1,0:T(8,128)(2,1)S(1)}, u32[]{:S(2)}, u32[]{:S(2)}) collective-permute-start(bf16[128,1024]{1,0:T(8,128)(2,1)S(1)} %get-tuple-element.142), channel_id=1, source_target_pairs={{0,2},{2,4},{4,6},{6,0},{1,3},{3,5},{5,7},{7,1},{8,10},{10,12},{12... | collective-permute-start | bytes 786440 | tf_op jit(solution)/shard_map/ppermute | solution.py:248
  499.8 41.2 %collective-permute-start.61 = (bf16[128,1024]{1,0:T(8,128)(2,1)S(1)}, bf16[128,1024]{1,0:T(8,128)(2,1)S(1)}, u32[]{:S(2)}, u32[]{:S(2)}) collective-permute-start(bf16[128,1024]{1,0:T(8,128)(2,1)S(1)} %get-tuple-element.141), channel_id=1, source_target_pairs={{0,4},{2,6},{4,0},{6,2},{1,5},{3,7},{5,1},{7,3},{8,12},{10,14},{12... | collective-permute-start | bytes 786440 | tf_op jit(solution)/shard_map/ppermute | solution.py:248
  506.1 50.6 %collective-permute-start.62 = (bf16[128,1024]{1,0:T(8,128)(2,1)S(1)}, bf16[128,1024]{1,0:T(8,128)(2,1)S(1)}, u32[]{:S(2)}, u32[]{:S(2)}) collective-permute-start(bf16[128,1024]{1,0:T(8,128)(2,1)S(1)} %get-tuple-element.140), channel_id=1, source_target_pairs={{0,6},{2,0},{4,2},{6,4},{1,7},{3,1},{5,3},{7,5},{8,14},{10,8},{12,... | collective-permute-start | bytes 786440 | tf_op jit(solution)/shard_map/ppermute | solution.py:248
  529.9 11.1 %collective-permute-start.69 = (bf16[1024,128]{1,0:T(8,128)(2,1)S(1)}, bf16[1024,128]{1,0:T(8,128)(2,1)S(1)}, u32[]{:S(2)}, u32[]{:S(2)}) collective-permute-start(bf16[1024,128]{1,0:T(8,128)(2,1)S(1)} %get-tuple-element.137), channel_id=1, source_target_pairs={{0,2},{2,4},{4,6},{6,0},{1,3},{3,5},{5,7},{7,1},{8,10},{10,12},{12... | collective-permute-start | bytes 786440 | tf_op jit(solution)/shard_map/ppermute | solution.py:248
  530.9 25.7 %collective-permute-start.70 = (bf16[1024,128]{1,0:T(8,128)(2,1)S(1)}, bf16[1024,128]{1,0:T(8,128)(2,1)S(1)}, u32[]{:S(2)}, u32[]{:S(2)}) collective-permute-start(bf16[1024,128]{1,0:T(8,128)(2,1)S(1)} %get-tuple-element.136), channel_id=1, source_target_pairs={{0,4},{2,6},{4,0},{6,2},{1,5},{3,7},{5,1},{7,3},{8,12},{10,14},{12... | collective-permute-start | bytes 786440 | tf_op jit(solution)/shard_map/ppermute | solution.py:248
  532.3 24.5 %collective-permute-start.71 = (bf16[1024,128]{1,0:T(8,128)(2,1)S(1)}, bf16[1024,128]{1,0:T(8,128)(2,1)S(1)}, u32[]{:S(2)}, u32[]{:S(2)}) collective-permute-start(bf16[1024,128]{1,0:T(8,128)(2,1)S(1)} %get-tuple-element.135), channel_id=1, source_target_pairs={{0,6},{2,0},{4,2},{6,4},{1,7},{3,1},{5,3},{7,5},{8,14},{10,8},{12,... | collective-permute-start | bytes 786440 | tf_op jit(solution)/shard_map/ppermute | solution.py:248
  (86 other events, 668.9 us)

commit v2 on v1

v2 whole, which is shorter than its diff:
```python
import functools

import jax
import jax.numpy as jnp
from jax import lax
from jax.experimental import pallas as pl
from jax.experimental.pallas import tpu as pltpu
from jax.sharding import PartitionSpec as P

epsilon = 1e-05
negative = -1e30
log2e = 1.4426950408889634
f32 = jnp.float32
low = jnp.bfloat16
vmem_bytes = 48 * 1024 * 1024


def dot(left, right):
    return jnp.dot(left, right, preferred_element_type=f32)


def contract_rows(left, right):
    return lax.dot_general(left, right, (((0,), (0,)), ((), ())), preferred_element_type=f32)


def contract_cols(left, right):
    return lax.dot_general(left, right, (((1,), (1,)), ((), ())), preferred_element_type=f32)


def allowed_mask(start, base, flip, pos_ref):
    offset = lax.broadcasted_iota(jnp.int32, (start, 1), 0)
    key_pos = base + (offset ^ flip)
    return (key_pos <= pos_ref[0:1, :]) & (key_pos >= pos_ref[1:2, :])


def over_blocks(info, body):
    body(0, True)
    lax.fori_loop(1, info[0], lambda s, c: (body(s, False), c)[1], 0)
    lax.fori_loop(info[0], info[1], lambda s, c: (body(s, True), c)[1], 0)


def gather_keys(near_ref, far_ref, head, places):
    rows = near_ref.shape[1]

    def one(s, carry):
        for side, ref in enumerate((near_ref, far_ref)):
            where = pl.multiple_of(s * 2 * rows + side * rows, rows)
            item = ref[s]
            for kind, target in enumerate(places):
                for turned, place in target:
                    part = item[:, kind * head : (kind + 1) * head]
                    if turned:
                        place[:, pl.ds(where, rows)] = part.T
                    else:
                        place[pl.ds(where, rows), :] = part
        return carry

    lax.fori_loop(0, near_ref.shape[0], one, 0)


def attend_kernel(
    scale,
    info,
    q_ref,
    near_ref,
    far_ref,
    pos_ref,
    o_ref,
    lse_ref,
    k_ref,
    vt_ref,
    m_ref,
    l_ref,
    acc_ref,
):
    span = q_ref.shape[0]
    head = k_ref.shape[1]
    pair = q_ref.shape[1] // head
    step = pl.program_id(0)

    @pl.when(step == 0)
    def _():
        gather_keys(near_ref, far_ref, head, [[(False, k_ref)], [(True, vt_ref)]])

    turned = [q_ref[:, h * head : (h + 1) * head].T for h in range(pair)]
    m_ref[...] = jnp.full_like(m_ref, negative)
    l_ref[...] = jnp.zeros_like(l_ref)
    acc_ref[...] = jnp.zeros_like(acc_ref)

    def body(s, masked):
        where = pl.multiple_of(s * span, span)
        key_block = k_ref[pl.ds(where, span), :]
        value_block = vt_ref[:, pl.ds(where, span)]
        if masked:
            allowed = allowed_mask(span, (info[2] - s) * span, info[3], pos_ref)
        for h in range(pair):
            scores = dot(key_block, turned[h]) * scale
            if masked:
                scores = jnp.where(allowed, scores, negative)
            before = m_ref[h]
            after = jnp.maximum(before, jnp.max(scores, axis=0, keepdims=True))
            weights = jnp.exp2(scores - after)
            shrink = jnp.exp2(before - after)
            m_ref[h] = after
            l_ref[h] = l_ref[h] * shrink + jnp.sum(weights, axis=0, keepdims=True)
            acc_ref[h] = acc_ref[h] * shrink + dot(value_block, weights.astype(low))

    over_blocks(info, body)
    for h in range(pair):
        total = l_ref[h]
        lse_ref[pl.ds(step * pair + h, 1), :] = m_ref[h] + jnp.log2(total)
        o_ref[:, h * head : (h + 1) * head] = (acc_ref[h] / total).T.astype(low)


def attend_back_kernel(
    scale,
    unit,
    info,
    q_ref,
    do_ref,
    o_ref,
    lse_ref,
    near_ref,
    far_ref,
    pos_ref,
    dq_ref,
    dkv_ref,
    k_ref,
    kt_ref,
    v_ref,
    dk_ref,
    dv_ref,
    dqt_ref,
):
    span = q_ref.shape[0]
    head = k_ref.shape[1]
    pair = q_ref.shape[1] // head
    step = pl.program_id(0)

    @pl.when(step == 0)
    def _():
        dk_ref[...] = jnp.zeros_like(dk_ref)
        dv_ref[...] = jnp.zeros_like(dv_ref)
        gather_keys(
            near_ref, far_ref, head, [[(False, k_ref), (True, kt_ref)], [(False, v_ref)]]
        )

    dqt_ref[...] = jnp.zeros_like(dqt_ref)
    queries = [q_ref[:, h * head : (h + 1) * head] for h in range(pair)]
    grads = [do_ref[:, h * head : (h + 1) * head] for h in range(pair)]
    queries_t = [item.T for item in queries]
    grads_t = [item.T for item in grads]
    inner = [
        jnp.sum(
            grads_t[h].astype(f32) * o_ref[:, h * head : (h + 1) * head].T.astype(f32),
            axis=0,
            keepdims=True,
        )
        for h in range(pair)
    ]
    totals = [lse_ref[pl.ds(step * pair + h, 1), :] for h in range(pair)]

    def body(s, masked):
        where = pl.multiple_of(s * span, span)
        key_block = k_ref[pl.ds(where, span), :]
        key_turned = kt_ref[:, pl.ds(where, span)]
        value_block = v_ref[pl.ds(where, span), :]
        if masked:
            allowed = allowed_mask(span, (info[2] - s) * span, info[3], pos_ref)
        key_part = jnp.zeros((span, head), f32)
        value_part = jnp.zeros((span, head), f32)
        for h in range(pair):
            scores = dot(key_block, queries_t[h]) * scale - totals[h]
            if masked:
                scores = jnp.where(allowed, scores, negative)
            probs = jnp.exp2(scores)
            grad_probs = dot(value_block, grads_t[h])
            grad_scores = (probs * (grad_probs - inner[h])).astype(low)
            key_part += dot(grad_scores, queries[h])
            value_part += dot(probs.astype(low), grads[h])
            dqt_ref[h] += dot(key_turned, grad_scores)
        dk_ref[pl.ds(where, span), :] += key_part
        dv_ref[pl.ds(where, span), :] += value_part

    over_blocks(info, body)
    for h in range(pair):
        dq_ref[:, h * head : (h + 1) * head] = (dqt_ref[h] * unit).T.astype(low)

    @pl.when(step == pl.num_programs(0) - 1)
    def _():
        dkv_ref[0] = (dk_ref[...] * unit).astype(low)
        dkv_ref[1] = dv_ref[...].astype(low)


def attend(info, query, near, far, pos, heads, head):
    span = query.shape[0]
    window = near.shape[0] * span
    pair = 2
    scale = head**-0.5 * log2e
    work = heads * span * window * head
    piece = pl.BlockSpec(near.shape, lambda i, s: (0, 0, 0))
    spec = pltpu.PrefetchScalarGridSpec(
        num_scalar_prefetch=1,
        grid=(heads // pair,),
        in_specs=[
            pl.BlockSpec((span, pair * head), lambda i, s: (0, i)),
            piece,
            piece,
            pl.BlockSpec(pos.shape, lambda i, s: (0, 0)),
        ],
        out_specs=[
            pl.BlockSpec((span, pair * head), lambda i, s: (0, i)),
            pl.BlockSpec((heads, span), lambda i, s: (0, 0)),
        ],
        scratch_shapes=[
            pltpu.VMEM((window, head), low),
            pltpu.VMEM((head, window), low),
            pltpu.VMEM((pair, 1, span), f32),
            pltpu.VMEM((pair, 1, span), f32),
            pltpu.VMEM((pair, head, span), f32),
        ],
    )
    return pl.pallas_call(
        functools.partial(attend_kernel, scale),
        grid_spec=spec,
        out_shape=(
            jax.ShapeDtypeStruct(query.shape, low),
            jax.ShapeDtypeStruct((heads, span), f32),
        ),
        compiler_params=pltpu.CompilerParams(vmem_limit_bytes=vmem_bytes),
        cost_estimate=pl.CostEstimate(
            flops=8 * work, bytes_accessed=4 * query.size, transcendentals=work // head
        ),
        name="attend",
    )(info, query, near, far, pos)


def attend_back(info, query, grad, attended, lse, near, far, pos, heads, head):
    span = query.shape[0]
    window = near.shape[0] * span
    pair = 2
    scale = head**-0.5 * log2e
    work = heads * span * window * head
    wide = pl.BlockSpec((span, pair * head), lambda i, s: (0, i))
    piece = pl.BlockSpec(near.shape, lambda i, s: (0, 0, 0))
    spec = pltpu.PrefetchScalarGridSpec(
        num_scalar_prefetch=1,
        grid=(heads // pair,),
        in_specs=[
            wide,
            wide,
            wide,
            pl.BlockSpec((heads, span), lambda i, s: (0, 0)),
            piece,
            piece,
            pl.BlockSpec(pos.shape, lambda i, s: (0, 0)),
        ],
        out_specs=[wide, pl.BlockSpec((2, window, head), lambda i, s: (0, 0, 0))],
        scratch_shapes=[
            pltpu.VMEM((window, head), low),
            pltpu.VMEM((head, window), low),
            pltpu.VMEM((window, head), low),
            pltpu.VMEM((window, head), f32),
            pltpu.VMEM((window, head), f32),
            pltpu.VMEM((pair, head, span), f32),
        ],
    )
    return pl.pallas_call(
        functools.partial(attend_back_kernel, scale, head**-0.5),
        grid_spec=spec,
        out_shape=(
            jax.ShapeDtypeStruct(query.shape, low),
            jax.ShapeDtypeStruct((2, window, head), low),
        ),
        compiler_params=pltpu.CompilerParams(vmem_limit_bytes=vmem_bytes),
        cost_estimate=pl.CostEstimate(
            flops=20 * work, bytes_accessed=8 * query.size, transcendentals=work // head
        ),
        name="attend_back",
    )(info, query, grad, attended, lse, near, far, pos)


def gelu_both(value, grad):
    inside = 0.7978845608028654 * (value + 0.044715 * value * value * value)
    bend = jnp.tanh(inside)
    half = 0.5 * (1.0 + bend)
    slope = half + 0.5 * value * (1.0 - bend * bend) * 0.7978845608028654 * (
        1.0 + 3.0 * 0.044715 * value * value
    )
    return (value * half).astype(low), (grad.astype(f32) * slope).astype(low)


def up_kernel(near_ref, far_ref, w_ref, b_ref, g_ref, act_ref, gh_ref, sum_ref, x_ref):
    rows = near_ref.shape[0]

    @pl.when(pl.program_id(0) == 0)
    def _():
        x_ref[:rows] = near_ref[...]
        x_ref[rows:] = far_ref[...]

    tile = min(256, w_ref.shape[1])
    for at in range(0, w_ref.shape[1], tile):
        cut = slice(at, at + tile)
        hidden = dot(x_ref[...], w_ref[:, cut]) + b_ref[:, cut]
        act, grad = gelu_both(hidden, g_ref[:, cut])
        act_ref[:, cut] = act
        gh_ref[:, cut] = grad
        sum_ref[:, cut] = jnp.sum(grad.astype(f32), axis=0, keepdims=True)


def up(near, far, w_up, bias, grad_act):
    rows, width = near.shape
    units = w_up.shape[1]
    tile = min(512, units)
    row = pl.BlockSpec((rows, width), lambda i: (0, 0))
    tall = pl.BlockSpec((2 * rows, tile), lambda i: (0, i))
    thin = pl.BlockSpec((1, tile), lambda i: (0, i))
    shape = jax.ShapeDtypeStruct((2 * rows, units), low)
    return pl.pallas_call(
        up_kernel,
        grid=(units // tile,),
        in_specs=[row, row, pl.BlockSpec((width, tile), lambda i: (0, i)), thin, tall],
        out_specs=[tall, tall, thin],
        out_shape=(shape, shape, jax.ShapeDtypeStruct((1, units), f32)),
        scratch_shapes=[pltpu.VMEM((2 * rows, width), low)],
        compiler_params=pltpu.CompilerParams(vmem_limit_bytes=vmem_bytes),
        cost_estimate=pl.CostEstimate(
            flops=4 * rows * width * units,
            bytes_accessed=2 * width * units + 16 * rows * units,
            transcendentals=2 * rows * units,
        ),
        name="up",
    )(near, far, w_up, bias.reshape(1, -1), grad_act)


def share_kernel(
    at, near_ref, far_ref, gnear_ref, gfar_ref, up_ref, down_ref, b_ref, act_ref, gh_ref, x_ref, g_ref
):
    rows = near_ref.shape[0]

    @pl.when(pl.program_id(0) == 0)
    def _():
        x_ref[:rows] = near_ref[...]
        x_ref[rows:] = far_ref[...]
        g_ref[:rows] = gnear_ref[...]
        g_ref[rows:] = gfar_ref[...]

    tile = min(256, up_ref.shape[1])
    for start in range(0, up_ref.shape[1], tile):
        cut = slice(start, start + tile)
        hidden = dot(x_ref[...], up_ref[:, cut]) + b_ref[:, cut]
        grad_act = contract_cols(g_ref[...], down_ref[cut, :])
        act, grad = gelu_both(hidden, grad_act)
        act_ref[:, cut] = act
        gh_ref[:, cut] = grad


def share(at, near, far, grad_near, grad_far, w_up, w_down, bias, units):
    rows, width = near.shape
    tile = min(512, units)
    tiles = units // tile
    row = pl.BlockSpec((rows, width), lambda i, s: (0, 0))
    tall = pl.BlockSpec((2 * rows, tile), lambda i, s: (0, i))
    shape = jax.ShapeDtypeStruct((2 * rows, units), low)
    spec = pltpu.PrefetchScalarGridSpec(
        num_scalar_prefetch=1,
        grid=(tiles,),
        in_specs=[
            row,
            row,
            row,
            row,
            pl.BlockSpec((width, tile), lambda i, s: (0, s[0] * tiles + i)),
            pl.BlockSpec((tile, width), lambda i, s: (s[0] * tiles + i, 0)),
            pl.BlockSpec((1, tile), lambda i, s: (0, s[0] * tiles + i)),
        ],
        out_specs=[tall, tall],
        scratch_shapes=[pltpu.VMEM((2 * rows, width), low)] * 2,
    )
    return pl.pallas_call(
        share_kernel,
        grid_spec=spec,
        out_shape=(shape, shape),
        compiler_params=pltpu.CompilerParams(vmem_limit_bytes=vmem_bytes),
        cost_estimate=pl.CostEstimate(
            flops=8 * rows * width * units,
            bytes_accessed=4 * width * units + 8 * rows * (units + width),
            transcendentals=2 * rows * units,
        ),
        name="share",
    )(at, near, far, grad_near, grad_far, w_up, w_down, bias.reshape(1, -1))


turns = ((3, 0), (1, 0), (3, 1), (2, 1), (1, 1), (2, 0), (0, 0), (0, 1))


def joined(items, place):
    if len(items) == 1:
        return items[0][...]
    start = 0
    for item in items:
        place[start : start + item.shape[0]] = item[...]
        start += item.shape[0]
    return place[...]


def store_turn(turn, result, outs):
    for index, out in enumerate(outs):

        @pl.when(turn // 2 == index)
        def _(out=out):
            out[0] = result.astype(out.dtype)


def hidden_kernel(lefts, at, *refs):
    left_refs, right_refs = refs[:lefts], refs[lefts:-6]
    outs, (left_place, right_place) = refs[-6:-2], refs[-2:]
    left = joined(left_refs, left_place)
    right = joined(right_refs, right_place)
    store_turn(pl.program_id(0), contract_rows(left, right), outs)


def hidden_weights(at, lefts, pieces, units, part, name):
    total = len(turns)
    span = lefts[0].shape[0]
    rows = span // 2
    half = units // 2
    depth = len(lefts) * span

    def left_of(own):
        def place(i, s):
            return (0, s[2 * total] * 2 + s[total + i] if own else s[total + i])

        return pl.BlockSpec((span, half), place)

    def out_of(index):
        return pl.BlockSpec((1, half, part), lambda i, s: (jnp.clip(i - 2 * index, 0, 1), 0, 0))

    spec = pltpu.PrefetchScalarGridSpec(
        num_scalar_prefetch=1,
        grid=(total,),
        in_specs=[left_of(n == 0) for n in range(len(lefts))]
        + [pl.BlockSpec((rows, part), lambda i, s: (0, s[i])) for _ in pieces],
        out_specs=[out_of(index) for index in range(4)],
        scratch_shapes=[pltpu.VMEM((depth, half), low), pltpu.VMEM((depth, part), low)],
    )
    return pl.pallas_call(
        functools.partial(hidden_kernel, len(lefts)),
        grid_spec=spec,
        out_shape=tuple(jax.ShapeDtypeStruct((2, half, part), low) for _ in range(4)),
        compiler_params=pltpu.CompilerParams(vmem_limit_bytes=60 * 1024 * 1024),
        cost_estimate=pl.CostEstimate(
            flops=2 * total * depth * half * part,
            bytes_accessed=4 * depth * (units + 4 * part),
            transcendentals=0,
        ),
        name=name,
    )(at, *lefts, *pieces)


def place_kernel(count, at, *refs):
    parts, (down_ref, up_ref) = refs[: 2 * count], refs[2 * count :]
    for step in range(count):

        @pl.when(pl.program_id(0) == step)
        def _(step=step):
            down_ref[...] = parts[step][0].astype(f32)
            up_ref[...] = parts[count + step][0].astype(f32).T


def place(at, downs, ups):
    count = len(downs)
    _, units, part = downs[0].shape
    piece = pl.BlockSpec((1, units, part), lambda i, s: (0, 0, 0))
    spec = pltpu.PrefetchScalarGridSpec(
        num_scalar_prefetch=1,
        grid=(count,),
        in_specs=[piece] * (2 * count),
        out_specs=[
            pl.BlockSpec((units, part), lambda i, s: (lax.rem(s[0] - i + count, count), 0)),
            pl.BlockSpec((part, units), lambda i, s: (0, lax.rem(s[0] - i + count, count))),
        ],
    )
    return pl.pallas_call(
        functools.partial(place_kernel, count),
        grid_spec=spec,
        out_shape=(
            jax.ShapeDtypeStruct((count * units, part), f32),
            jax.ShapeDtypeStruct((part, count * units), f32),
        ),
        compiler_params=pltpu.CompilerParams(vmem_limit_bytes=vmem_bytes),
        cost_estimate=pl.CostEstimate(
            flops=0, bytes_accessed=12 * count * units * part, transcendentals=0
        ),
        name="place",
    )(at, *downs, *ups)


def branch_kernel(at, near_ref, far_ref, y_ref, *refs):
    outs, place = refs[:4], refs[4]
    result = contract_rows(joined((near_ref, far_ref), place), y_ref[...])
    store_turn(pl.program_id(0), result, outs)


def branch_weights(at, near, far, right, part, name):
    total = len(turns)
    rows = near.shape[0]
    half = part // 2
    wide = right.shape[1]
    piece = pl.BlockSpec((rows, half), lambda i, s: (0, s[i] * 2 + s[total + i]))

    def all_of(item):
        return pl.BlockSpec(item.shape, lambda i, s: (0, 0))

    def out_of(index):
        return pl.BlockSpec((1, half, wide), lambda i, s: (jnp.clip(i - 2 * index, 0, 1), 0, 0))

    spec = pltpu.PrefetchScalarGridSpec(
        num_scalar_prefetch=1,
        grid=(total,),
        in_specs=[piece, piece, all_of(right)],
        out_specs=[out_of(index) for index in range(4)],
        scratch_shapes=[pltpu.VMEM((2 * rows, half), low)],
    )
    return pl.pallas_call(
        branch_kernel,
        grid_spec=spec,
        out_shape=tuple(jax.ShapeDtypeStruct((2, half, wide), low) for _ in range(4)),
        compiler_params=pltpu.CompilerParams(vmem_limit_bytes=vmem_bytes),
        cost_estimate=pl.CostEstimate(
            flops=4 * total * rows * half * wide,
            bytes_accessed=2 * total * half * wide,
            transcendentals=0,
        ),
        name=name,
    )(at, near, far, right)


def swap(item):
    return lax.ppermute(item, "tensor", [(0, 1), (1, 0)])


def cross(item, bits):
    size = lax.axis_size("dp")
    return lax.ppermute(item, "dp", [(i, i ^ bits) for i in range(size)])


def shift(item, by):
    size = lax.axis_size("seq")
    return lax.ppermute(item, "seq", [(i, (i + by) % size) for i in range(size)])


def shift_up(item, by):
    size = lax.axis_size("seq")
    return lax.ppermute(item, "seq", [(i, i + by) for i in range(size - by)])


def shift_down(item, by):
    size = lax.axis_size("seq")
    return lax.ppermute(item, "seq", [(i + by, i) for i in range(size - by)])


def pair_gather(item):
    return jnp.concatenate([item, swap(item)], axis=0)


def after(item, *others):
    return lax.optimization_barrier((item, *others))


def pair_sum(both):
    half = both.shape[0] // 2
    return both[:half].astype(f32) + swap(both[half:]).astype(f32)


def dp_first(parts, size):
    send_x, send_y, kept, own = (item.reshape(2, size, *item.shape[1:]) for item in parts)
    got_x = cross(send_x, 1)
    got_y = cross(send_y, 2)
    second_a = (kept[1].astype(f32) + got_x[0].astype(f32)).astype(low)
    second_b = (kept[0].astype(f32) + got_y[0].astype(f32)).astype(low)
    return second_a, second_b, own, got_x, got_y


def dp_last(second_a, second_b, own, got_x, got_y):
    last_a = cross(second_a, 2)
    last_b = cross(second_b, 1)
    return jnp.concatenate(
        [
            own[0].astype(f32) + got_x[1].astype(f32) + last_a.astype(f32),
            own[1].astype(f32) + got_y[1].astype(f32) + last_b.astype(f32),
        ],
        axis=1,
    )


def norm_parts(rows):
    centre = rows - jnp.mean(rows, axis=-1, keepdims=True)
    inverse = lax.rsqrt(jnp.mean(centre * centre, axis=-1, keepdims=True) + epsilon)
    return centre * inverse, inverse


def norm_back(grad, unit, inverse, gain):
    scaled = grad * gain
    part = (
        scaled
        - jnp.mean(scaled, axis=-1, keepdims=True)
        - unit * jnp.mean(scaled * unit, axis=-1, keepdims=True)
    )
    return part * inverse, jnp.sum(grad * unit, axis=0), jnp.sum(grad, axis=0)


def on_device(
    tokens,
    lengths,
    ln1_gain,
    ln1_bias,
    w_query,
    b_query,
    w_key,
    w_value,
    b_value,
    w_out,
    b_out,
    ln2_gain,
    ln2_bias,
    w_up,
    b_up,
    w_down,
    b_down,
    cotangent,
):
    shard = tokens[0].astype(f32)
    rows_own, width = shard.shape
    seqs = lax.axis_size("seq")
    dps = lax.axis_size("dp")
    span = 2 * rows_own
    heads, head = b_query.shape
    at_dp, at_seq, at_core = (lax.axis_index(name) for name in ("dp", "seq", "tensor"))
    flip = at_core * rows_own
    span_start = at_seq * span
    hidden_local = w_up.shape[1]
    hidden_part = hidden_local // seqs
    dp_part = width // dps
    out_part = dp_part // seqs

    ends = jnp.cumsum(lengths[0], dtype=jnp.int32)
    row_pos = span_start + (jnp.arange(span, dtype=jnp.int32) ^ flip)
    row_start = jnp.max(
        jnp.where(row_pos[:, None] >= ends[None, :], ends[None, :], 0), axis=1
    ).astype(jnp.int32)
    pos = jnp.zeros((8, span), jnp.int32).at[0].set(row_pos).at[1].set(row_start)
    first, last = jnp.min(row_start), jnp.max(row_start)
    whole_to = jnp.clip(at_seq + 1 - (last + span - 1) // span, 1, at_seq + 1)
    some_to = jnp.clip(at_seq + 1 - first // span, whole_to, at_seq + 1)
    info = jnp.stack([whole_to, some_to, at_seq, flip]).astype(jnp.int32)

    unit_one, inverse_one = norm_parts(shard)
    normed = (unit_one * ln1_gain + ln1_bias).astype(low)
    w_both = jnp.concatenate([w_key, w_value], axis=1)
    b_both = jnp.concatenate([jnp.zeros_like(b_value), b_value])
    both_own = (dot(normed, w_both) + b_both).astype(low)
    pieces = [shift_up(both_own, by) for by in range(1, seqs)]
    grad_own = cotangent[0]
    grad_own, both_own = after(grad_own, both_own)
    grad_held = [grad_own]
    for step in range(1, seqs):
        grad_held.append(shift(grad_held[-1], 1))
    grad_far = [swap(grad_own)]
    grad_act = contract_cols(jnp.concatenate([grad_own, grad_far[0]], axis=0), w_down).astype(low)
    grad_act, *pieces = after(grad_act, *pieces)
    near = jnp.stack([both_own] + pieces)
    far = swap(near)
    normed_far = swap(normed)
    normed_all = jnp.concatenate([normed, normed_far], axis=0)
    query = (dot(normed_all, w_query) + b_query.reshape(-1)).astype(low)

    if seqs > 1:
        query, grad_held[1] = after(query, grad_held[1])
    attended, lse = attend(info, query, near, far, pos, heads, head)
    if seqs > 2:
        attended, grad_held[2] = after(attended, grad_held[2])
    middle = shard + (pair_sum(dot(attended, w_out).astype(low)) + b_out)
    unit_two, inverse_two = norm_parts(middle)
    normed_two = (unit_two * ln2_gain + ln2_bias).astype(low)

    held = [normed_two]
    for step in range(1, seqs):
        held.append(shift(held[-1], 1))
    held_far = [swap(normed_two)]
    activated, grad_hidden, grad_b_up = up(held[0], held_far[0], w_up, b_up, grad_act)
    if seqs > 3:
        grad_hidden, grad_held[3] = after(grad_hidden, grad_held[3])
    grad_normed_two = contract_cols(grad_hidden, w_up).astype(low)
    if seqs > 1:
        grad_normed_two, held[1] = after(grad_normed_two, held[1])
    grad_normed_two = pair_sum(grad_normed_two)

    back, grad_ln2_gain, grad_ln2_bias = norm_back(
        grad_normed_two, unit_two, inverse_two, ln2_gain
    )
    grad_out = grad_own.astype(f32)
    grad_b_down = jnp.sum(grad_out, axis=0)
    grad_middle = grad_out + back
    grad_branch = grad_middle.astype(low)
    grad_b_out = jnp.sum(grad_branch.astype(f32), axis=0)
    grad_branch_far = swap(grad_branch)
    grad_branch_all = jnp.concatenate([grad_branch, grad_branch_far], axis=0)
    grad_attended = contract_cols(grad_branch_all, w_out).astype(low)
    blocks = [at_dp ^ r for r, _ in turns]
    halves = [jnp.int32(half) for _, half in turns]
    table = jnp.stack(blocks + halves + [at_seq, at_core]).astype(jnp.int32)

    parts_out = branch_weights(
        table, grad_branch, grad_branch_far, attended, dp_part, "weight_out"
    )

    share_at = at_seq.reshape(1).astype(jnp.int32)
    acts, grads = [activated], [grad_hidden]

    def shared_part(step):
        held_far.append(swap(held[step]))
        grad_far.append(swap(grad_held[step]))
        act, grad = share(
            share_at,
            held[step],
            held_far[step],
            grad_held[step],
            grad_far[step],
            w_up,
            w_down,
            b_up,
            hidden_part,
        )
        acts.append(act)
        grads.append(grad)

    if seqs > 2:
        shared_part(1)
        grad_attended, acts[1], held[2], *parts_out = after(
            grad_attended, acts[1], held[2], *parts_out
        )
    first_out = dp_first(parts_out, 1)

    grad_query, grad_both = attend_back(
        info, query, grad_attended, attended, lse, near, far, pos, heads, head
    )
    if seqs > 1:
        grad_both, held[-1], *seconds = after(grad_both, held[-1], *first_out[:2])
        first_out = (*seconds, *first_out[2:])
    grad_both = grad_both.reshape(2, seqs, 2, rows_own, head)
    kept = lax.dynamic_index_in_dim(grad_both, at_core, 0, False)
    given = lax.dynamic_index_in_dim(grad_both, 1 - at_core, 0, False)
    grad_kv = (kept.astype(f32) + swap(given)[:, ::-1].astype(f32)).astype(low)
    grad_kv = grad_kv.reshape(seqs, span, head)
    total = grad_kv[0].astype(f32)
    for by in range(1, seqs):
        total = total + shift_down(grad_kv[by], by).astype(f32)
    grad_kv = total.astype(low)
    grad_qkv = jnp.concatenate([grad_query, grad_kv], axis=1)
    w_qkv = jnp.concatenate([w_query, jnp.where(at_core == 0, w_key, w_value)], axis=1)
    grad_normed = pair_sum(contract_cols(grad_qkv, w_qkv).astype(low))
    back, grad_ln1_gain, grad_ln1_bias = norm_back(
        grad_normed, unit_one, inverse_one, ln1_gain
    )
    grad_input = (grad_middle + back).astype(low)[None]

    parts = branch_weights(table, normed, normed_far, grad_qkv, dp_part, "weight_query")
    grad_b_value = jnp.where(at_core == 1, jnp.sum(grad_kv.astype(f32), axis=0), 0.0)
    grad_b_query = jnp.sum(grad_query.astype(f32), axis=0)
    features = [
        grad_ln1_gain,
        grad_ln1_bias,
        grad_b_out,
        grad_ln2_gain,
        grad_ln2_bias,
        grad_b_down,
    ]
    count = len(features)
    features = jnp.concatenate([item.reshape(-1, head) for item in features], axis=0)
    rows = features.shape[0]
    features = features + swap(features)
    values = grad_b_value.reshape(1, head)
    values = values + swap(values)
    packed = jnp.concatenate(
        [
            features,
            grad_b_up.reshape(-1, head),
            grad_b_query.reshape(-1, head),
            jnp.broadcast_to(values, (8, head)),
        ],
        axis=0,
    )
    share_at, packed, *parts = after(share_at, packed, *parts)
    first_query = dp_first(parts, 1)
    total = packed + cross(packed, 1) + cross(packed, 2) + cross(packed, 3)

    for step in range(len(acts), seqs):
        shared_part(step)
    acts[-1], total, *seconds = after(acts[-1], total, *first_query[:2])
    first_query = (*seconds, *first_query[2:])
    downs = hidden_weights(
        table,
        acts,
        [item for couple in zip(grad_held, grad_far) for item in couple],
        hidden_part,
        dp_part,
        "weight_down",
    )
    sum_branch = jnp.concatenate([dp_last(*first_out)[0], dp_last(*first_query)[0]], axis=1)
    grads[0], sum_branch, *downs = after(grads[0], sum_branch, *downs)
    first_down = dp_first(downs, 1)
    packed = total
    for by in range(1, seqs):
        total = total + shift(packed, by)
    ups = hidden_weights(
        table,
        grads,
        [item for couple in zip(held, held_far) for item in couple],
        hidden_part,
        dp_part,
        "weight_up",
    )
    activated, *ups = after(activated, *ups)
    first_up = dp_first(ups, 1)
    activated, *seconds = after(activated, *first_down[:2])
    first_down = (*seconds, *first_down[2:])
    result = dot(activated, w_down).astype(low)
    sum_down = dp_last(*first_down).astype(low)
    result, sum_down, *seconds = after(result, sum_down, *first_up[:2])
    first_up = (*seconds, *first_up[2:])
    output = (middle + (pair_sum(result) + b_down)).astype(low)[None]
    sum_up = dp_last(*first_up).astype(low)

    def to_seq(item, by, axis):
        at = lax.rem(at_seq + by, seqs)
        return lax.dynamic_slice_in_dim(item, at * out_part, out_part, axis)

    downs, ups = [], []
    for items, whole in ((downs, sum_down), (ups, sum_up)):
        items.append(to_seq(whole, 0, 2))
        for by in range(1, seqs):
            items.append(shift(to_seq(whole, by, 2), by))
    out_w_down, out_w_up = place(share_at, downs, ups)

    narrow = sum_branch.astype(low)
    branch = to_seq(sum_branch, 0, 0)
    for by in range(1, seqs):
        branch = branch + shift(to_seq(narrow, by, 0), by).astype(f32)
    out_w_out = branch[:, : heads * head].T
    out_qkv = branch[:, heads * head :]
    out_w_query = out_qkv[:, : heads * head]
    half = out_part // 2
    last_kv = out_qkv[:, heads * head :]
    mine = lax.dynamic_slice_in_dim(last_kv, at_core * half, half, 0)
    other = swap(lax.dynamic_slice_in_dim(last_kv, (1 - at_core) * half, half, 0))
    out_w_key = jnp.where(at_core == 0, mine, other)
    out_w_value = jnp.where(at_core == 0, other, mine)

    place_own = at_dp * seqs + at_seq

    def own_part(item, size, index):
        return lax.dynamic_slice_in_dim(item, index * size, size, item.ndim - 1)

    vectors = own_part(
        total[:rows].reshape(count, width), out_part // 2, place_own * 2 + at_core
    )
    thin = head // (dps * seqs)
    up_rows = b_up.shape[0]
    sum_b_up = own_part(total[rows : rows + up_rows], thin, place_own)
    sum_b_query = own_part(total[rows + up_rows : rows + up_rows + heads], thin, place_own)
    sum_b_value = own_part(total[rows + up_rows + heads], thin // 2, place_own * 2 + at_core)
    return (
        output,
        grad_input,
        vectors[0],
        vectors[1],
        out_w_query,
        sum_b_query,
        out_w_key,
        out_w_value,
        sum_b_value,
        out_w_out,
        vectors[2],
        vectors[3],
        vectors[4],
        out_w_up,
        sum_b_up,
        out_w_down,
        vectors[5],
    )


def solution(mesh):
    in_specs = (
        P("dp", ("seq", "tensor"), None),
        P("dp", None),
        P(),
        P(),
        P(None, "tensor"),
        P("tensor", None),
        P(),
        P(),
        P(),
        P("tensor", None),
        P(),
        P(),
        P(),
        P(None, "tensor"),
        P("tensor", None),
        P("tensor", None),
        P(),
        P("dp", ("seq", "tensor"), None),
    )
    out_specs = (
        P("dp", ("seq", "tensor"), None),
        P("dp", ("seq", "tensor"), None),
        P(("dp", "seq", "tensor")),
        P(("dp", "seq", "tensor")),
        P(("dp", "seq"), "tensor"),
        P("tensor", ("dp", "seq")),
        P(("dp", "seq", "tensor"), None),
        P(("dp", "seq", "tensor"), None),
        P(("dp", "seq", "tensor")),
        P("tensor", ("dp", "seq")),
        P(("dp", "seq", "tensor")),
        P(("dp", "seq", "tensor")),
        P(("dp", "seq", "tensor")),
        P(("dp", "seq"), "tensor"),
        P("tensor", ("dp", "seq")),
        P("tensor", ("dp", "seq")),
        P(("dp", "seq", "tensor")),
    )
    return jax.shard_map(
        on_device, mesh=mesh, in_specs=in_specs, out_specs=out_specs, check_vma=False
    )
```

time: 570 us -> 471 us (0.83)
  matrix products: 195 us -> 55.8 us
  Pallas kernels: 16.4 us -> 117 us
  local copies, waits for them, and re-layouts: 68.6 us -> 13.1 us
  starting transfers between devices: 90.1 us -> 74.5 us
  waiting for transfers between devices: 144 us -> 158 us
    pallas_call x0 -> x9, Pallas kernels: none -> 100 us  [the longest x2 36 us: hidden_weights(): pl.pallas_call(functools.partial(hidden_kernel, len(lefts)), grid_spec=sp...]
    dot_general x16 -> x0, matrix products: 50.3 us -> none  [contract_rows(): lax.dot_general(left, right, (((0,), (0,)), ((), ())), preferred_element_...]
    dot_general x11 -> x4, matrix products: 69.1 us -> 20.3 us  [dot(): return jnp.dot(left, right, preferred_element_type=f32)]
    dot_general x9 -> x4, matrix products: 75.9 us -> 35.5 us  [contract_cols(): lax.dot_general(left, right, (((1,), (1,)), ((), ())), preferred_element_...]
    ppermute x21 -> x18, waiting for transfers between devices: 65.7 us -> 105 us  [shift(): lax.ppermute(item, 'seq', [(i, (i + by) % size) for i in range(size)])]
    unnamed x171 -> x133, local copies, waits for them, and re-layouts: 33.8 us -> 8.32 us
    slice x17 -> x8, local copies, waits for them, and re-layouts: 16.5 us -> 1.35 us  [the longest x4 1.34 us: pair_sum(): return both[:half].astype(f32) + swap(both[half:]).astype(f32)]
    ppermute x27 -> x19, waiting for transfers between devices: 54.6 us -> 39.7 us  [cross(): return lax.ppermute(item, 'dp', [(i, i ^ bits) for i in range(size)])]
  transfers between devices with their start and end apart: 72 -> 62, of which waited for: 22 -> 24; matrix products, arithmetic and copies ran while one was open for 53% -> 18% of each run, Pallas kernels for 3% -> 25%
where the time goes in v2:
time: 471 us; the launch traced here: 465 us
  waiting for transfers between devices  158 us (34%)
  Pallas kernels  117 us (25%)
  starting transfers between devices  74.5 us (16%)
  matrix products  55.8 us (12%)
  other arithmetic  40.5 us (9%)
  local copies, waits for them, and re-layouts  13.1 us (3%)
  between operations  5.43 us (1%)
    ppermute x18, waiting for transfers between devices, shift(): lax.ppermute(item, 'seq', [(i, (i + by) % size) for i in range(size)])  105 us
    ppermute x19, waiting for transfers between devices, cross(): return lax.ppermute(item, 'dp', [(i, i ^ bits) for i in range(size)])  39.7 us
    pallas_call x2, Pallas kernels, hidden_weights(): pl.pallas_call(functools.partial(hidden_kernel, len(lefts)), grid_spec=sp...  36 us
    dot_general x4, matrix products, contract_cols(): lax.dot_general(left, right, (((1,), (1,)), ((), ())), preferred_element_...  35.5 us
    ppermute x18, starting transfers between devices, shift(): lax.ppermute(item, 'seq', [(i, (i + by) % size) for i in range(size)])  29.8 us
    pallas_call x3, Pallas kernels, share(): pl.pallas_call(share_kernel, grid_spec=spec, out_shape=(shape, shape), co...  26.6 us
    ppermute x19, starting transfers between devices, cross(): return lax.ppermute(item, 'dp', [(i, i ^ bits) for i in range(size)])  24 us
    dot_general x4, matrix products, dot(): return jnp.dot(left, right, preferred_element_type=f32)  20.3 us
  transfers between devices with their start and end apart: 62, of which 24 were waited for; matrix products, arithmetic and copies ran while one was open for 18% of the time, Pallas kernels for 25%

profile of v2, /device:TPU:0, one launch (start us, length us, event | category | flops | bytes accessed | tf_op | source)
XLA Modules:
  0.0 464.5 jit_solution(9498097177352340240)
XLA Ops:
  0.7 1.6 convert_reduce_fusion.1
  2.3 1.6 fusion.23
  5.5 6.5 %collective-permute-start.5 = (bf16[256,256]{1,0:T(8,128)(2,1)S(1)}, bf16[256,256]{1,0:T(8,128)(2,1)S(1)}, u32[]{:S(2)}, u32[]{:S(2)}) collective-permute-start(bf16[256,256]{1,0:T(8,128)(2,1)S(1)} %fusion.50), channel_id=1, source_target_pairs={{0,6},{1,7},{8,14},{9,15},{16,22},{17,23},{24,30},{25,31}} | collective-permute-start | bytes 393224 | tf_op jit(solution)/shard_map/ppermute | solution.py:555
  12.1 2.0 collective-permute-start.4
  14.0 3.1 collective-permute-start.3
  22.2 14.4 %convolution_convert_fusion.g_ref = bf16[512,4096]{1,0:T(8,128)(2,1)} fusion(bf16[4096,2048]{1,0:T(8,128)(2,1)} %down_ref.5, bf16[256,2048]{1,0:T(8,128)(2,1)} %collective-permute-done.2.refs_5_, bf16[256,2048]{1,0:T(8,128)(2,1)} %bitcast.8.refs_4_), kind=kOutput, calls=%fused_computation | convolution fusion | flops 8596226048 | bytes 23068672 | tf_op jit(solution)/shard_map/dot_general | solution.py:27
  38.2 5.9 %collective-permute-done.1.gnear_ref.refs_6_ = bf16[256,2048]{1,0:T(8,128)(2,1)S(1)} collective-permute-done((bf16[256,2048]{1,0:T(8,128)(2,1)}, bf16[256,2048]{1,0:T(8,128)(2,1)S(1)}, u32[]{:S(2)}, u32[]{:S(2)}) %collective-permute-start.1) | collective-permute-done | bytes 1048608 | tf_op jit(solution)/shard_map/ppermute | solution.py:550
  44.1 4.0 collective-permute-start.7
  48.1 4.9 %add_convert_fusion.2.q_ref = bf16[512,1024]{1,0:T(8,128)(2,1)S(1)} fusion(bf16[2048,1024]{1,0:T(8,128)(2,1)} %param.26, bf16[256,2048]{1,0:T(8,128)(2,1)S(1)} %collective-permute-done.far_ref, bf16[256,2048]{1,0:T(8,128)(2,1)S(1)} %fusion.16.near_ref, f32[1024]{0:T(1024)S(1)} %bitcast.235), kind=kOutput, calls=%fused_computation.53 | convolution fusion | flops 2152726528 | bytes 7344128 | tf_op jit(solution)/shard_map/dot_general | solution.py:19
  53.1 7.0 %attend.1 = (bf16[512,1024]{1,0:T(8,128)(2,1)S(1)}, f32[8,512]{1,0:T(8,128)S(1)}) custom-call(s32[4]{0:T(128)S(1)} %pad_add_fusion.info, bf16[512,1024]{1,0:T(8,128)(2,1)S(1)} %add_convert_fusion.2.q_ref, bf16[4,256,256]{2,1,0:T(8,128)(2,1)S(1)} %pad_maximum_fusion.3.near_ref, bf16[4,256,256]{2,1,0:T(8,128)(2,1)S(1)} %collective-permute-done.6.far_ref, ...), custom_call_target="tpu_custom_call" | custom-call | flops 8589934592 | bytes 2097152 | tf_op jit(solution)/shard_map/attend/pallas_call | solution.py:223
  60.2 11.2 %collective-permute-done.7.gnear_ref.refs_8_ = bf16[256,2048]{1,0:T(8,128)(2,1)S(1)} collective-permute-done((bf16[256,2048]{1,0:T(8,128)(2,1)S(1)}, bf16[256,2048]{1,0:T(8,128)(2,1)S(1)}, u32[]{:S(2)}, u32[]{:S(2)}) %collective-permute-start.7) | collective-permute-done | bytes 1048608 | tf_op jit(solution)/shard_map/ppermute | solution.py:550
  71.4 2.3 convolution_convert_fusion.1
  73.9 2.6 collective-permute-done.8
  78.7 1.9 collective-permute-start.10
  80.6 2.6 collective-permute-start.11
  83.2 19.6 %up.1 = (bf16[512,4096]{1,0:T(8,128)(2,1)}, bf16[512,4096]{1,0:T(8,128)(2,1)}, f32[1,4096]{1,0:T(1,128)S(1)}) custom-call(bf16[256,2048]{1,0:T(8,128)(2,1)S(1)} %add_convert_fusion.1.near_ref.refs_4_, bf16[256,2048]{1,0:T(8,128)(2,1)S(1)} %collective-permute-done.9.far_ref.refs_5_, bf16[2048,4096]{1,0:T(8,128)(2,1)} %up_ref.5, f32[1,4096]{1,0:T(1,128)S(1)} %bitcast.215, ...), custom_call_target="tpu_custom_call" | custom-call | flops 8589934592 | bytes 33554432 | tf_op jit(solution)/shard_map/up/pallas_call | solution.py:319
  102.8 4.4 collective-permute-done.10.gnear_ref.refs_10_
  108.1 13.6 %convolution_convert_fusion.3 = bf16[512,2048]{1,0:T(8,128)(2,1)S(1)} fusion(bf16[512,4096]{1,0:T(8,128)(2,1)} %get-tuple-element.181.refs_0_, bf16[2048,4096]{1,0:T(8,128)(2,1)} %up_ref.5), kind=kOutput, calls=%fused_computation.9 | convolution fusion | flops 8590983168 | bytes 23068672 | tf_op jit(solution)/shard_map/dot_general | solution.py:27
  121.8 7.5 %collective-permute-done.11.near_ref.refs_6_ = bf16[256,2048]{1,0:T(8,128)(2,1)S(1)} collective-permute-done((bf16[256,2048]{1,0:T(8,128)(2,1)S(1)}, bf16[256,2048]{1,0:T(8,128)(2,1)S(1)}, u32[]{:S(2)}, u32[]{:S(2)}) %collective-permute-start.11) | collective-permute-done | bytes 1048608 | tf_op jit(solution)/shard_map/ppermute | solution.py:550
  130.1 2.8 collective-permute-done.12
  134.0 4.3 convert_reduce_fusion.3
  138.6 18.9 %collective-permute-done.16.near_ref.refs_8_ = bf16[256,2048]{1,0:T(8,128)(2,1)} collective-permute-done((bf16[256,2048]{1,0:T(8,128)(2,1)S(1)}, bf16[256,2048]{1,0:T(8,128)(2,1)}, u32[]{:S(2)}, u32[]{:S(2)}) %collective-permute-start.16) | collective-permute-done | bytes 1048608 | tf_op jit(solution)/shard_map/ppermute | solution.py:550
  157.9 9.0 %share.3 = (bf16[512,1024]{1,0:T(8,128)(2,1)S(1)}, bf16[512,1024]{1,0:T(8,128)(2,1)S(1)}) custom-call(s32[1]{0:T(128)} %bitcast.5.at, bf16[256,2048]{1,0:T(8,128)(2,1)S(1)} %collective-permute-done.11.near_ref.refs_6_, bf16[256,2048]{1,0:T(8,128)(2,1)S(1)} %collective-permute-done.14.far_ref.refs_7_, ...), custom_call_target="tpu_custom_call" | custom-call | flops 4294967296 | bytes 14680064 | tf_op jit(solution)/shard_map/share/pallas_call | solution.py:380
  168.0 4.3 fusion.43.do_ref
  172.3 7.7 %weight_out.1 = (bf16[2,256,1024]{2,1,0:T(8,128)(2,1)S(1)}, bf16[2,256,1024]{2,1,0:T(8,128)(2,1)S(1)}, bf16[2,256,1024]{2,1,0:T(8,128)(2,1)S(1)}, bf16[2,256,1024]{2,1,0:T(8,128)(2,1)S(1)}) custom-call(s32[18]{0:T(128)S(1)} %stack.68.at, bf16[256,2048]{1,0:T(8,128)(2,1)} %get-tuple-element.271.near_ref, bf16[256,2048]{1,0:T(8,128)(2,1)} %collective-permute-done.13.far_ref, ...), custom_call_target="tpu_custom_call" | custom-call | flops 2147483648 | bytes 4194304 | tf_op jit(solution)/shard_map/weight_out/pallas_call | solution.py:525
  183.1 10.0 %attend_back.1 = (bf16[512,1024]{1,0:T(8,128)(2,1)S(1)}, bf16[2,2048,128]{2,1,0:T(8,128)(2,1)S(1)}) custom-call(s32[4]{0:T(128)S(1)} %pad_add_fusion.info, bf16[512,1024]{1,0:T(8,128)(2,1)S(1)} %copy-done.30, bf16[512,1024]{1,0:T(8,128)(2,1)S(1)} %fusion.43.do_ref, bf16[512,1024]{1,0:T(8,128)(2,1)} %copy-done.28, f32[8,512]{1,0:T(8,128)S(1)} %get-tuple-element.148.lse_ref, ...), custom_call_target="tpu_custom_call" | custom-call | flops 21474836480 | bytes 4194304 | tf_op jit(solution)/shard_map/attend_back/pallas_call | solution.py:268
  193.1 11.7 %collective-permute-done.17 = bf16[2,1,256,1024]{3,2,1,0:T(8,128)(2,1)S(1)} collective-permute-done((bf16[2,1,256,1024]{3,2,1,0:T(8,128)(2,1)S(1)}, bf16[2,1,256,1024]{3,2,1,0:T(8,128)(2,1)S(1)}, u32[]{:S(2)}, u32[]{:S(2)}) %collective-permute-start.17) | collective-permute-done | bytes 1048608 | tf_op jit(solution)/shard_map/ppermute | solution.py:545
  212.2 10.4 %collective-permute-done.20 = bf16[1,256,1024]{2,1,0:T(8,128)(2,1)S(1)} collective-permute-done((bf16[1,256,1024]{2,1,0:T(8,128)(2,1)S(1)}, bf16[1,256,1024]{2,1,0:T(8,128)(2,1)S(1)}, u32[]{:S(2)}, u32[]{:S(2)}) %collective-permute-start.20) | collective-permute-done | bytes 524320 | tf_op jit(solution)/shard_map/ppermute | solution.py:545
  224.0 1.7 collective-permute-start.23
  226.4 4.5 collective-permute-done.24
  230.9 2.3 collective-permute-done.23
  233.3 3.2 fusion.4
  236.6 1.6 maximum_bitcast_fusion.1
  239.9 8.0 %weight_query.1 = (bf16[2,256,1152]{2,1,0:T(8,128)(2,1)S(1)}, bf16[2,256,1152]{2,1,0:T(8,128)(2,1)S(1)}, bf16[2,256,1152]{2,1,0:T(8,128)(2,1)S(1)}, bf16[2,256,1152]{2,1,0:T(8,128)(2,1)}) custom-call(s32[18]{0:T(128)S(1)} %stack.68.at, bf16[256,2048]{1,0:T(8,128)(2,1)S(1)} %copy-done.11, bf16[256,2048]{1,0:T(8,128)(2,1)S(1)} %copy-done.19, ...), custom_call_target="tpu_custom_call" | custom-call | flops 2415919104 | bytes 4718592 | tf_op jit(solution)/shard_map/weight_query/pallas_call | solution.py:525
  248.7 2.4 fusion.18
  254.6 3.2 fusion.72
  259.3 8.9 %share.5 = (bf16[512,1024]{1,0:T(8,128)(2,1)S(1)}, bf16[512,1024]{1,0:T(8,128)(2,1)S(1)}) custom-call(s32[1]{0:T(128)} %bitcast.5.at, bf16[256,2048]{1,0:T(8,128)(2,1)} %collective-permute-done.16.near_ref.refs_8_, bf16[256,2048]{1,0:T(8,128)(2,1)S(1)} %collective-permute-done.38.far_ref.refs_9_, bf16[256,2048]{1,0:T(8,128)(2,1)S(1)} %copy-done.4, ...), custom_call_target="tpu_custom_call" | custom-call | flops 4294967296 | bytes 14680064 | tf_op jit(solution)/shard_map/share/pallas_call | solution.py:380
  271.3 8.6 %share.4 = (bf16[512,1024]{1,0:T(8,128)(2,1)S(1)}, bf16[512,1024]{1,0:T(8,128)(2,1)S(1)}) custom-call(s32[1]{0:T(128)} %bitcast.5.at, bf16[256,2048]{1,0:T(8,128)(2,1)S(1)} %collective-permute-done.18.near_ref.refs_10_, bf16[256,2048]{1,0:T(8,128)(2,1)S(1)} %collective-permute-done.30.far_ref.refs_11_, bf16[256,2048]{1,0:T(8,128)(2,1)S(1)} %copy-done.6, ...), custom_call_target="tpu_custom_call" | custom-call | flops 4294967296 | bytes 14680064 | tf_op jit(solution)/shard_map/share/pallas_call | solution.py:380
  280.0 3.9 collective-permute-done.34
  284.1 2.8 fusion.47
  286.8 7.4 %collective-permute-start.49 = (f32[144,128]{1,0:T(8,128)S(1)}, f32[144,128]{1,0:T(8,128)S(1)}, u32[]{:S(2)}, u32[]{:S(2)}) collective-permute-start(f32[144,128]{1,0:T(8,128)S(1)} %add_add_fusion.1), channel_id=1, source_target_pairs={{0,6},{2,0},{4,2},{6,4},{1,7},{3,1},{5,3},{7,5},{8,14},{10,8},{12,... | collective-permute-start | bytes 221192 | tf_op jit(solution)/shard_map/ppermute | solution.py:550
  295.3 2.0 collective-permute-start.47
  299.3 18.2 %weight_down.1 = (bf16[2,512,512]{2,1,0:T(8,128)(2,1)}, bf16[2,512,512]{2,1,0:T(8,128)(2,1)}, bf16[2,512,512]{2,1,0:T(8,128)(2,1)}, bf16[2,512,512]{2,1,0:T(8,128)(2,1)}) custom-call(s32[18]{0:T(128)} %copy-done.16, bf16[512,4096]{1,0:T(8,128)(2,1)} %get-tuple-element.193.refs_0_, bf16[512,1024]{1,0:T(8,128)(2,1)} %copy-done.21, ...), custom_call_target="tpu_custom_call" | custom-call | flops 8589934592 | bytes 25165824 | tf_op jit(solution)/shard_map/weight_down/pallas_call | solution.py:447
  320.2 2.0 fusion.49
  323.7 2.4 pad_maximum_fusion
  328.2 17.9 %weight_up.1 = (bf16[2,512,512]{2,1,0:T(8,128)(2,1)}, bf16[2,512,512]{2,1,0:T(8,128)(2,1)}, bf16[2,512,512]{2,1,0:T(8,128)(2,1)}, bf16[2,512,512]{2,1,0:T(8,128)(2,1)}) custom-call(s32[18]{0:T(128)} %copy-done.16, bf16[512,4096]{1,0:T(8,128)(2,1)} %get-tuple-element.181.refs_0_, bf16[512,1024]{1,0:T(8,128)(2,1)} %copy-done.20, bf16[512,1024]{1,0:T(8,128)(2,1)} %copy-done.22, ...), custom_call_target="tpu_custom_call" | custom-call | flops 8589934592 | bytes 25165824 | tf_op jit(solution)/shard_map/weight_up/pallas_call | solution.py:447
  348.1 2.5 convert_element_type.602
  352.3 2.0 collective-permute-start.42
  354.4 1.8 collective-permute-start.43
  356.2 12.5 %convolution_convert_fusion.2 = bf16[512,2048]{1,0:T(8,128)(2,1)S(1)} fusion(bf16[512,4096]{1,0:T(8,128)(2,1)S(1)} %copy-done.62, bf16[4096,2048]{1,0:T(8,128)(2,1)} %down_ref.5), kind=kOutput, calls=%fused_computation.8 | convolution fusion | flops 8590983168 | bytes 23068672 | tf_op jit(solution)/shard_map/dot_general | solution.py:19
  368.8 5.7 %collective-permute-done.44 = bf16[2,1,512,512]{3,2,1,0:T(8,128)(2,1)S(1)} collective-permute-done((bf16[2,1,512,512]{3,2,1,0:T(8,128)(2,1)}, bf16[2,1,512,512]{3,2,1,0:T(8,128)(2,1)S(1)}, u32[]{:S(2)}, u32[]{:S(2)}) %collective-permute-start.44) | collective-permute-done | bytes 1048608 | tf_op jit(solution)/shard_map/ppermute | solution.py:545
  374.5 2.2 collective-permute-start.52
  377.0 5.8 %collective-permute-done.42 = bf16[1,512,512]{2,1,0:T(8,128)(2,1)S(1)} collective-permute-done((bf16[1,512,512]{2,1,0:T(8,128)(2,1)S(1)}, bf16[1,512,512]{2,1,0:T(8,128)(2,1)S(1)}, u32[]{:S(2)}, u32[]{:S(2)}) %collective-permute-start.42) | collective-permute-done | bytes 524320 | tf_op jit(solution)/shard_map/ppermute | solution.py:545
  383.4 1.7 collective-permute-start.57
  385.0 1.7 collective-permute-start.58
  386.7 2.2 collective-permute-done.52
  389.0 18.2 %collective-permute-done.51 = bf16[128,2176]{1,0:T(8,128)(2,1)S(1)} collective-permute-done((bf16[128,2176]{1,0:T(8,128)(2,1)S(1)}, bf16[128,2176]{1,0:T(8,128)(2,1)S(1)}, u32[]{:S(2)}, u32[]{:S(2)}) %collective-permute-start.51) | collective-permute-done | bytes 557088 | tf_op jit(solution)/shard_map/ppermute | solution.py:550
  410.5 4.0 collective-permute-start.56
  416.5 3.2 collective-permute-start.61
  421.3 15.9 %collective-permute-done.55.refs_2_ = bf16[1,1024,128]{2,1,0:T(8,128)(2,1)S(1)} collective-permute-done((bf16[1,1024,128]{2,1,0:T(8,128)(2,1)S(1)}, bf16[1,1024,128]{2,1,0:T(8,128)(2,1)S(1)}, u32[]{:S(2)}, u32[]{:S(2)}) %collective-permute-start.55) | collective-permute-done | bytes 262176 | tf_op jit(solution)/shard_map/ppermute | solution.py:550
  439.7 4.5 collective-permute-done.59.refs_5_
  444.2 14.4 %collective-permute-done.60.refs_6_ = bf16[1,1024,128]{2,1,0:T(8,128)(2,1)S(1)} collective-permute-done((bf16[1,1024,128]{2,1,0:T(8,128)(2,1)S(1)}, bf16[1,1024,128]{2,1,0:T(8,128)(2,1)S(1)}, u32[]{:S(2)}, u32[]{:S(2)}) %collective-permute-start.60) | collective-permute-done | bytes 262176 | tf_op jit(solution)/shard_map/ppermute | solution.py:550
  458.7 2.6 place.1
  461.3 3.0 fusion.51
  (293 shorter events, 58.2 us)
Async XLA Ops:
  5.0 17.1 %collective-permute-start.2 = (bf16[256,2048]{1,0:T(8,128)(2,1)}, bf16[256,2048]{1,0:T(8,128)(2,1)}, u32[]{:S(2)}, u32[]{:S(2)}) collective-permute-start(bf16[256,2048]{1,0:T(8,128)(2,1)} %bitcast.8.refs_4_), channel_id=1, source_target_pairs={{0,1},{1,0},{2,3},{3,2},{4,5},{5,4},{6,7},{7,6},{8,9},{9,8},{10,11... | collective-permute-start | bytes 3145736 | tf_op jit(solution)/shard_map/ppermute | solution.py:540
  5.5 31.1 %collective-permute-start.5 = (bf16[256,256]{1,0:T(8,128)(2,1)S(1)}, bf16[256,256]{1,0:T(8,128)(2,1)S(1)}, u32[]{:S(2)}, u32[]{:S(2)}) collective-permute-start(bf16[256,256]{1,0:T(8,128)(2,1)S(1)} %fusion.50), channel_id=1, source_target_pairs={{0,6},{1,7},{8,14},{9,15},{16,22},{17,23},{24,30},{25,31}} | collective-permute-start | bytes 393224 | tf_op jit(solution)/shard_map/ppermute | solution.py:555
  12.1 24.6 %collective-permute-start.4 = (bf16[256,256]{1,0:T(8,128)(2,1)S(1)}, bf16[256,256]{1,0:T(8,128)(2,1)}, u32[]{:S(2)}, u32[]{:S(2)}) collective-permute-start(bf16[256,256]{1,0:T(8,128)(2,1)S(1)} %fusion.50), channel_id=1, source_target_pairs={{0,4},{2,6},{1,5},{3,7},{8,12},{10,14},{9,13},{11,15},{16,20},{18,... | collective-permute-start | bytes 393224 | tf_op jit(solution)/shard_map/ppermute | solution.py:555
  14.0 22.6 %collective-permute-start.3 = (bf16[256,256]{1,0:T(8,128)(2,1)S(1)}, bf16[256,256]{1,0:T(8,128)(2,1)}, u32[]{:S(2)}, u32[]{:S(2)}) collective-permute-start(bf16[256,256]{1,0:T(8,128)(2,1)S(1)} %fusion.50), channel_id=1, source_target_pairs={{0,2},{2,4},{4,6},{1,3},{3,5},{5,7},{8,10},{10,12},{12,14},{9,11},... | collective-permute-start | bytes 393224 | tf_op jit(solution)/shard_map/ppermute | solution.py:555
  17.1 27.0 %collective-permute-start.1 = (bf16[256,2048]{1,0:T(8,128)(2,1)}, bf16[256,2048]{1,0:T(8,128)(2,1)S(1)}, u32[]{:S(2)}, u32[]{:S(2)}) collective-permute-start(bf16[256,2048]{1,0:T(8,128)(2,1)} %bitcast.8.refs_4_), channel_id=1, source_target_pairs={{0,2},{2,4},{4,6},{6,0},{1,3},{3,5},{5,7},{7,1},{8,10},{10,12},{12... | collective-permute-start | bytes 3145736 | tf_op jit(solution)/shard_map/ppermute | solution.py:550
  22.1 26.0 %collective-permute-start = (bf16[256,2048]{1,0:T(8,128)(2,1)S(1)}, bf16[256,2048]{1,0:T(8,128)(2,1)S(1)}, u32[]{:S(2)}, u32[]{:S(2)}) collective-permute-start(bf16[256,2048]{1,0:T(8,128)(2,1)S(1)} %fusion.16.near_ref), channel_id=1, source_target_pairs={{0,1},{1,0},{2,3},{3,2},{4,5},{5,4},{6,7},{7,6},{8,9},{9,8},{10,11... | collective-permute-start | bytes 3145736 | tf_op jit(solution)/shard_map/ppermute | solution.py:540
  37.7 15.4 %collective-permute-start.6 = (bf16[4,256,256]{2,1,0:T(8,128)(2,1)S(1)}, bf16[4,256,256]{2,1,0:T(8,128)(2,1)S(1)}, u32[]{:S(2)}, u32[]{:S(2)}) collective-permute-start(bf16[4,256,256]{2,1,0:T(8,128)(2,1)S(1)} %pad_maximum_fusion.3.near_ref), channel_id=1, source_target_pairs={{0,1},{1,0},{2,3},{3,2},{4,5},{5,4},{6,7},{7,6},{8,9},{9,8},{10,11... | collective-permute-start | bytes 1572872 | tf_op jit(solution)/shard_map/ppermute | solution.py:540
  44.1 113.8 %copy-start = (bf16[256,2048]{1,0:T(8,128)(2,1)}, bf16[256,2048]{1,0:T(8,128)(2,1)S(1)}, u32[]{:S(2)}) copy-start(bf16[256,2048]{1,0:T(8,128)(2,1)S(1)} %collective-permute-done.1.gnear_ref.refs_6_) | copy-start | bytes 3145732
  44.1 27.2 %collective-permute-start.7 = (bf16[256,2048]{1,0:T(8,128)(2,1)S(1)}, bf16[256,2048]{1,0:T(8,128)(2,1)S(1)}, u32[]{:S(2)}, u32[]{:S(2)}) collective-permute-start(bf16[256,2048]{1,0:T(8,128)(2,1)S(1)} %collective-permute-done.1.gnear_ref.refs_6_), channel_id=1, source_target_pairs={{0,2},{2,4},{4,6},{6,0},{1,3},{3,5},{5,7},{7,1},{8,10},{10,12},{12... | collective-permute-start | bytes 3145736 | tf_op jit(solution)/shard_map/ppermute | solution.py:550
  73.8 2.7 collective-permute-start.8
  78.5 4.7 %collective-permute-start.9 = (bf16[256,2048]{1,0:T(8,128)(2,1)S(1)}, bf16[256,2048]{1,0:T(8,128)(2,1)S(1)}, u32[]{:S(2)}, u32[]{:S(2)}) collective-permute-start(bf16[256,2048]{1,0:T(8,128)(2,1)S(1)} %add_convert_fusion.1.near_ref.refs_4_), channel_id=1, source_target_pairs={{0,1},{1,0},{2,3},{3,2},{4,5},{5,4},{6,7},{7,6},{8,9},{9,8},{10,11... | collective-permute-start | bytes 3145736 | tf_op jit(solution)/shard_map/ppermute | solution.py:540
  78.7 28.5 %collective-permute-start.10 = (bf16[256,2048]{1,0:T(8,128)(2,1)S(1)}, bf16[256,2048]{1,0:T(8,128)(2,1)S(1)}, u32[]{:S(2)}, u32[]{:S(2)}) collective-permute-start(bf16[256,2048]{1,0:T(8,128)(2,1)S(1)} %collective-permute-done.7.gnear_ref.refs_8_), channel_id=1, source_target_pairs={{0,2},{2,4},{4,6},{6,0},{1,3},{3,5},{5,7},{7,1},{8,10},{10,12},{12... | collective-permute-start | bytes 3145736 | tf_op jit(solution)/shard_map/ppermute | solution.py:550
  80.6 48.7 %collective-permute-start.11 = (bf16[256,2048]{1,0:T(8,128)(2,1)S(1)}, bf16[256,2048]{1,0:T(8,128)(2,1)S(1)}, u32[]{:S(2)}, u32[]{:S(2)}) collective-permute-start(bf16[256,2048]{1,0:T(8,128)(2,1)S(1)} %add_convert_fusion.1.near_ref.refs_4_), channel_id=1, source_target_pairs={{0,2},{2,4},{4,6},{6,0},{1,3},{3,5},{5,7},{7,1},{8,10},{10,12},{12... | collective-permute-start | bytes 3145736 | tf_op jit(solution)/shard_map/ppermute | solution.py:550
  129.4 3.4 collective-permute-start.12
  129.5 28.4 %collective-permute-start.15 = (bf16[256,2048]{1,0:T(8,128)(2,1)S(1)}, bf16[256,2048]{1,0:T(8,128)(2,1)}, u32[]{:S(2)}, u32[]{:S(2)}) collective-permute-start(bf16[256,2048]{1,0:T(8,128)(2,1)S(1)} %collective-permute-done.1.gnear_ref.refs_6_), channel_id=1, source_target_pairs={{0,1},{1,0},{2,3},{3,2},{4,5},{5,4},{6,7},{7,6},{8,9},{9,8},{10,11... | collective-permute-start | bytes 3145736 | tf_op jit(solution)/shard_map/ppermute | solution.py:540
  130.0 27.9 %collective-permute-start.14 = (bf16[256,2048]{1,0:T(8,128)(2,1)S(1)}, bf16[256,2048]{1,0:T(8,128)(2,1)S(1)}, u32[]{:S(2)}, u32[]{:S(2)}) collective-permute-start(bf16[256,2048]{1,0:T(8,128)(2,1)S(1)} %collective-permute-done.11.near_ref.refs_6_), channel_id=1, source_target_pairs={{0,1},{1,0},{2,3},{3,2},{4,5},{5,4},{6,7},{7,6},{8,9},{9,8},{10,11... | collective-permute-start | bytes 3145736 | tf_op jit(solution)/shard_map/ppermute | solution.py:540
  130.1 27.4 %collective-permute-start.16 = (bf16[256,2048]{1,0:T(8,128)(2,1)S(1)}, bf16[256,2048]{1,0:T(8,128)(2,1)}, u32[]{:S(2)}, u32[]{:S(2)}) collective-permute-start(bf16[256,2048]{1,0:T(8,128)(2,1)S(1)} %collective-permute-done.11.near_ref.refs_6_), channel_id=1, source_target_pairs={{0,2},{2,4},{4,6},{6,0},{1,3},{3,5},{5,7},{7,1},{8,10},{10,12},{12... | collective-permute-start | bytes 3145736 | tf_op jit(solution)/shard_map/ppermute | solution.py:550
  138.3 29.6 %collective-permute-start.13 = (bf16[256,2048]{1,0:T(8,128)(2,1)}, bf16[256,2048]{1,0:T(8,128)(2,1)}, u32[]{:S(2)}, u32[]{:S(2)}) collective-permute-start(bf16[256,2048]{1,0:T(8,128)(2,1)} %get-tuple-element.271.near_ref), channel_id=1, source_target_pairs={{0,1},{1,0},{2,3},{3,2},{4,5},{5,4},{6,7},{7,6},{8,9},{9,8},{10,11... | collective-permute-start | bytes 3145736 | tf_op jit(solution)/shard_map/ppermute | solution.py:540
  138.6 101.3 %copy-start.16 = (s32[18]{0:T(128)}, s32[18]{0:T(128)S(1)}, u32[]{:S(2)}) copy-start(s32[18]{0:T(128)S(1)} %stack.68.at) | copy-start | bytes 220
  157.5 48.9 %collective-permute-start.18 = (bf16[256,2048]{1,0:T(8,128)(2,1)}, bf16[256,2048]{1,0:T(8,128)(2,1)S(1)}, u32[]{:S(2)}, u32[]{:S(2)}) collective-permute-start(bf16[256,2048]{1,0:T(8,128)(2,1)} %collective-permute-done.16.near_ref.refs_8_), channel_id=1, source_target_pairs={{0,2},{2,4},{4,6},{6,0},{1,3},{3,5},{5,7},{7,1},{8,10},{10,12},{12... | collective-permute-start | bytes 3145736 | tf_op jit(solution)/shard_map/ppermute | solution.py:550
  180.0 24.8 %collective-permute-start.17 = (bf16[2,1,256,1024]{3,2,1,0:T(8,128)(2,1)S(1)}, bf16[2,1,256,1024]{3,2,1,0:T(8,128)(2,1)S(1)}, u32[]{:S(2)}, u32[]{:S(2)}) collective-permute-start(bf16[2,1,256,1024]{3,2,1,0:T(8,128)(2,1)S(1)} %bitcast.223), channel_id=1, source_target_pairs={{0,8},{8,0},{16,24},{24,16},{1,9},{9,1},{17,25},{25,17},{2,10},{10... | collective-permute-start | bytes 3145736 | tf_op jit(solution)/shard_map/ppermute | solution.py:545
  181.5 24.4 %collective-permute-start.19 = (bf16[2,1,256,1024]{3,2,1,0:T(8,128)(2,1)S(1)}, bf16[2,1,256,1024]{3,2,1,0:T(8,128)(2,1)S(1)}, u32[]{:S(2)}, u32[]{:S(2)}) collective-permute-start(bf16[2,1,256,1024]{3,2,1,0:T(8,128)(2,1)S(1)} %bitcast.222), channel_id=1, source_target_pairs={{0,16},{8,24},{16,0},{24,8},{1,17},{9,25},{17,1},{25,9},{2,18},{10... | collective-permute-start | bytes 3145736 | tf_op jit(solution)/shard_map/ppermute | solution.py:545
  206.5 4.2 collective-permute-start.22
  208.0 45.1 %collective-permute-start.39 = (bf16[256,2048]{1,0:T(8,128)(2,1)S(1)}, bf16[256,2048]{1,0:T(8,128)(2,1)S(1)}, u32[]{:S(2)}, u32[]{:S(2)}) collective-permute-start(bf16[256,2048]{1,0:T(8,128)(2,1)S(1)} %copy-done.4), channel_id=1, source_target_pairs={{0,1},{1,0},{2,3},{3,2},{4,5},{5,4},{6,7},{7,6},{8,9},{9,8},{10,11... | collective-permute-start | bytes 3145736 | tf_op jit(solution)/shard_map/ppermute | solution.py:540
  208.3 60.9 %collective-permute-start.31 = (bf16[256,2048]{1,0:T(8,128)(2,1)S(1)}, bf16[256,2048]{1,0:T(8,128)(2,1)}, u32[]{:S(2)}, u32[]{:S(2)}) collective-permute-start(bf16[256,2048]{1,0:T(8,128)(2,1)S(1)} %copy-done.6), channel_id=1, source_target_pairs={{0,1},{1,0},{2,3},{3,2},{4,5},{5,4},{6,7},{7,6},{8,9},{9,8},{10,11... | collective-permute-start | bytes 3145736 | tf_op jit(solution)/shard_map/ppermute | solution.py:540
  208.5 14.1 %collective-permute-start.20 = (bf16[1,256,1024]{2,1,0:T(8,128)(2,1)S(1)}, bf16[1,256,1024]{2,1,0:T(8,128)(2,1)S(1)}, u32[]{:S(2)}, u32[]{:S(2)}) collective-permute-start(bf16[1,256,1024]{2,1,0:T(8,128)(2,1)S(1)} %get-tuple-element.152), channel_id=1, source_target_pairs={{0,16},{8,24},{16,0},{24,8},{1,17},{9,25},{17,1},{25,9},{2,18},{10... | collective-permute-start | bytes 1572872 | tf_op jit(solution)/shard_map/ppermute | solution.py:545
  210.0 13.9 %collective-permute-start.21 = (bf16[1,256,1024]{2,1,0:T(8,128)(2,1)S(1)}, bf16[1,256,1024]{2,1,0:T(8,128)(2,1)S(1)}, u32[]{:S(2)}, u32[]{:S(2)}) collective-permute-start(bf16[1,256,1024]{2,1,0:T(8,128)(2,1)S(1)} %get-tuple-element.153), channel_id=1, source_target_pairs={{0,8},{8,0},{16,24},{24,16},{1,9},{9,1},{17,25},{25,17},{2,10},{10... | collective-permute-start | bytes 1572872 | tf_op jit(solution)/shard_map/ppermute | solution.py:545
  210.9 15.4 %collective-permute-start.25 = (bf16[512,128]{1,0:T(8,128)(2,1)S(1)}, bf16[512,128]{1,0:T(8,128)(2,1)S(1)}, u32[]{:S(2)}, u32[]{:S(2)}) collective-permute-start(bf16[512,128]{1,0:T(8,128)(2,1)S(1)} %bitcast.228), channel_id=1, source_target_pairs={{6,0},{7,1},{14,8},{15,9},{22,16},{23,17},{30,24},{31,25}} | collective-permute-start | bytes 393224 | tf_op jit(solution)/shard_map/ppermute | solution.py:560
  222.7 8.2 %collective-permute-start.24 = (bf16[512,128]{1,0:T(8,128)(2,1)S(1)}, bf16[512,128]{1,0:T(8,128)(2,1)S(1)}, u32[]{:S(2)}, u32[]{:S(2)}) collective-permute-start(bf16[512,128]{1,0:T(8,128)(2,1)S(1)} %bitcast.227), channel_id=1, source_target_pairs={{4,0},{6,2},{5,1},{7,3},{12,8},{14,10},{13,9},{15,11},{20,16},{22,... | collective-permute-start | bytes 393224 | tf_op jit(solution)/shard_map/ppermute | solution.py:560
  224.0 9.2 %collective-permute-start.23 = (bf16[512,128]{1,0:T(8,128)(2,1)S(1)}, bf16[512,128]{1,0:T(8,128)(2,1)S(1)}, u32[]{:S(2)}, u32[]{:S(2)}) collective-permute-start(bf16[512,128]{1,0:T(8,128)(2,1)S(1)} %bitcast.226), channel_id=1, source_target_pairs={{2,0},{4,2},{6,4},{3,1},{5,3},{7,5},{10,8},{12,10},{14,12},{11,9},... | collective-permute-start | bytes 393224 | tf_op jit(solution)/shard_map/ppermute | solution.py:560
  226.3 31.5 %collective-permute-start.38 = (bf16[256,2048]{1,0:T(8,128)(2,1)}, bf16[256,2048]{1,0:T(8,128)(2,1)S(1)}, u32[]{:S(2)}, u32[]{:S(2)}) collective-permute-start(bf16[256,2048]{1,0:T(8,128)(2,1)} %collective-permute-done.16.near_ref.refs_8_), channel_id=1, source_target_pairs={{0,1},{1,0},{2,3},{3,2},{4,5},{5,4},{6,7},{7,6},{8,9},{9,8},{10,11... | collective-permute-start | bytes 3145736 | tf_op jit(solution)/shard_map/ppermute | solution.py:540
  236.5 12.1 %collective-permute-start.26 = (bf16[256,2048]{1,0:T(8,128)(2,1)S(1)}, bf16[256,2048]{1,0:T(8,128)(2,1)}, u32[]{:S(2)}, u32[]{:S(2)}) collective-permute-start(bf16[256,2048]{1,0:T(8,128)(2,1)S(1)} %slice.291), channel_id=1, source_target_pairs={{0,1},{1,0},{2,3},{3,2},{4,5},{5,4},{6,7},{7,6},{8,9},{9,8},{10,11... | collective-permute-start | bytes 3145736 | tf_op jit(solution)/shard_map/ppermute | solution.py:540
  238.2 9.7 %collective-permute-start.28 = (f32[1,128]{1,0:T(1,128)S(1)}, f32[1,128]{1,0:T(1,128)S(1)}, u32[]{:S(2)}, u32[]{:S(2)}) collective-permute-start(f32[1,128]{1,0:T(1,128)S(1)} %fusion.80), channel_id=1, source_target_pairs={{0,1},{1,0},{2,3},{3,2},{4,5},{5,4},{6,7},{7,6},{8,9},{9,8},{10,11... | collective-permute-start | bytes 1544 | tf_op jit(solution)/shard_map/ppermute | solution.py:540
  247.9 22.9 %collective-permute-start.30 = (bf16[256,2048]{1,0:T(8,128)(2,1)S(1)}, bf16[256,2048]{1,0:T(8,128)(2,1)S(1)}, u32[]{:S(2)}, u32[]{:S(2)}) collective-permute-start(bf16[256,2048]{1,0:T(8,128)(2,1)S(1)} %collective-permute-done.18.near_ref.refs_10_), channel_id=1, source_target_pairs={{0,1},{1,0},{2,3},{3,2},{4,5},{5,4},{6,7},{7,6},{8,9},{9,8},{10,11... | collective-permute-start | bytes 3145736 | tf_op jit(solution)/shard_map/ppermute | solution.py:540
  251.1 1.3 collective-permute-start.27
  252.5 31.6 %collective-permute-start.29 = (bf16[2,1,256,1152]{3,2,1,0:T(8,128)(2,1)S(1)}, bf16[2,1,256,1152]{3,2,1,0:T(8,128)(2,1)S(1)}, u32[]{:S(2)}, u32[]{:S(2)}) collective-permute-start(bf16[2,1,256,1152]{3,2,1,0:T(8,128)(2,1)S(1)} %bitcast.221), channel_id=1, source_target_pairs={{0,8},{8,0},{16,24},{24,16},{1,9},{9,1},{17,25},{25,17},{2,10},{10... | collective-permute-start | bytes 3538952 | tf_op jit(solution)/shard_map/ppermute | solution.py:545
  253.1 31.0 %collective-permute-start.35 = (bf16[2,1,256,1152]{3,2,1,0:T(8,128)(2,1)S(1)}, bf16[2,1,256,1152]{3,2,1,0:T(8,128)(2,1)}, u32[]{:S(2)}, u32[]{:S(2)}) collective-permute-start(bf16[2,1,256,1152]{3,2,1,0:T(8,128)(2,1)S(1)} %bitcast.220), channel_id=1, source_target_pairs={{0,16},{8,24},{16,0},{24,8},{1,17},{9,25},{17,1},{25,9},{2,18},{10... | collective-permute-start | bytes 3538952 | tf_op jit(solution)/shard_map/ppermute | solution.py:545
  257.8 26.1 %collective-permute-start.34 = (f32[144,128]{1,0:T(8,128)S(1)}, f32[144,128]{1,0:T(8,128)S(1)}, u32[]{:S(2)}, u32[]{:S(2)}) collective-permute-start(f32[144,128]{1,0:T(8,128)S(1)} %pad_maximum_fusion.4), channel_id=1, source_target_pairs={{0,24},{8,16},{16,8},{24,0},{1,25},{9,17},{17,9},{25,1},{2,26},{10... | collective-permute-start | bytes 221192 | tf_op jit(solution)/shard_map/ppermute | solution.py:545
  269.3 14.8 %collective-permute-start.33 = (f32[144,128]{1,0:T(8,128)S(1)}, f32[144,128]{1,0:T(8,128)S(1)}, u32[]{:S(2)}, u32[]{:S(2)}) collective-permute-start(f32[144,128]{1,0:T(8,128)S(1)} %pad_maximum_fusion.4), channel_id=1, source_target_pairs={{0,16},{8,24},{16,0},{24,8},{1,17},{9,25},{17,1},{25,9},{2,18},{10... | collective-permute-start | bytes 221192 | tf_op jit(solution)/shard_map/ppermute | solution.py:545
  270.8 13.2 %collective-permute-start.32 = (f32[144,128]{1,0:T(8,128)S(1)}, f32[144,128]{1,0:T(8,128)S(1)}, u32[]{:S(2)}, u32[]{:S(2)}) collective-permute-start(f32[144,128]{1,0:T(8,128)S(1)} %pad_maximum_fusion.4), channel_id=1, source_target_pairs={{0,8},{8,0},{16,24},{24,16},{1,9},{9,1},{17,25},{25,17},{2,10},{10... | collective-permute-start | bytes 221192 | tf_op jit(solution)/shard_map/ppermute | solution.py:545
  286.8 30.6 %collective-permute-start.49 = (f32[144,128]{1,0:T(8,128)S(1)}, f32[144,128]{1,0:T(8,128)S(1)}, u32[]{:S(2)}, u32[]{:S(2)}) collective-permute-start(f32[144,128]{1,0:T(8,128)S(1)} %add_add_fusion.1), channel_id=1, source_target_pairs={{0,6},{2,0},{4,2},{6,4},{1,7},{3,1},{5,3},{7,5},{8,14},{10,8},{12,... | collective-permute-start | bytes 221192 | tf_op jit(solution)/shard_map/ppermute | solution.py:550
  294.2 23.2 %collective-permute-start.48 = (f32[144,128]{1,0:T(8,128)S(1)}, f32[144,128]{1,0:T(8,128)S(1)}, u32[]{:S(2)}, u32[]{:S(2)}) collective-permute-start(f32[144,128]{1,0:T(8,128)S(1)} %add_add_fusion.1), channel_id=1, source_target_pairs={{0,4},{2,6},{4,0},{6,2},{1,5},{3,7},{5,1},{7,3},{8,12},{10,14},{12... | collective-permute-start | bytes 221192 | tf_op jit(solution)/shard_map/ppermute | solution.py:550
  295.3 22.2 %collective-permute-start.47 = (f32[144,128]{1,0:T(8,128)S(1)}, f32[144,128]{1,0:T(8,128)S(1)}, u32[]{:S(2)}, u32[]{:S(2)}) collective-permute-start(f32[144,128]{1,0:T(8,128)S(1)} %add_add_fusion.1), channel_id=1, source_target_pairs={{0,2},{2,4},{4,6},{6,0},{1,3},{3,5},{5,7},{7,1},{8,10},{10,12},{12... | collective-permute-start | bytes 221192 | tf_op jit(solution)/shard_map/ppermute | solution.py:550
  297.3 22.9 %collective-permute-start.36 = (bf16[1,256,1152]{2,1,0:T(8,128)(2,1)}, bf16[1,256,1152]{2,1,0:T(8,128)(2,1)S(1)}, u32[]{:S(2)}, u32[]{:S(2)}) collective-permute-start(bf16[1,256,1152]{2,1,0:T(8,128)(2,1)} %get-tuple-element.170), channel_id=1, source_target_pairs={{0,16},{8,24},{16,0},{24,8},{1,17},{9,25},{17,1},{25,9},{2,18},{10... | collective-permute-start | bytes 1769480 | tf_op jit(solution)/shard_map/ppermute | solution.py:545
  297.8 22.3 %collective-permute-start.37 = (bf16[1,256,1152]{2,1,0:T(8,128)(2,1)}, bf16[1,256,1152]{2,1,0:T(8,128)(2,1)}, u32[]{:S(2)}, u32[]{:S(2)}) collective-permute-start(bf16[1,256,1152]{2,1,0:T(8,128)(2,1)} %get-tuple-element.171), channel_id=1, source_target_pairs={{0,8},{8,0},{16,24},{24,16},{1,9},{9,1},{17,25},{25,17},{2,10},{10... | collective-permute-start | bytes 1769480 | tf_op jit(solution)/shard_map/ppermute | solution.py:545
  326.2 25.9 %collective-permute-start.40 = (bf16[2,1,512,512]{3,2,1,0:T(8,128)(2,1)}, bf16[2,1,512,512]{3,2,1,0:T(8,128)(2,1)S(1)}, u32[]{:S(2)}, u32[]{:S(2)}) collective-permute-start(bf16[2,1,512,512]{3,2,1,0:T(8,128)(2,1)} %bitcast.51), channel_id=1, source_target_pairs={{0,8},{8,0},{16,24},{24,16},{1,9},{9,1},{17,25},{25,17},{2,10},{10... | collective-permute-start | bytes 3145736 | tf_op jit(solution)/shard_map/ppermute | solution.py:545
  326.7 25.4 %collective-permute-start.41 = (bf16[2,1,512,512]{3,2,1,0:T(8,128)(2,1)S(1)}, bf16[2,1,512,512]{3,2,1,0:T(8,128)(2,1)S(1)}, u32[]{:S(2)}, u32[]{:S(2)}) collective-permute-start(bf16[2,1,512,512]{3,2,1,0:T(8,128)(2,1)S(1)} %bitcast.232), channel_id=1, source_target_pairs={{0,16},{8,24},{16,0},{24,8},{1,17},{9,25},{17,1},{25,9},{2,18},{10... | collective-permute-start | bytes 3145736 | tf_op jit(solution)/shard_map/ppermute | solution.py:545
  346.1 28.4 %collective-permute-start.44 = (bf16[2,1,512,512]{3,2,1,0:T(8,128)(2,1)}, bf16[2,1,512,512]{3,2,1,0:T(8,128)(2,1)S(1)}, u32[]{:S(2)}, u32[]{:S(2)}) collective-permute-start(bf16[2,1,512,512]{3,2,1,0:T(8,128)(2,1)} %bitcast.234), channel_id=1, source_target_pairs={{0,8},{8,0},{16,24},{24,16},{1,9},{9,1},{17,25},{25,17},{2,10},{10... | collective-permute-start | bytes 3145736 | tf_op jit(solution)/shard_map/ppermute | solution.py:545
  347.6 29.0 %collective-permute-start.45 = (bf16[2,1,512,512]{3,2,1,0:T(8,128)(2,1)}, bf16[2,1,512,512]{3,2,1,0:T(8,128)(2,1)S(1)}, u32[]{:S(2)}, u32[]{:S(2)}) collective-permute-start(bf16[2,1,512,512]{3,2,1,0:T(8,128)(2,1)} %bitcast.233), channel_id=1, source_target_pairs={{0,16},{8,24},{16,0},{24,8},{1,17},{9,25},{17,1},{25,9},{2,18},{10... | collective-permute-start | bytes 3145736 | tf_op jit(solution)/shard_map/ppermute | solution.py:545
  350.8 36.0 %collective-permute-start.50 = (bf16[128,2176]{1,0:T(8,128)(2,1)S(1)}, bf16[128,2176]{1,0:T(8,128)(2,1)S(1)}, u32[]{:S(2)}, u32[]{:S(2)}) collective-permute-start(bf16[128,2176]{1,0:T(8,128)(2,1)S(1)} %get-tuple-element.277), channel_id=1, source_target_pairs={{0,2},{2,4},{4,6},{6,0},{1,3},{3,5},{5,7},{7,1},{8,10},{10,12},{12... | collective-permute-start | bytes 1671176 | tf_op jit(solution)/shard_map/ppermute | solution.py:550
  352.3 30.5 %collective-permute-start.42 = (bf16[1,512,512]{2,1,0:T(8,128)(2,1)S(1)}, bf16[1,512,512]{2,1,0:T(8,128)(2,1)S(1)}, u32[]{:S(2)}, u32[]{:S(2)}) collective-permute-start(bf16[1,512,512]{2,1,0:T(8,128)(2,1)S(1)} %get-tuple-element.195), channel_id=1, source_target_pairs={{0,16},{8,24},{16,0},{24,8},{1,17},{9,25},{17,1},{25,9},{2,18},{10... | collective-permute-start | bytes 1572872 | tf_op jit(solution)/shard_map/ppermute | solution.py:545
  354.4 28.5 %collective-permute-start.43 = (bf16[1,512,512]{2,1,0:T(8,128)(2,1)S(1)}, bf16[1,512,512]{2,1,0:T(8,128)(2,1)S(1)}, u32[]{:S(2)}, u32[]{:S(2)}) collective-permute-start(bf16[1,512,512]{2,1,0:T(8,128)(2,1)S(1)} %get-tuple-element.196), channel_id=1, source_target_pairs={{0,8},{8,0},{16,24},{24,16},{1,9},{9,1},{17,25},{25,17},{2,10},{10... | collective-permute-start | bytes 1572872 | tf_op jit(solution)/shard_map/ppermute | solution.py:545
  374.5 14.5 %collective-permute-start.52 = (bf16[128,2176]{1,0:T(8,128)(2,1)S(1)}, bf16[128,2176]{1,0:T(8,128)(2,1)S(1)}, u32[]{:S(2)}, u32[]{:S(2)}) collective-permute-start(bf16[128,2176]{1,0:T(8,128)(2,1)S(1)} %get-tuple-element.278), channel_id=1, source_target_pairs={{0,6},{2,0},{4,2},{6,4},{1,7},{3,1},{5,3},{7,5},{8,14},{10,8},{12,... | collective-permute-start | bytes 1671176 | tf_op jit(solution)/shard_map/ppermute | solution.py:550
  376.7 30.5 %collective-permute-start.51 = (bf16[128,2176]{1,0:T(8,128)(2,1)S(1)}, bf16[128,2176]{1,0:T(8,128)(2,1)S(1)}, u32[]{:S(2)}, u32[]{:S(2)}) collective-permute-start(bf16[128,2176]{1,0:T(8,128)(2,1)S(1)} %get-tuple-element.279), channel_id=1, source_target_pairs={{0,4},{2,6},{4,0},{6,2},{1,5},{3,7},{5,1},{7,3},{8,12},{10,14},{12... | collective-permute-start | bytes 1671176 | tf_op jit(solution)/shard_map/ppermute | solution.py:550
  383.4 31.2 %collective-permute-start.57 = (bf16[1,512,512]{2,1,0:T(8,128)(2,1)S(1)}, bf16[1,512,512]{2,1,0:T(8,128)(2,1)S(1)}, u32[]{:S(2)}, u32[]{:S(2)}) collective-permute-start(bf16[1,512,512]{2,1,0:T(8,128)(2,1)S(1)} %get-tuple-element.205), channel_id=1, source_target_pairs={{0,16},{8,24},{16,0},{24,8},{1,17},{9,25},{17,1},{25,9},{2,18},{10... | collective-permute-start | bytes 1572872 | tf_op jit(solution)/shard_map/ppermute | solution.py:545
  385.0 29.5 %collective-permute-start.58 = (bf16[1,512,512]{2,1,0:T(8,128)(2,1)S(1)}, bf16[1,512,512]{2,1,0:T(8,128)(2,1)S(1)}, u32[]{:S(2)}, u32[]{:S(2)}) collective-permute-start(bf16[1,512,512]{2,1,0:T(8,128)(2,1)S(1)} %get-tuple-element.206), channel_id=1, source_target_pairs={{0,8},{8,0},{16,24},{24,16},{1,9},{9,1},{17,25},{25,17},{2,10},{10... | collective-permute-start | bytes 1572872 | tf_op jit(solution)/shard_map/ppermute | solution.py:545
  408.7 7.8 %collective-permute-start.53 = (f32[64,128]{1,0:T(8,128)S(1)}, f32[64,128]{1,0:T(8,128)S(1)}, u32[]{:S(2)}, u32[]{:S(2)}) collective-permute-start(f32[64,128]{1,0:T(8,128)S(1)} %constant_dynamic-slice_fusion.6), channel_id=1, source_target_pairs={{0,1},{1,0},{2,3},{3,2},{4,5},{5,4},{6,7},{7,6},{8,9},{9,8},{10,11... | collective-permute-start | bytes 98312 | tf_op jit(solution)/shard_map/ppermute | solution.py:540
  409.8 51.5 %collective-permute-start.46 = (bf16[256,2048]{1,0:T(8,128)(2,1)}, bf16[256,2048]{1,0:T(8,128)(2,1)}, u32[]{:S(2)}, u32[]{:S(2)}) collective-permute-start(bf16[256,2048]{1,0:T(8,128)(2,1)} %slice.262), channel_id=1, source_target_pairs={{0,1},{1,0},{2,3},{3,2},{4,5},{5,4},{6,7},{7,6},{8,9},{9,8},{10,11... | collective-permute-start | bytes 3145736 | tf_op jit(solution)/shard_map/ppermute | solution.py:540
  410.5 10.8 %collective-permute-start.56 = (bf16[1,1024,128]{2,1,0:T(8,128)(2,1)S(1)}, bf16[1,1024,128]{2,1,0:T(8,128)(2,1)S(1)}, u32[]{:S(2)}, u32[]{:S(2)}) collective-permute-start(bf16[1,1024,128]{2,1,0:T(8,128)(2,1)S(1)} %get-tuple-element.292), channel_id=1, source_target_pairs={{0,6},{2,0},{4,2},{6,4},{1,7},{3,1},{5,3},{7,5},{8,14},{10,8},{12,... | collective-permute-start | bytes 786440 | tf_op jit(solution)/shard_map/ppermute | solution.py:550
  414.5 22.6 %collective-permute-start.55 = (bf16[1,1024,128]{2,1,0:T(8,128)(2,1)S(1)}, bf16[1,1024,128]{2,1,0:T(8,128)(2,1)S(1)}, u32[]{:S(2)}, u32[]{:S(2)}) collective-permute-start(bf16[1,1024,128]{2,1,0:T(8,128)(2,1)S(1)} %get-tuple-element.293), channel_id=1, source_target_pairs={{0,4},{2,6},{4,0},{6,2},{1,5},{3,7},{5,1},{7,3},{8,12},{10,14},{12... | collective-permute-start | bytes 786440 | tf_op jit(solution)/shard_map/ppermute | solution.py:550
  414.5 25.2 %collective-permute-start.54 = (bf16[1,1024,128]{2,1,0:T(8,128)(2,1)S(1)}, bf16[1,1024,128]{2,1,0:T(8,128)(2,1)S(1)}, u32[]{:S(2)}, u32[]{:S(2)}) collective-permute-start(bf16[1,1024,128]{2,1,0:T(8,128)(2,1)S(1)} %get-tuple-element.294), channel_id=1, source_target_pairs={{0,2},{2,4},{4,6},{6,0},{1,3},{3,5},{5,7},{7,1},{8,10},{10,12},{12... | collective-permute-start | bytes 786440 | tf_op jit(solution)/shard_map/ppermute | solution.py:550
  416.5 23.2 %collective-permute-start.61 = (bf16[1,1024,128]{2,1,0:T(8,128)(2,1)}, bf16[1,1024,128]{2,1,0:T(8,128)(2,1)S(1)}, u32[]{:S(2)}, u32[]{:S(2)}) collective-permute-start(bf16[1,1024,128]{2,1,0:T(8,128)(2,1)} %get-tuple-element.286), channel_id=1, source_target_pairs={{0,6},{2,0},{4,2},{6,4},{1,7},{3,1},{5,3},{7,5},{8,14},{10,8},{12,... | collective-permute-start | bytes 786440 | tf_op jit(solution)/shard_map/ppermute | solution.py:550
  421.3 23.0 %collective-permute-start.59 = (bf16[1,1024,128]{2,1,0:T(8,128)(2,1)S(1)}, bf16[1,1024,128]{2,1,0:T(8,128)(2,1)S(1)}, u32[]{:S(2)}, u32[]{:S(2)}) collective-permute-start(bf16[1,1024,128]{2,1,0:T(8,128)(2,1)S(1)} %get-tuple-element.288), channel_id=1, source_target_pairs={{0,2},{2,4},{4,6},{6,0},{1,3},{3,5},{5,7},{7,1},{8,10},{10,12},{12... | collective-permute-start | bytes 786440 | tf_op jit(solution)/shard_map/ppermute | solution.py:550
  437.2 21.5 %collective-permute-start.60 = (bf16[1,1024,128]{2,1,0:T(8,128)(2,1)S(1)}, bf16[1,1024,128]{2,1,0:T(8,128)(2,1)S(1)}, u32[]{:S(2)}, u32[]{:S(2)}) collective-permute-start(bf16[1,1024,128]{2,1,0:T(8,128)(2,1)S(1)} %get-tuple-element.289), channel_id=1, source_target_pairs={{0,4},{2,6},{4,0},{6,2},{1,5},{3,7},{5,1},{7,3},{8,12},{10,14},{12... | collective-permute-start | bytes 786440 | tf_op jit(solution)/shard_map/ppermute | solution.py:550
  (61 other events, 744.1 us)

commit v3 on v2

--- a/solution.py
+++ b/solution.py
@@ -582,9 +582,11 @@
     return second_a, second_b, own, got_x, got_y
 
 
-def dp_last(second_a, second_b, own, got_x, got_y):
-    last_a = cross(second_a, 2)
-    last_b = cross(second_b, 1)
+def dp_second(second_a, second_b):
+    return cross(second_a, 2), cross(second_b, 1)
+
+
+def dp_join(own, got_x, got_y, last_a, last_b):
     return jnp.concatenate(
         [
             own[0].astype(f32) + got_x[1].astype(f32) + last_a.astype(f32),
@@ -592,6 +594,10 @@
         ],
         axis=1,
     )
+
+
+def dp_last(second_a, second_b, own, got_x, got_y):
+    return dp_join(own, got_x, got_y, *dp_second(second_a, second_b))
 
 
 def norm_parts(rows):
@@ -692,9 +698,9 @@
     if seqs > 3:
         grad_hidden, grad_held[3] = after(grad_hidden, grad_held[3])
     grad_normed_two = contract_cols(grad_hidden, w_up).astype(low)
-    if seqs > 1:
-        grad_normed_two, held[1] = after(grad_normed_two, held[1])
     grad_normed_two = pair_sum(grad_normed_two)
+    result = dot(activated, w_down).astype(low)
+    grad_normed_two, result, *held[1:2] = after(grad_normed_two, result, *held[1:2])
 
     back, grad_ln2_gain, grad_ln2_bias = norm_back(
         grad_normed_two, unit_two, inverse_two, ln2_gain
@@ -740,14 +746,53 @@
         grad_attended, acts[1], held[2], *parts_out = after(
             grad_attended, acts[1], held[2], *parts_out
         )
+        for step in range(3, seqs):
+            held[step] = shift(held[step - 1], 1)
     first_out = dp_first(parts_out, 1)
+
+    def to_seq(item, by, axis):
+        at = lax.rem(at_seq + by, seqs)
+        return lax.dynamic_slice_in_dim(item, at * out_part, out_part, axis)
 
     grad_query, grad_both = attend_back(
         info, query, grad_attended, attended, lse, near, far, pos, heads, head
     )
+    seconds = first_out[:2]
     if seqs > 1:
-        grad_both, held[-1], *seconds = after(grad_both, held[-1], *first_out[:2])
-        first_out = (*seconds, *first_out[2:])
+        grad_query, grad_both, held[-1], *seconds = after(
+            grad_query, grad_both, held[-1], *seconds
+        )
+    last_out = dp_second(*seconds)
+
+    for step in range(len(acts), seqs):
+        shared_part(step)
+    acts[-1], *last_out = after(acts[-1], *last_out)
+    sum_out = dp_join(*first_out[2:], *last_out)[0]
+    downs = hidden_weights(
+        table,
+        acts,
+        [item for couple in zip(grad_held, grad_far) for item in couple],
+        hidden_part,
+        dp_part,
+        "weight_down",
+    )
+    grads[0], sum_out, *downs = after(grads[0], sum_out, *downs)
+    first_down = dp_first(downs, 1)
+    narrow = sum_out.astype(low)
+    out_parts = [shift(to_seq(narrow, by, 0), by) for by in range(1, seqs)]
+    ups = hidden_weights(
+        table,
+        grads,
+        [item for couple in zip(held, held_far) for item in couple],
+        hidden_part,
+        dp_part,
+        "weight_up",
+    )
+    grad_query, grad_both, *rest = after(grad_query, grad_both, *first_down[:2], *ups, *out_parts)
+    last_down = dp_second(*rest[:2])
+    first_up = dp_first(rest[2:6], 1)
+    out_parts = rest[6:]
+
     grad_both = grad_both.reshape(2, seqs, 2, rows_own, head)
     kept = lax.dynamic_index_in_dim(grad_both, at_core, 0, False)
     given = lax.dynamic_index_in_dim(grad_both, 1 - at_core, 0, False)
@@ -759,13 +804,23 @@
     grad_kv = total.astype(low)
     grad_qkv = jnp.concatenate([grad_query, grad_kv], axis=1)
     w_qkv = jnp.concatenate([w_query, jnp.where(at_core == 0, w_key, w_value)], axis=1)
-    grad_normed = pair_sum(contract_cols(grad_qkv, w_qkv).astype(low))
+    grad_normed = contract_cols(grad_qkv, w_qkv).astype(low)
+    grad_normed, *last_down = after(grad_normed, *last_down)
+    grad_normed = pair_sum(grad_normed)
+    sum_down = dp_join(*first_down[2:], *last_down).astype(low)
+
+    downs = [to_seq(sum_down, by, 2) for by in range(seqs)]
+    grad_qkv, *downs = after(grad_qkv, *downs)
+    downs = [downs[0]] + [shift(downs[by], by) for by in range(1, seqs)]
+    parts = branch_weights(table, normed, normed_far, grad_qkv, dp_part, "weight_query")
+    rest = after(*parts, *first_up[:2])
+    first_query = dp_first(rest[:4], 1)
+    last_up = dp_second(*rest[4:6])
+
     back, grad_ln1_gain, grad_ln1_bias = norm_back(
         grad_normed, unit_one, inverse_one, ln1_gain
     )
     grad_input = (grad_middle + back).astype(low)[None]
-
-    parts = branch_weights(table, normed, normed_far, grad_qkv, dp_part, "weight_query")
     grad_b_value = jnp.where(at_core == 1, jnp.sum(grad_kv.astype(f32), axis=0), 0.0)
     grad_b_query = jnp.sum(grad_query.astype(f32), axis=0)
     features = [
@@ -791,64 +846,33 @@
         ],
         axis=0,
     )
-    share_at, packed, *parts = after(share_at, packed, *parts)
-    first_query = dp_first(parts, 1)
+    rest = after(packed, *last_up, *first_query[:2], *downs)
+    packed, last_up, downs = rest[0], rest[1:3], rest[5:]
+    last_query = dp_second(*rest[3:5])
+    sum_up = dp_join(*first_up[2:], *last_up).astype(low)
+    ups = [to_seq(sum_up, 0, 2)]
+    for by in range(1, seqs):
+        ups.append(shift(to_seq(sum_up, by, 2), by))
     total = packed + cross(packed, 1) + cross(packed, 2) + cross(packed, 3)
-
-    for step in range(len(acts), seqs):
-        shared_part(step)
-    acts[-1], total, *seconds = after(acts[-1], total, *first_query[:2])
-    first_query = (*seconds, *first_query[2:])
-    downs = hidden_weights(
-        table,
-        acts,
-        [item for couple in zip(grad_held, grad_far) for item in couple],
-        hidden_part,
-        dp_part,
-        "weight_down",
-    )
-    sum_branch = jnp.concatenate([dp_last(*first_out)[0], dp_last(*first_query)[0]], axis=1)
-    grads[0], sum_branch, *downs = after(grads[0], sum_branch, *downs)
-    first_down = dp_first(downs, 1)
+    total, *last_query = after(total, *last_query)
     packed = total
     for by in range(1, seqs):
         total = total + shift(packed, by)
-    ups = hidden_weights(
-        table,
-        grads,
-        [item for couple in zip(held, held_far) for item in couple],
-        hidden_part,
-        dp_part,
-        "weight_up",
-    )
-    activated, *ups = after(activated, *ups)
-    first_up = dp_first(ups, 1)
-    activated, *seconds = after(activated, *first_down[:2])
-    first_down = (*seconds, *first_down[2:])
-    result = dot(activated, w_down).astype(low)
-    sum_down = dp_last(*first_down).astype(low)
-    result, sum_down, *seconds = after(result, sum_down, *first_up[:2])
-    first_up = (*seconds, *first_up[2:])
+    sum_query = dp_join(*first_query[2:], *last_query)[0]
+    narrow = sum_query.astype(low)
+    query_parts = [to_seq(narrow, by, 0) for by in range(1, seqs)]
+    share_at, *query_parts = after(share_at, *query_parts)
+    query_parts = [shift(item, by + 1) for by, item in enumerate(query_parts)]
     output = (middle + (pair_sum(result) + b_down)).astype(low)[None]
-    sum_up = dp_last(*first_up).astype(low)
-
-    def to_seq(item, by, axis):
-        at = lax.rem(at_seq + by, seqs)
-        return lax.dynamic_slice_in_dim(item, at * out_part, out_part, axis)
-
-    downs, ups = [], []
-    for items, whole in ((downs, sum_down), (ups, sum_up)):
-        items.append(to_seq(whole, 0, 2))
-        for by in range(1, seqs):
-            items.append(shift(to_seq(whole, by, 2), by))
     out_w_down, out_w_up = place(share_at, downs, ups)
 
-    narrow = sum_branch.astype(low)
-    branch = to_seq(sum_branch, 0, 0)
-    for by in range(1, seqs):
-        branch = branch + shift(to_seq(narrow, by, 0), by).astype(f32)
-    out_w_out = branch[:, : heads * head].T
-    out_qkv = branch[:, heads * head :]
+    out_qkv = to_seq(sum_query, 0, 0)
+    for item in query_parts:
+        out_qkv = out_qkv + item.astype(f32)
+    out_w_out = to_seq(sum_out, 0, 0)
+    for item in out_parts:
+        out_w_out = out_w_out + item.astype(f32)
+    out_w_out = out_w_out.T
     out_w_query = out_qkv[:, : heads * head]
     half = out_part // 2
     last_kv = out_qkv[:, heads * head :]

time: 471 us -> 434 us (0.921)
  waiting for transfers between devices: 158 us -> 110 us
  starting transfers between devices: 74.5 us -> 85.1 us
  other arithmetic: 40.5 us -> 31.6 us
  local copies, waits for them, and re-layouts: 13.1 us -> 19.8 us
    ppermute x18 -> x21, waiting for transfers between devices: 105 us -> 36.1 us  [shift(): lax.ppermute(item, 'seq', [(i, (i + by) % size) for i in range(size)])]
    ppermute x18 -> x21, starting transfers between devices: 29.8 us -> 46.7 us  [shift(): lax.ppermute(item, 'seq', [(i, (i + by) % size) for i in range(size)])]
    ppermute x19, waiting for transfers between devices: 39.7 us -> 55.1 us  [cross(): return lax.ppermute(item, 'dp', [(i, i ^ bits) for i in range(size)])]
    unnamed x133 -> x143, local copies, waits for them, and re-layouts: 8.32 us -> 10.1 us
  transfers between devices with their start and end apart: 62 -> 65, of which waited for: 24 -> 23; matrix products, arithmetic and copies ran while one was open for 18% -> 21% of each run, Pallas kernels for 25% -> 23%
where the time goes in v3:
time: 434 us; the launch traced here: 428 us
  Pallas kernels  118 us (27%)
  waiting for transfers between devices  110 us (25%)
  starting transfers between devices  85.1 us (20%)
  matrix products  57.3 us (13%)
  other arithmetic  31.6 us (7%)
  local copies, waits for them, and re-layouts  19.8 us (5%)
  between operations  5.79 us (1%)
    ppermute x19, waiting for transfers between devices, cross(): return lax.ppermute(item, 'dp', [(i, i ^ bits) for i in range(size)])  55.1 us
    ppermute x21, starting transfers between devices, shift(): lax.ppermute(item, 'seq', [(i, (i + by) % size) for i in range(size)])  46.7 us
    dot_general x4, matrix products, contract_cols(): lax.dot_general(left, right, (((1,), (1,)), ((), ())), preferred_element_...  38.5 us
    ppermute x21, waiting for transfers between devices, shift(): lax.ppermute(item, 'seq', [(i, (i + by) % size) for i in range(size)])  36.1 us
    pallas_call x2, Pallas kernels, hidden_weights(): pl.pallas_call(functools.partial(hidden_kernel, len(lefts)), grid_spec=sp...  35.9 us
    pallas_call x3, Pallas kernels, share(): pl.pallas_call(share_kernel, grid_spec=spec, out_shape=(shape, shape), co...  27.2 us
    ppermute x19, starting transfers between devices, cross(): return lax.ppermute(item, 'dp', [(i, i ^ bits) for i in range(size)])  22.6 us
    pallas_call x1, Pallas kernels, up(): pl.pallas_call(up_kernel, grid=(units // tile,), in_specs=[row, row, pl.B...  19.6 us
  transfers between devices with their start and end apart: 65, of which 23 were waited for; matrix products, arithmetic and copies ran while one was open for 21% of the time, Pallas kernels for 23%

profile of v3, /device:TPU:0, one launch (start us, length us, event | category | flops | bytes accessed | tf_op | source)
XLA Modules:
  0.0 428.1 jit_solution(12969041739453631359)
XLA Ops:
  0.7 1.6 convert_reduce_fusion.1
  2.3 1.6 fusion.24
  5.7 3.0 collective-permute-start.1
  8.7 3.5 collective-permute-start.3
  12.1 3.6 collective-permute-start.4
  20.7 1.6 collective-permute-start.5
  22.3 14.4 %convolution_convert_fusion.g_ref = bf16[512,4096]{1,0:T(8,128)(2,1)} fusion(bf16[4096,2048]{1,0:T(8,128)(2,1)} %down_ref.5, bf16[256,2048]{1,0:T(8,128)(2,1)} %collective-permute-done.2.refs_5_, bf16[256,2048]{1,0:T(8,128)(2,1)} %bitcast.8.refs_4_), kind=kOutput, calls=%fused_computation | convolution fusion | flops 8596226048 | bytes 23068672 | tf_op jit(solution)/shard_map/dot_general | solution.py:27
  38.1 1.9 collective-permute-done.5
  41.1 4.6 %collective-permute-start.7 = (bf16[256,2048]{1,0:T(8,128)(2,1)S(1)}, bf16[256,2048]{1,0:T(8,128)(2,1)S(1)}, u32[]{:S(2)}, u32[]{:S(2)}) collective-permute-start(bf16[256,2048]{1,0:T(8,128)(2,1)S(1)} %collective-permute-done.1.gnear_ref.refs_6_), channel_id=1, source_target_pairs={{0,2},{2,4},{4,6},{6,0},{1,3},{3,5},{5,7},{7,1},{8,10},{10,12},{12... | collective-permute-start | bytes 3145736 | tf_op jit(solution)/shard_map/ppermute | solution.py:550
  45.7 2.4 add_convert_fusion.2.q_ref
  48.2 7.0 %attend.1 = (bf16[512,1024]{1,0:T(8,128)(2,1)S(1)}, f32[8,512]{1,0:T(8,128)S(1)}) custom-call(s32[4]{0:T(128)S(1)} %pad_add_fusion.info, bf16[512,1024]{1,0:T(8,128)(2,1)S(1)} %add_convert_fusion.2.q_ref, bf16[4,256,256]{2,1,0:T(8,128)(2,1)S(1)} %pad_maximum_fusion.2.near_ref, bf16[4,256,256]{2,1,0:T(8,128)(2,1)S(1)} %collective-permute-done.6.far_ref, ...), custom_call_target="tpu_custom_call" | custom-call | flops 8589934592 | bytes 2097152 | tf_op jit(solution)/shard_map/attend/pallas_call | solution.py:223
  55.2 17.2 %collective-permute-done.7.gnear_ref.refs_8_ = bf16[256,2048]{1,0:T(8,128)(2,1)S(1)} collective-permute-done((bf16[256,2048]{1,0:T(8,128)(2,1)S(1)}, bf16[256,2048]{1,0:T(8,128)(2,1)S(1)}, u32[]{:S(2)}, u32[]{:S(2)}) %collective-permute-start.7) | collective-permute-done | bytes 1048608 | tf_op jit(solution)/shard_map/ppermute | solution.py:550
  72.4 2.3 convolution_convert_fusion.1
  74.9 2.6 collective-permute-done.8
  80.5 1.7 collective-permute-done.9.far_ref.refs_5_
  82.2 19.6 %up.1 = (bf16[512,4096]{1,0:T(8,128)(2,1)}, bf16[512,4096]{1,0:T(8,128)(2,1)}, f32[1,4096]{1,0:T(1,128)S(1)}) custom-call(bf16[256,2048]{1,0:T(8,128)(2,1)S(1)} %add_convert_fusion.1.near_ref.refs_4_, bf16[256,2048]{1,0:T(8,128)(2,1)S(1)} %collective-permute-done.9.far_ref.refs_5_, bf16[2048,4096]{1,0:T(8,128)(2,1)} %up_ref.5, f32[1,4096]{1,0:T(1,128)S(1)} %bitcast.227, ...), custom_call_target="tpu_custom_call" | custom-call | flops 8589934592 | bytes 33554432 | tf_op jit(solution)/shard_map/up/pallas_call | solution.py:319
  101.7 5.7 %collective-permute-done.10.gnear_ref.refs_10_ = bf16[256,2048]{1,0:T(8,128)(2,1)S(1)} collective-permute-done((bf16[256,2048]{1,0:T(8,128)(2,1)S(1)}, bf16[256,2048]{1,0:T(8,128)(2,1)S(1)}, u32[]{:S(2)}, u32[]{:S(2)}) %collective-permute-start.10) | collective-permute-done | bytes 1048608 | tf_op jit(solution)/shard_map/ppermute | solution.py:550
  108.4 13.7 %convolution_convert_fusion.3 = bf16[512,2048]{1,0:T(8,128)(2,1)S(1)} fusion(bf16[512,4096]{1,0:T(8,128)(2,1)} %get-tuple-element.199.refs_0_, bf16[2048,4096]{1,0:T(8,128)(2,1)} %up_ref.5), kind=kOutput, calls=%fused_computation.8 | convolution fusion | flops 8590983168 | bytes 23068672 | tf_op jit(solution)/shard_map/dot_general | solution.py:27
  122.2 13.6 %convolution_convert_fusion.2 = bf16[512,2048]{1,0:T(8,128)(2,1)S(1)} fusion(bf16[512,4096]{1,0:T(8,128)(2,1)} %get-tuple-element.160.refs_0_, bf16[4096,2048]{1,0:T(8,128)(2,1)} %down_ref.5), kind=kOutput, calls=%fused_computation.7 | convolution fusion | flops 8590983168 | bytes 23068672 | tf_op jit(solution)/shard_map/dot_general | solution.py:19
  138.3 1.6 collective-permute-done.13
  139.9 4.4 %convert_reduce_fusion.3 = (f32[2048]{0:T(1024)S(1)}, bf16[256,2048]{1,0:T(8,128)(2,1)}, f32[256,2048]{1,0:T(8,128)}, bf16[1,256,2048]{2,1,0:T(8,128)(2,1)}, f32[2048]{0:T(1024)S(1)}) fusion(f32[256]{0:T(256)S(1)} %get-tuple-element.369, f32[256]{0:T(256)S(1)} %add_rsqrt_fusion, f32[256,2048]{1,0:T(8,128)S(1)} %get-tuple-element.324, ...), kind=kLoop, calls=%fused_computation.48 | loop fusion | flops 9957376 | bytes 11571200 | tf_op jit(solution)/shard_map/reduce_sum | solution.py:712
  145.2 9.0 %share.3 = (bf16[512,1024]{1,0:T(8,128)(2,1)S(1)}, bf16[512,1024]{1,0:T(8,128)(2,1)S(1)}) custom-call(s32[1]{0:T(128)} %bitcast.5.at, bf16[256,2048]{1,0:T(8,128)(2,1)S(1)} %collective-permute-done.12.near_ref.refs_6_, bf16[256,2048]{1,0:T(8,128)(2,1)S(1)} %collective-permute-done.15.far_ref.refs_7_, ...), custom_call_target="tpu_custom_call" | custom-call | flops 4294967296 | bytes 14680064 | tf_op jit(solution)/shard_map/share/pallas_call | solution.py:380
  156.3 7.7 %weight_out.1 = (bf16[2,256,1024]{2,1,0:T(8,128)(2,1)S(1)}, bf16[2,256,1024]{2,1,0:T(8,128)(2,1)S(1)}, bf16[2,256,1024]{2,1,0:T(8,128)(2,1)S(1)}, bf16[2,256,1024]{2,1,0:T(8,128)(2,1)S(1)}) custom-call(s32[18]{0:T(128)S(1)} %stack.68.at, bf16[256,2048]{1,0:T(8,128)(2,1)} %get-tuple-element.319.near_ref, bf16[256,2048]{1,0:T(8,128)(2,1)} %collective-permute-done.14.far_ref, ...), custom_call_target="tpu_custom_call" | custom-call | flops 2147483648 | bytes 4194304 | tf_op jit(solution)/shard_map/weight_out/pallas_call | solution.py:525
  164.0 5.3 %fusion.41.do_ref = bf16[512,1024]{1,0:T(8,128)(2,1)S(1)} fusion(bf16[1024,2048]{1,0:T(8,128)(2,1)} %param.31, bf16[256,2048]{1,0:T(8,128)(2,1)} %collective-permute-done.14.far_ref, bf16[256,2048]{1,0:T(8,128)(2,1)} %get-tuple-element.319.near_ref), kind=kOutput, calls=%fused_computation.61 | convolution fusion | flops 2152202240 | bytes 7340032 | tf_op jit(solution)/shard_map/dot_general | solution.py:27
  169.3 3.1 collective-permute-done.17.near_ref.refs_8_
  172.4 1.6 collective-permute-start.20
  174.0 1.5 collective-permute-start.19
  175.5 10.0 %attend_back.1 = (bf16[512,1024]{1,0:T(8,128)(2,1)S(1)}, bf16[2,2048,128]{2,1,0:T(8,128)(2,1)S(1)}) custom-call(s32[4]{0:T(128)S(1)} %pad_add_fusion.info, bf16[512,1024]{1,0:T(8,128)(2,1)S(1)} %copy-done.34, bf16[512,1024]{1,0:T(8,128)(2,1)S(1)} %fusion.41.do_ref, bf16[512,1024]{1,0:T(8,128)(2,1)} %copy-done.32, f32[8,512]{1,0:T(8,128)S(1)} %get-tuple-element.171.lse_ref, ...), custom_call_target="tpu_custom_call" | custom-call | flops 21474836480 | bytes 4194304 | tf_op jit(solution)/shard_map/attend_back/pallas_call | solution.py:268
  185.5 12.5 %collective-permute-done.20 = bf16[2,1,256,1024]{3,2,1,0:T(8,128)(2,1)S(1)} collective-permute-done((bf16[2,1,256,1024]{3,2,1,0:T(8,128)(2,1)S(1)}, bf16[2,1,256,1024]{3,2,1,0:T(8,128)(2,1)S(1)}, u32[]{:S(2)}, u32[]{:S(2)}) %collective-permute-start.20) | collective-permute-done | bytes 1048608 | tf_op jit(solution)/shard_map/ppermute | solution.py:545
  201.2 1.5 collective-permute-start.24
  202.7 9.0 %share.5 = (bf16[512,1024]{1,0:T(8,128)(2,1)S(1)}, bf16[512,1024]{1,0:T(8,128)(2,1)S(1)}) custom-call(s32[1]{0:T(128)} %bitcast.5.at, bf16[256,2048]{1,0:T(8,128)(2,1)S(1)} %collective-permute-done.17.near_ref.refs_8_, bf16[256,2048]{1,0:T(8,128)(2,1)S(1)} %collective-permute-done.25.far_ref.refs_9_, bf16[256,2048]{1,0:T(8,128)(2,1)S(1)} %copy-done.7, ...), custom_call_target="tpu_custom_call" | custom-call | flops 4294967296 | bytes 14680064 | tf_op jit(solution)/shard_map/share/pallas_call | solution.py:380
  214.7 9.2 %share.4 = (bf16[512,1024]{1,0:T(8,128)(2,1)S(1)}, bf16[512,1024]{1,0:T(8,128)(2,1)S(1)}) custom-call(s32[1]{0:T(128)} %bitcast.5.at, bf16[256,2048]{1,0:T(8,128)(2,1)S(1)} %collective-permute-done.18.near_ref.refs_10_, bf16[256,2048]{1,0:T(8,128)(2,1)S(1)} %collective-permute-done.21.far_ref.refs_11_, bf16[256,2048]{1,0:T(8,128)(2,1)S(1)} %copy-done.10, ...), custom_call_target="tpu_custom_call" | custom-call | flops 4294967296 | bytes 14680064 | tf_op jit(solution)/shard_map/share/pallas_call | solution.py:380
  225.4 17.9 %weight_down.1 = (bf16[2,512,512]{2,1,0:T(8,128)(2,1)}, bf16[2,512,512]{2,1,0:T(8,128)(2,1)}, bf16[2,512,512]{2,1,0:T(8,128)(2,1)}, bf16[2,512,512]{2,1,0:T(8,128)(2,1)}) custom-call(s32[18]{0:T(128)} %copy-done.19, bf16[512,4096]{1,0:T(8,128)(2,1)} %get-tuple-element.160.refs_0_, bf16[512,1024]{1,0:T(8,128)(2,1)} %copy-done.27, ...), custom_call_target="tpu_custom_call" | custom-call | flops 8589934592 | bytes 25165824 | tf_op jit(solution)/shard_map/weight_down/pallas_call | solution.py:447
  243.4 1.4 collective-permute-start.28
  245.6 11.3 %collective-permute-start.30 = (bf16[128,1024]{1,0:T(8,128)(2,1)S(1)}, bf16[128,1024]{1,0:T(8,128)(2,1)}, u32[]{:S(2)}, u32[]{:S(2)}) collective-permute-start(bf16[128,1024]{1,0:T(8,128)(2,1)S(1)} %get-tuple-element.349), channel_id=1, source_target_pairs={{0,4},{2,6},{4,0},{6,2},{1,5},{3,7},{5,1},{7,3},{8,12},{10,14},{12... | collective-permute-start | bytes 786440 | tf_op jit(solution)/shard_map/ppermute | solution.py:550
  256.9 17.9 %weight_up.1 = (bf16[2,512,512]{2,1,0:T(8,128)(2,1)}, bf16[2,512,512]{2,1,0:T(8,128)(2,1)}, bf16[2,512,512]{2,1,0:T(8,128)(2,1)}, bf16[2,512,512]{2,1,0:T(8,128)(2,1)}) custom-call(s32[18]{0:T(128)} %copy-done.19, bf16[512,4096]{1,0:T(8,128)(2,1)} %get-tuple-element.199.refs_0_, bf16[512,1024]{1,0:T(8,128)(2,1)} %copy-done.24, bf16[512,1024]{1,0:T(8,128)(2,1)} %copy-done.25, ...), custom_call_target="tpu_custom_call" | custom-call | flops 8589934592 | bytes 25165824 | tf_op jit(solution)/shard_map/weight_up/pallas_call | solution.py:447
  274.9 2.6 fusion.64
  280.2 1.4 add_bitcast_fusion
  286.9 6.6 %collective-permute-done.35 = bf16[512,128]{1,0:T(8,128)(2,1)S(1)} collective-permute-done((bf16[512,128]{1,0:T(8,128)(2,1)S(1)}, bf16[512,128]{1,0:T(8,128)(2,1)S(1)}, u32[]{:S(2)}, u32[]{:S(2)}) %collective-permute-start.35) | collective-permute-done | bytes 131104 | tf_op jit(solution)/shard_map/ppermute | solution.py:560
  293.6 1.7 collective-permute-start.42
  295.2 3.2 collective-permute-done.34
  299.1 5.1 %fusion.4 = bf16[512,2048]{1,0:T(8,128)(2,1)S(1)} fusion(bf16[2048,128]{1,0:T(8,128)(2,1)S(1)} %copy-done.50, bf16[2048,1024]{1,0:T(8,128)(2,1)} %param.26, bf16[512,128]{1,0:T(8,128)(2,1)S(1)} %get-tuple-element.322, bf16[512,1024]{1,0:T(8,128)(2,1)S(1)} %get-tuple-element.208), kind=kOutput, calls=%fused_computation.5 | convolution fusion | flops 2428764160 | bytes 7995392 | tf_op jit(solution)/shard_map/dot_general | solution.py:27
  305.5 1.9 fusion.60
  309.5 2.3 collective-permute-start.47
  311.8 8.2 %weight_query.1 = (bf16[2,256,1152]{2,1,0:T(8,128)(2,1)S(1)}, bf16[2,256,1152]{2,1,0:T(8,128)(2,1)S(1)}, bf16[2,256,1152]{2,1,0:T(8,128)(2,1)S(1)}, bf16[2,256,1152]{2,1,0:T(8,128)(2,1)}) custom-call(s32[18]{0:T(128)S(1)} %copy-done.20, bf16[256,2048]{1,0:T(8,128)(2,1)S(1)} %copy-done.12, bf16[256,2048]{1,0:T(8,128)(2,1)S(1)} %copy-done.22, ...), custom_call_target="tpu_custom_call" | custom-call | flops 2415919104 | bytes 4718592 | tf_op jit(solution)/shard_map/weight_query/pallas_call | solution.py:525
  320.2 2.6 collective-permute-done.41
  323.1 1.7 collective-permute-start.46
  324.8 1.4 collective-permute-start.45
  327.6 2.0 fusion.70
  329.6 19.7 %collective-permute-done.46 = bf16[2,1,256,1152]{3,2,1,0:T(8,128)(2,1)S(1)} collective-permute-done((bf16[2,1,256,1152]{3,2,1,0:T(8,128)(2,1)S(1)}, bf16[2,1,256,1152]{3,2,1,0:T(8,128)(2,1)S(1)}, u32[]{:S(2)}, u32[]{:S(2)}) %collective-permute-start.46) | collective-permute-done | bytes 1179680 | tf_op jit(solution)/shard_map/ppermute | solution.py:545
  349.3 1.6 collective-permute-start.43
  351.1 2.0 collective-permute-start.44
  353.5 7.0 %collective-permute-done.43 = bf16[1,512,512]{2,1,0:T(8,128)(2,1)S(1)} collective-permute-done((bf16[1,512,512]{2,1,0:T(8,128)(2,1)S(1)}, bf16[1,512,512]{2,1,0:T(8,128)(2,1)S(1)}, u32[]{:S(2)}, u32[]{:S(2)}) %collective-permute-start.43) | collective-permute-done | bytes 524320 | tf_op jit(solution)/shard_map/ppermute | solution.py:545
  360.4 3.0 collective-permute-done.44
  364.7 2.0 collective-permute-start.51
  367.3 1.5 collective-permute-start.54
  371.9 1.4 collective-permute-start.64
  373.4 6.4 %collective-permute-done.53 = bf16[1,256,1152]{2,1,0:T(8,128)(2,1)S(1)} collective-permute-done((bf16[1,256,1152]{2,1,0:T(8,128)(2,1)S(1)}, bf16[1,256,1152]{2,1,0:T(8,128)(2,1)S(1)}, u32[]{:S(2)}, u32[]{:S(2)}) %collective-permute-start.53) | collective-permute-done | bytes 589856 | tf_op jit(solution)/shard_map/ppermute | solution.py:545
  380.3 1.4 collective-permute-start.57
  382.2 7.8 %collective-permute-start.55 = (f32[144,128]{1,0:T(8,128)S(1)}, f32[144,128]{1,0:T(8,128)S(1)}, u32[]{:S(2)}, u32[]{:S(2)}) collective-permute-start(f32[144,128]{1,0:T(8,128)S(1)} %add_add_fusion.1), channel_id=1, source_target_pairs={{0,2},{2,4},{4,6},{6,0},{1,3},{3,5},{5,7},{7,1},{8,10},{10,12},{12... | collective-permute-start | bytes 221192 | tf_op jit(solution)/shard_map/ppermute | solution.py:550
  390.8 12.7 %collective-permute-start.60 = (bf16[128,1152]{1,0:T(8,128)(2,1)}, bf16[128,1152]{1,0:T(8,128)(2,1)S(1)}, u32[]{:S(2)}, u32[]{:S(2)}) collective-permute-start(bf16[128,1152]{1,0:T(8,128)(2,1)} %get-tuple-element.243), channel_id=1, source_target_pairs={{0,6},{2,0},{4,2},{6,4},{1,7},{3,1},{5,3},{7,5},{8,14},{10,8},{12,... | collective-permute-start | bytes 884744 | tf_op jit(solution)/shard_map/ppermute | solution.py:550
  403.5 2.6 place.1
  408.0 1.4 reshape.657
  412.7 10.2 %collective-permute-done.59 = bf16[128,1152]{1,0:T(8,128)(2,1)S(1)} collective-permute-done((bf16[128,1152]{1,0:T(8,128)(2,1)S(1)}, bf16[128,1152]{1,0:T(8,128)(2,1)S(1)}, u32[]{:S(2)}, u32[]{:S(2)}) %collective-permute-start.59) | collective-permute-done | bytes 294944 | tf_op jit(solution)/shard_map/ppermute | solution.py:550
  (310 shorter events, 54.3 us)
Async XLA Ops:
  5.0 15.7 %collective-permute-start.2 = (bf16[256,2048]{1,0:T(8,128)(2,1)}, bf16[256,2048]{1,0:T(8,128)(2,1)}, u32[]{:S(2)}, u32[]{:S(2)}) collective-permute-start(bf16[256,2048]{1,0:T(8,128)(2,1)} %bitcast.8.refs_4_), channel_id=1, source_target_pairs={{0,1},{1,0},{2,3},{3,2},{4,5},{5,4},{6,7},{7,6},{8,9},{9,8},{10,11... | collective-permute-start | bytes 3145736 | tf_op jit(solution)/shard_map/ppermute | solution.py:540
  5.6 40.1 %collective-permute-start = (bf16[256,2048]{1,0:T(8,128)(2,1)S(1)}, bf16[256,2048]{1,0:T(8,128)(2,1)S(1)}, u32[]{:S(2)}, u32[]{:S(2)}) collective-permute-start(bf16[256,2048]{1,0:T(8,128)(2,1)S(1)} %fusion.17.near_ref), channel_id=1, source_target_pairs={{0,1},{1,0},{2,3},{3,2},{4,5},{5,4},{6,7},{7,6},{8,9},{9,8},{10,11... | collective-permute-start | bytes 3145736 | tf_op jit(solution)/shard_map/ppermute | solution.py:540
  5.7 35.4 %collective-permute-start.1 = (bf16[256,2048]{1,0:T(8,128)(2,1)}, bf16[256,2048]{1,0:T(8,128)(2,1)S(1)}, u32[]{:S(2)}, u32[]{:S(2)}) collective-permute-start(bf16[256,2048]{1,0:T(8,128)(2,1)} %bitcast.8.refs_4_), channel_id=1, source_target_pairs={{0,2},{2,4},{4,6},{6,0},{1,3},{3,5},{5,7},{7,1},{8,10},{10,12},{12... | collective-permute-start | bytes 3145736 | tf_op jit(solution)/shard_map/ppermute | solution.py:550
  8.7 28.1 %collective-permute-start.3 = (bf16[256,256]{1,0:T(8,128)(2,1)S(1)}, bf16[256,256]{1,0:T(8,128)(2,1)S(1)}, u32[]{:S(2)}, u32[]{:S(2)}) collective-permute-start(bf16[256,256]{1,0:T(8,128)(2,1)S(1)} %fusion.48), channel_id=1, source_target_pairs={{0,2},{2,4},{4,6},{1,3},{3,5},{5,7},{8,10},{10,12},{12,14},{9,11},... | collective-permute-start | bytes 393224 | tf_op jit(solution)/shard_map/ppermute | solution.py:555
  12.1 25.9 %collective-permute-start.4 = (bf16[256,256]{1,0:T(8,128)(2,1)S(1)}, bf16[256,256]{1,0:T(8,128)(2,1)}, u32[]{:S(2)}, u32[]{:S(2)}) collective-permute-start(bf16[256,256]{1,0:T(8,128)(2,1)S(1)} %fusion.48), channel_id=1, source_target_pairs={{0,4},{2,6},{1,5},{3,7},{8,12},{10,14},{9,13},{11,15},{16,20},{18,... | collective-permute-start | bytes 393224 | tf_op jit(solution)/shard_map/ppermute | solution.py:555
  20.7 19.3 %collective-permute-start.5 = (bf16[256,256]{1,0:T(8,128)(2,1)S(1)}, bf16[256,256]{1,0:T(8,128)(2,1)S(1)}, u32[]{:S(2)}, u32[]{:S(2)}) collective-permute-start(bf16[256,256]{1,0:T(8,128)(2,1)S(1)} %fusion.48), channel_id=1, source_target_pairs={{0,6},{1,7},{8,14},{9,15},{16,22},{17,23},{24,30},{25,31}} | collective-permute-start | bytes 393224 | tf_op jit(solution)/shard_map/ppermute | solution.py:555
  41.0 7.2 %collective-permute-start.6 = (bf16[4,256,256]{2,1,0:T(8,128)(2,1)S(1)}, bf16[4,256,256]{2,1,0:T(8,128)(2,1)S(1)}, u32[]{:S(2)}, u32[]{:S(2)}) collective-permute-start(bf16[4,256,256]{2,1,0:T(8,128)(2,1)S(1)} %pad_maximum_fusion.2.near_ref), channel_id=1, source_target_pairs={{0,1},{1,0},{2,3},{3,2},{4,5},{5,4},{6,7},{7,6},{8,9},{9,8},{10,11... | collective-permute-start | bytes 1572872 | tf_op jit(solution)/shard_map/ppermute | solution.py:540
  41.1 31.3 %collective-permute-start.7 = (bf16[256,2048]{1,0:T(8,128)(2,1)S(1)}, bf16[256,2048]{1,0:T(8,128)(2,1)S(1)}, u32[]{:S(2)}, u32[]{:S(2)}) collective-permute-start(bf16[256,2048]{1,0:T(8,128)(2,1)S(1)} %collective-permute-done.1.gnear_ref.refs_6_), channel_id=1, source_target_pairs={{0,2},{2,4},{4,6},{6,0},{1,3},{3,5},{5,7},{7,1},{8,10},{10,12},{12... | collective-permute-start | bytes 3145736 | tf_op jit(solution)/shard_map/ppermute | solution.py:550
  74.8 2.7 collective-permute-start.8
  79.4 2.7 collective-permute-start.9
  79.6 27.8 %collective-permute-start.10 = (bf16[256,2048]{1,0:T(8,128)(2,1)S(1)}, bf16[256,2048]{1,0:T(8,128)(2,1)S(1)}, u32[]{:S(2)}, u32[]{:S(2)}) collective-permute-start(bf16[256,2048]{1,0:T(8,128)(2,1)S(1)} %collective-permute-done.7.gnear_ref.refs_8_), channel_id=1, source_target_pairs={{0,2},{2,4},{4,6},{6,0},{1,3},{3,5},{5,7},{7,1},{8,10},{10,12},{12... | collective-permute-start | bytes 3145736 | tf_op jit(solution)/shard_map/ppermute | solution.py:550
  79.6 56.6 %collective-permute-start.12 = (bf16[256,2048]{1,0:T(8,128)(2,1)S(1)}, bf16[256,2048]{1,0:T(8,128)(2,1)S(1)}, u32[]{:S(2)}, u32[]{:S(2)}) collective-permute-start(bf16[256,2048]{1,0:T(8,128)(2,1)S(1)} %add_convert_fusion.1.near_ref.refs_4_), channel_id=1, source_target_pairs={{0,2},{2,4},{4,6},{6,0},{1,3},{3,5},{5,7},{7,1},{8,10},{10,12},{12... | collective-permute-start | bytes 3145736 | tf_op jit(solution)/shard_map/ppermute | solution.py:550
  122.1 13.7 %collective-permute-start.11 = (bf16[256,2048]{1,0:T(8,128)(2,1)S(1)}, bf16[256,2048]{1,0:T(8,128)(2,1)S(1)}, u32[]{:S(2)}, u32[]{:S(2)}) collective-permute-start(bf16[256,2048]{1,0:T(8,128)(2,1)S(1)} %slice.276), channel_id=1, source_target_pairs={{0,1},{1,0},{2,3},{3,2},{4,5},{5,4},{6,7},{7,6},{8,9},{9,8},{10,11... | collective-permute-start | bytes 3145736 | tf_op jit(solution)/shard_map/ppermute | solution.py:540
  136.3 3.5 collective-permute-start.13
  136.9 8.3 %collective-permute-start.16 = (bf16[256,2048]{1,0:T(8,128)(2,1)S(1)}, bf16[256,2048]{1,0:T(8,128)(2,1)}, u32[]{:S(2)}, u32[]{:S(2)}) collective-permute-start(bf16[256,2048]{1,0:T(8,128)(2,1)S(1)} %collective-permute-done.1.gnear_ref.refs_6_), channel_id=1, source_target_pairs={{0,1},{1,0},{2,3},{3,2},{4,5},{5,4},{6,7},{7,6},{8,9},{9,8},{10,11... | collective-permute-start | bytes 3145736 | tf_op jit(solution)/shard_map/ppermute | solution.py:540
  137.0 8.2 %collective-permute-start.15 = (bf16[256,2048]{1,0:T(8,128)(2,1)S(1)}, bf16[256,2048]{1,0:T(8,128)(2,1)S(1)}, u32[]{:S(2)}, u32[]{:S(2)}) collective-permute-start(bf16[256,2048]{1,0:T(8,128)(2,1)S(1)} %collective-permute-done.12.near_ref.refs_6_), channel_id=1, source_target_pairs={{0,1},{1,0},{2,3},{3,2},{4,5},{5,4},{6,7},{7,6},{8,9},{9,8},{10,11... | collective-permute-start | bytes 3145736 | tf_op jit(solution)/shard_map/ppermute | solution.py:540
  144.3 12.0 %collective-permute-start.14 = (bf16[256,2048]{1,0:T(8,128)(2,1)}, bf16[256,2048]{1,0:T(8,128)(2,1)}, u32[]{:S(2)}, u32[]{:S(2)}) collective-permute-start(bf16[256,2048]{1,0:T(8,128)(2,1)} %get-tuple-element.319.near_ref), channel_id=1, source_target_pairs={{0,1},{1,0},{2,3},{3,2},{4,5},{5,4},{6,7},{7,6},{8,9},{9,8},{10,11... | collective-permute-start | bytes 3145736 | tf_op jit(solution)/shard_map/ppermute | solution.py:540
  144.8 56.4 %collective-permute-start.26 = (bf16[256,2048]{1,0:T(8,128)(2,1)}, bf16[256,2048]{1,0:T(8,128)(2,1)}, u32[]{:S(2)}, u32[]{:S(2)}) collective-permute-start(bf16[256,2048]{1,0:T(8,128)(2,1)} %copy-done.6), channel_id=1, source_target_pairs={{0,1},{1,0},{2,3},{3,2},{4,5},{5,4},{6,7},{7,6},{8,9},{9,8},{10,11... | collective-permute-start | bytes 3145736 | tf_op jit(solution)/shard_map/ppermute | solution.py:540
  145.0 27.4 %collective-permute-start.17 = (bf16[256,2048]{1,0:T(8,128)(2,1)S(1)}, bf16[256,2048]{1,0:T(8,128)(2,1)S(1)}, u32[]{:S(2)}, u32[]{:S(2)}) collective-permute-start(bf16[256,2048]{1,0:T(8,128)(2,1)S(1)} %collective-permute-done.12.near_ref.refs_6_), channel_id=1, source_target_pairs={{0,2},{2,4},{4,6},{6,0},{1,3},{3,5},{5,7},{7,1},{8,10},{10,12},{12... | collective-permute-start | bytes 3145736 | tf_op jit(solution)/shard_map/ppermute | solution.py:550
  172.4 28.0 %collective-permute-start.18 = (bf16[256,2048]{1,0:T(8,128)(2,1)S(1)}, bf16[256,2048]{1,0:T(8,128)(2,1)S(1)}, u32[]{:S(2)}, u32[]{:S(2)}) collective-permute-start(bf16[256,2048]{1,0:T(8,128)(2,1)S(1)} %collective-permute-done.17.near_ref.refs_8_), channel_id=1, source_target_pairs={{0,2},{2,4},{4,6},{6,0},{1,3},{3,5},{5,7},{7,1},{8,10},{10,12},{12... | collective-permute-start | bytes 3145736 | tf_op jit(solution)/shard_map/ppermute | solution.py:550
  172.4 30.3 %collective-permute-start.25 = (bf16[256,2048]{1,0:T(8,128)(2,1)S(1)}, bf16[256,2048]{1,0:T(8,128)(2,1)S(1)}, u32[]{:S(2)}, u32[]{:S(2)}) collective-permute-start(bf16[256,2048]{1,0:T(8,128)(2,1)S(1)} %collective-permute-done.17.near_ref.refs_8_), channel_id=1, source_target_pairs={{0,1},{1,0},{2,3},{3,2},{4,5},{5,4},{6,7},{7,6},{8,9},{9,8},{10,11... | collective-permute-start | bytes 3145736 | tf_op jit(solution)/shard_map/ppermute | solution.py:540
  172.4 25.6 %collective-permute-start.20 = (bf16[2,1,256,1024]{3,2,1,0:T(8,128)(2,1)S(1)}, bf16[2,1,256,1024]{3,2,1,0:T(8,128)(2,1)S(1)}, u32[]{:S(2)}, u32[]{:S(2)}) collective-permute-start(bf16[2,1,256,1024]{3,2,1,0:T(8,128)(2,1)S(1)} %bitcast.235), channel_id=1, source_target_pairs={{0,16},{8,24},{16,0},{24,8},{1,17},{9,25},{17,1},{25,9},{2,18},{10... | collective-permute-start | bytes 3145736 | tf_op jit(solution)/shard_map/ppermute | solution.py:545
  174.0 25.2 %collective-permute-start.19 = (bf16[2,1,256,1024]{3,2,1,0:T(8,128)(2,1)S(1)}, bf16[2,1,256,1024]{3,2,1,0:T(8,128)(2,1)S(1)}, u32[]{:S(2)}, u32[]{:S(2)}) collective-permute-start(bf16[2,1,256,1024]{3,2,1,0:T(8,128)(2,1)S(1)} %bitcast.234), channel_id=1, source_target_pairs={{0,8},{8,0},{16,24},{24,16},{1,9},{9,1},{17,25},{25,17},{2,10},{10... | collective-permute-start | bytes 3145736 | tf_op jit(solution)/shard_map/ppermute | solution.py:545
  198.0 15.7 %collective-permute-start.22 = (bf16[256,2048]{1,0:T(8,128)(2,1)S(1)}, bf16[256,2048]{1,0:T(8,128)(2,1)S(1)}, u32[]{:S(2)}, u32[]{:S(2)}) collective-permute-start(bf16[256,2048]{1,0:T(8,128)(2,1)S(1)} %copy-done.10), channel_id=1, source_target_pairs={{0,1},{1,0},{2,3},{3,2},{4,5},{5,4},{6,7},{7,6},{8,9},{9,8},{10,11... | collective-permute-start | bytes 3145736 | tf_op jit(solution)/shard_map/ppermute | solution.py:540
  200.4 13.3 %collective-permute-start.21 = (bf16[256,2048]{1,0:T(8,128)(2,1)S(1)}, bf16[256,2048]{1,0:T(8,128)(2,1)S(1)}, u32[]{:S(2)}, u32[]{:S(2)}) collective-permute-start(bf16[256,2048]{1,0:T(8,128)(2,1)S(1)} %collective-permute-done.18.near_ref.refs_10_), channel_id=1, source_target_pairs={{0,1},{1,0},{2,3},{3,2},{4,5},{5,4},{6,7},{7,6},{8,9},{9,8},{10,11... | collective-permute-start | bytes 3145736 | tf_op jit(solution)/shard_map/ppermute | solution.py:540
  200.4 23.6 %collective-permute-start.23 = (bf16[1,256,1024]{2,1,0:T(8,128)(2,1)}, bf16[1,256,1024]{2,1,0:T(8,128)(2,1)S(1)}, u32[]{:S(2)}, u32[]{:S(2)}) collective-permute-start(bf16[1,256,1024]{2,1,0:T(8,128)(2,1)} %get-tuple-element.184), channel_id=1, source_target_pairs={{0,16},{8,24},{16,0},{24,8},{1,17},{9,25},{17,1},{25,9},{2,18},{10... | collective-permute-start | bytes 1572872 | tf_op jit(solution)/shard_map/ppermute | solution.py:545
  201.2 22.8 %collective-permute-start.24 = (bf16[1,256,1024]{2,1,0:T(8,128)(2,1)S(1)}, bf16[1,256,1024]{2,1,0:T(8,128)(2,1)S(1)}, u32[]{:S(2)}, u32[]{:S(2)}) collective-permute-start(bf16[1,256,1024]{2,1,0:T(8,128)(2,1)S(1)} %get-tuple-element.185), channel_id=1, source_target_pairs={{0,8},{8,0},{16,24},{24,16},{1,9},{9,1},{17,25},{25,17},{2,10},{10... | collective-permute-start | bytes 1572872 | tf_op jit(solution)/shard_map/ppermute | solution.py:545
  243.4 31.5 %collective-permute-start.28 = (bf16[2,1,512,512]{3,2,1,0:T(8,128)(2,1)}, bf16[2,1,512,512]{3,2,1,0:T(8,128)(2,1)}, u32[]{:S(2)}, u32[]{:S(2)}) collective-permute-start(bf16[2,1,512,512]{3,2,1,0:T(8,128)(2,1)} %bitcast.246), channel_id=1, source_target_pairs={{0,16},{8,24},{16,0},{24,8},{1,17},{9,25},{17,1},{25,9},{2,18},{10... | collective-permute-start | bytes 3145736 | tf_op jit(solution)/shard_map/ppermute | solution.py:545
  244.8 30.1 %collective-permute-start.27 = (bf16[2,1,512,512]{3,2,1,0:T(8,128)(2,1)}, bf16[2,1,512,512]{3,2,1,0:T(8,128)(2,1)}, u32[]{:S(2)}, u32[]{:S(2)}) collective-permute-start(bf16[2,1,512,512]{3,2,1,0:T(8,128)(2,1)} %bitcast.245), channel_id=1, source_target_pairs={{0,8},{8,0},{16,24},{24,16},{1,9},{9,1},{17,25},{25,17},{2,10},{10... | collective-permute-start | bytes 3145736 | tf_op jit(solution)/shard_map/ppermute | solution.py:545
  245.5 32.0 %collective-permute-start.29 = (bf16[128,1024]{1,0:T(8,128)(2,1)S(1)}, bf16[128,1024]{1,0:T(8,128)(2,1)}, u32[]{:S(2)}, u32[]{:S(2)}) collective-permute-start(bf16[128,1024]{1,0:T(8,128)(2,1)S(1)} %get-tuple-element.350), channel_id=1, source_target_pairs={{0,2},{2,4},{4,6},{6,0},{1,3},{3,5},{5,7},{7,1},{8,10},{10,12},{12... | collective-permute-start | bytes 786440 | tf_op jit(solution)/shard_map/ppermute | solution.py:550
  245.6 31.9 %collective-permute-start.30 = (bf16[128,1024]{1,0:T(8,128)(2,1)S(1)}, bf16[128,1024]{1,0:T(8,128)(2,1)}, u32[]{:S(2)}, u32[]{:S(2)}) collective-permute-start(bf16[128,1024]{1,0:T(8,128)(2,1)S(1)} %get-tuple-element.349), channel_id=1, source_target_pairs={{0,4},{2,6},{4,0},{6,2},{1,5},{3,7},{5,1},{7,3},{8,12},{10,14},{12... | collective-permute-start | bytes 786440 | tf_op jit(solution)/shard_map/ppermute | solution.py:550
  256.8 20.7 %collective-permute-start.31 = (bf16[128,1024]{1,0:T(8,128)(2,1)S(1)}, bf16[128,1024]{1,0:T(8,128)(2,1)}, u32[]{:S(2)}, u32[]{:S(2)}) collective-permute-start(bf16[128,1024]{1,0:T(8,128)(2,1)S(1)} %get-tuple-element.348), channel_id=1, source_target_pairs={{0,6},{2,0},{4,2},{6,4},{1,7},{3,1},{5,3},{7,5},{8,14},{10,8},{12,... | collective-permute-start | bytes 786440 | tf_op jit(solution)/shard_map/ppermute | solution.py:550
  278.4 4.3 %collective-permute-start.32 = (bf16[4,2,256,128]{3,2,1,0:T(8,128)(2,1)}, bf16[4,2,256,128]{3,2,1,0:T(8,128)(2,1)S(1)}, u32[]{:S(2)}, u32[]{:S(2)}) collective-permute-start(bf16[4,2,256,128]{3,2,1,0:T(8,128)(2,1)} %dynamic-slice_bitcast_fusion), channel_id=1, source_target_pairs={{0,1},{1,0},{2,3},{3,2},{4,5},{5,4},{6,7},{7,6},{8,9},{9,8},{10,11... | collective-permute-start | bytes 1572872 | tf_op jit(solution)/shard_map/ppermute | solution.py:540
  279.2 25.0 %collective-permute-start.36 = (bf16[1,512,512]{2,1,0:T(8,128)(2,1)}, bf16[1,512,512]{2,1,0:T(8,128)(2,1)}, u32[]{:S(2)}, u32[]{:S(2)}) collective-permute-start(bf16[1,512,512]{2,1,0:T(8,128)(2,1)} %get-tuple-element.210), channel_id=1, source_target_pairs={{0,16},{8,24},{16,0},{24,8},{1,17},{9,25},{17,1},{25,9},{2,18},{10... | collective-permute-start | bytes 1572872 | tf_op jit(solution)/shard_map/ppermute | solution.py:545
  279.6 24.6 %collective-permute-start.37 = (bf16[1,512,512]{2,1,0:T(8,128)(2,1)}, bf16[1,512,512]{2,1,0:T(8,128)(2,1)}, u32[]{:S(2)}, u32[]{:S(2)}) collective-permute-start(bf16[1,512,512]{2,1,0:T(8,128)(2,1)} %get-tuple-element.211), channel_id=1, source_target_pairs={{0,8},{8,0},{16,24},{24,16},{1,9},{9,1},{17,25},{25,17},{2,10},{10... | collective-permute-start | bytes 1572872 | tf_op jit(solution)/shard_map/ppermute | solution.py:545
  282.8 10.7 %collective-permute-start.35 = (bf16[512,128]{1,0:T(8,128)(2,1)S(1)}, bf16[512,128]{1,0:T(8,128)(2,1)S(1)}, u32[]{:S(2)}, u32[]{:S(2)}) collective-permute-start(bf16[512,128]{1,0:T(8,128)(2,1)S(1)} %bitcast.240), channel_id=1, source_target_pairs={{6,0},{7,1},{14,8},{15,9},{22,16},{23,17},{30,24},{31,25}} | collective-permute-start | bytes 393224 | tf_op jit(solution)/shard_map/ppermute | solution.py:560
  284.1 14.3 %collective-permute-start.34 = (bf16[512,128]{1,0:T(8,128)(2,1)S(1)}, bf16[512,128]{1,0:T(8,128)(2,1)S(1)}, u32[]{:S(2)}, u32[]{:S(2)}) collective-permute-start(bf16[512,128]{1,0:T(8,128)(2,1)S(1)} %bitcast.239), channel_id=1, source_target_pairs={{4,0},{6,2},{5,1},{7,3},{12,8},{14,10},{13,9},{15,11},{20,16},{22,... | collective-permute-start | bytes 393224 | tf_op jit(solution)/shard_map/ppermute | solution.py:560
  285.4 13.6 %collective-permute-start.33 = (bf16[512,128]{1,0:T(8,128)(2,1)S(1)}, bf16[512,128]{1,0:T(8,128)(2,1)S(1)}, u32[]{:S(2)}, u32[]{:S(2)}) collective-permute-start(bf16[512,128]{1,0:T(8,128)(2,1)S(1)} %bitcast.238), channel_id=1, source_target_pairs={{2,0},{4,2},{6,4},{3,1},{5,3},{7,5},{10,8},{12,10},{14,12},{11,9},... | collective-permute-start | bytes 393224 | tf_op jit(solution)/shard_map/ppermute | solution.py:560
  293.6 26.6 %collective-permute-start.42 = (bf16[2,1,512,512]{3,2,1,0:T(8,128)(2,1)}, bf16[2,1,512,512]{3,2,1,0:T(8,128)(2,1)S(1)}, u32[]{:S(2)}, u32[]{:S(2)}) collective-permute-start(bf16[2,1,512,512]{3,2,1,0:T(8,128)(2,1)} %bitcast.54), channel_id=1, source_target_pairs={{0,16},{8,24},{16,0},{24,8},{1,17},{9,25},{17,1},{25,9},{2,18},{10... | collective-permute-start | bytes 3145736 | tf_op jit(solution)/shard_map/ppermute | solution.py:545
  298.5 24.4 %collective-permute-start.41 = (bf16[2,1,512,512]{3,2,1,0:T(8,128)(2,1)}, bf16[2,1,512,512]{3,2,1,0:T(8,128)(2,1)S(1)}, u32[]{:S(2)}, u32[]{:S(2)}) collective-permute-start(bf16[2,1,512,512]{3,2,1,0:T(8,128)(2,1)} %bitcast.52), channel_id=1, source_target_pairs={{0,8},{8,0},{16,24},{24,16},{1,9},{9,1},{17,25},{25,17},{2,10},{10... | collective-permute-start | bytes 3145736 | tf_op jit(solution)/shard_map/ppermute | solution.py:545
  304.4 21.9 %collective-permute-start.38 = (bf16[256,2048]{1,0:T(8,128)(2,1)S(1)}, bf16[256,2048]{1,0:T(8,128)(2,1)S(1)}, u32[]{:S(2)}, u32[]{:S(2)}) collective-permute-start(bf16[256,2048]{1,0:T(8,128)(2,1)S(1)} %slice.240), channel_id=1, source_target_pairs={{0,1},{1,0},{2,3},{3,2},{4,5},{5,4},{6,7},{7,6},{8,9},{9,8},{10,11... | collective-permute-start | bytes 3145736 | tf_op jit(solution)/shard_map/ppermute | solution.py:540
  304.5 15.6 %collective-permute-start.40 = (f32[1,128]{1,0:T(1,128)S(1)}, f32[1,128]{1,0:T(1,128)S(1)}, u32[]{:S(2)}, u32[]{:S(2)}) collective-permute-start(f32[1,128]{1,0:T(1,128)S(1)} %fusion.87), channel_id=1, source_target_pairs={{0,1},{1,0},{2,3},{3,2},{4,5},{5,4},{6,7},{7,6},{8,9},{9,8},{10,11... | collective-permute-start | bytes 1544 | tf_op jit(solution)/shard_map/ppermute | solution.py:540
  309.5 43.9 %collective-permute-start.47 = (bf16[1,1024,128]{2,1,0:T(8,128)(2,1)}, bf16[1,1024,128]{2,1,0:T(8,128)(2,1)S(1)}, u32[]{:S(2)}, u32[]{:S(2)}) collective-permute-start(bf16[1,1024,128]{2,1,0:T(8,128)(2,1)} %get-tuple-element.231), channel_id=1, source_target_pairs={{0,2},{2,4},{4,6},{6,0},{1,3},{3,5},{5,7},{7,1},{8,10},{10,12},{12... | collective-permute-start | bytes 786440 | tf_op jit(solution)/shard_map/ppermute | solution.py:550
  320.1 33.3 %collective-permute-start.48 = (bf16[1,1024,128]{2,1,0:T(8,128)(2,1)}, bf16[1,1024,128]{2,1,0:T(8,128)(2,1)S(1)}, u32[]{:S(2)}, u32[]{:S(2)}) collective-permute-start(bf16[1,1024,128]{2,1,0:T(8,128)(2,1)} %get-tuple-element.232), channel_id=1, source_target_pairs={{0,4},{2,6},{4,0},{6,2},{1,5},{3,7},{5,1},{7,3},{8,12},{10,14},{12... | collective-permute-start | bytes 786440 | tf_op jit(solution)/shard_map/ppermute | solution.py:550
  323.1 26.2 %collective-permute-start.46 = (bf16[2,1,256,1152]{3,2,1,0:T(8,128)(2,1)S(1)}, bf16[2,1,256,1152]{3,2,1,0:T(8,128)(2,1)S(1)}, u32[]{:S(2)}, u32[]{:S(2)}) collective-permute-start(bf16[2,1,256,1152]{3,2,1,0:T(8,128)(2,1)S(1)} %bitcast.233), channel_id=1, source_target_pairs={{0,16},{8,24},{16,0},{24,8},{1,17},{9,25},{17,1},{25,9},{2,18},{10... | collective-permute-start | bytes 3538952 | tf_op jit(solution)/shard_map/ppermute | solution.py:545
  324.8 26.3 %collective-permute-start.45 = (bf16[2,1,256,1152]{3,2,1,0:T(8,128)(2,1)S(1)}, bf16[2,1,256,1152]{3,2,1,0:T(8,128)(2,1)S(1)}, u32[]{:S(2)}, u32[]{:S(2)}) collective-permute-start(bf16[2,1,256,1152]{3,2,1,0:T(8,128)(2,1)S(1)} %bitcast.232), channel_id=1, source_target_pairs={{0,8},{8,0},{16,24},{24,16},{1,9},{9,1},{17,25},{25,17},{2,10},{10... | collective-permute-start | bytes 3538952 | tf_op jit(solution)/shard_map/ppermute | solution.py:545
  329.6 23.9 %collective-permute-start.49 = (bf16[1,1024,128]{2,1,0:T(8,128)(2,1)S(1)}, bf16[1,1024,128]{2,1,0:T(8,128)(2,1)S(1)}, u32[]{:S(2)}, u32[]{:S(2)}) collective-permute-start(bf16[1,1024,128]{2,1,0:T(8,128)(2,1)S(1)} %get-tuple-element.233), channel_id=1, source_target_pairs={{0,6},{2,0},{4,2},{6,4},{1,7},{3,1},{5,3},{7,5},{8,14},{10,8},{12,... | collective-permute-start | bytes 786440 | tf_op jit(solution)/shard_map/ppermute | solution.py:550
  349.3 11.1 %collective-permute-start.43 = (bf16[1,512,512]{2,1,0:T(8,128)(2,1)S(1)}, bf16[1,512,512]{2,1,0:T(8,128)(2,1)S(1)}, u32[]{:S(2)}, u32[]{:S(2)}) collective-permute-start(bf16[1,512,512]{2,1,0:T(8,128)(2,1)S(1)} %get-tuple-element.225), channel_id=1, source_target_pairs={{0,16},{8,24},{16,0},{24,8},{1,17},{9,25},{17,1},{25,9},{2,18},{10... | collective-permute-start | bytes 1572872 | tf_op jit(solution)/shard_map/ppermute | solution.py:545
  351.1 12.3 %collective-permute-start.44 = (bf16[1,512,512]{2,1,0:T(8,128)(2,1)S(1)}, bf16[1,512,512]{2,1,0:T(8,128)(2,1)S(1)}, u32[]{:S(2)}, u32[]{:S(2)}) collective-permute-start(bf16[1,512,512]{2,1,0:T(8,128)(2,1)S(1)} %get-tuple-element.226), channel_id=1, source_target_pairs={{0,8},{8,0},{16,24},{24,16},{1,9},{9,1},{17,25},{25,17},{2,10},{10... | collective-permute-start | bytes 1572872 | tf_op jit(solution)/shard_map/ppermute | solution.py:545
  363.4 6.1 %collective-permute-start.52 = (f32[144,128]{1,0:T(8,128)S(1)}, f32[144,128]{1,0:T(8,128)S(1)}, u32[]{:S(2)}, u32[]{:S(2)}) collective-permute-start(f32[144,128]{1,0:T(8,128)S(1)} %pad_maximum_fusion.3), channel_id=1, source_target_pairs={{0,24},{8,16},{16,8},{24,0},{1,25},{9,17},{17,9},{25,1},{2,26},{10... | collective-permute-start | bytes 221192 | tf_op jit(solution)/shard_map/ppermute | solution.py:545
  364.7 5.8 %collective-permute-start.51 = (f32[144,128]{1,0:T(8,128)S(1)}, f32[144,128]{1,0:T(8,128)S(1)}, u32[]{:S(2)}, u32[]{:S(2)}) collective-permute-start(f32[144,128]{1,0:T(8,128)S(1)} %pad_maximum_fusion.3), channel_id=1, source_target_pairs={{0,16},{8,24},{16,0},{24,8},{1,17},{9,25},{17,1},{25,9},{2,18},{10... | collective-permute-start | bytes 221192 | tf_op jit(solution)/shard_map/ppermute | solution.py:545
  366.7 5.2 %collective-permute-start.50 = (f32[144,128]{1,0:T(8,128)S(1)}, f32[144,128]{1,0:T(8,128)S(1)}, u32[]{:S(2)}, u32[]{:S(2)}) collective-permute-start(f32[144,128]{1,0:T(8,128)S(1)} %pad_maximum_fusion.3), channel_id=1, source_target_pairs={{0,8},{8,0},{16,24},{24,16},{1,9},{9,1},{17,25},{25,17},{2,10},{10... | collective-permute-start | bytes 221192 | tf_op jit(solution)/shard_map/ppermute | solution.py:545
  366.9 12.9 %collective-permute-start.53 = (bf16[1,256,1152]{2,1,0:T(8,128)(2,1)S(1)}, bf16[1,256,1152]{2,1,0:T(8,128)(2,1)S(1)}, u32[]{:S(2)}, u32[]{:S(2)}) collective-permute-start(bf16[1,256,1152]{2,1,0:T(8,128)(2,1)S(1)} %get-tuple-element.235), channel_id=1, source_target_pairs={{0,16},{8,24},{16,0},{24,8},{1,17},{9,25},{17,1},{25,9},{2,18},{10... | collective-permute-start | bytes 1769480 | tf_op jit(solution)/shard_map/ppermute | solution.py:545
  367.3 13.0 %collective-permute-start.54 = (bf16[1,256,1152]{2,1,0:T(8,128)(2,1)S(1)}, bf16[1,256,1152]{2,1,0:T(8,128)(2,1)S(1)}, u32[]{:S(2)}, u32[]{:S(2)}) collective-permute-start(bf16[1,256,1152]{2,1,0:T(8,128)(2,1)S(1)} %get-tuple-element.236), channel_id=1, source_target_pairs={{0,8},{8,0},{16,24},{24,16},{1,9},{9,1},{17,25},{25,17},{2,10},{10... | collective-permute-start | bytes 1769480 | tf_op jit(solution)/shard_map/ppermute | solution.py:545
  369.5 12.8 %collective-permute-start.62 = (bf16[1,1024,128]{2,1,0:T(8,128)(2,1)S(1)}, bf16[1,1024,128]{2,1,0:T(8,128)(2,1)S(1)}, u32[]{:S(2)}, u32[]{:S(2)}) collective-permute-start(bf16[1,1024,128]{2,1,0:T(8,128)(2,1)S(1)} %get-tuple-element.335), channel_id=1, source_target_pairs={{0,2},{2,4},{4,6},{6,0},{1,3},{3,5},{5,7},{7,1},{8,10},{10,12},{12... | collective-permute-start | bytes 786440 | tf_op jit(solution)/shard_map/ppermute | solution.py:550
  370.5 20.3 %collective-permute-start.63 = (bf16[1,1024,128]{2,1,0:T(8,128)(2,1)S(1)}, bf16[1,1024,128]{2,1,0:T(8,128)(2,1)S(1)}, u32[]{:S(2)}, u32[]{:S(2)}) collective-permute-start(bf16[1,1024,128]{2,1,0:T(8,128)(2,1)S(1)} %get-tuple-element.336), channel_id=1, source_target_pairs={{0,4},{2,6},{4,0},{6,2},{1,5},{3,7},{5,1},{7,3},{8,12},{10,14},{12... | collective-permute-start | bytes 786440 | tf_op jit(solution)/shard_map/ppermute | solution.py:550
  371.9 31.6 %collective-permute-start.64 = (bf16[1,1024,128]{2,1,0:T(8,128)(2,1)S(1)}, bf16[1,1024,128]{2,1,0:T(8,128)(2,1)S(1)}, u32[]{:S(2)}, u32[]{:S(2)}) collective-permute-start(bf16[1,1024,128]{2,1,0:T(8,128)(2,1)S(1)} %get-tuple-element.333), channel_id=1, source_target_pairs={{0,6},{2,0},{4,2},{6,4},{1,7},{3,1},{5,3},{7,5},{8,14},{10,8},{12,... | collective-permute-start | bytes 786440 | tf_op jit(solution)/shard_map/ppermute | solution.py:550
  380.3 25.8 %collective-permute-start.57 = (f32[144,128]{1,0:T(8,128)S(1)}, f32[144,128]{1,0:T(8,128)S(1)}, u32[]{:S(2)}, u32[]{:S(2)}) collective-permute-start(f32[144,128]{1,0:T(8,128)S(1)} %add_add_fusion.1), channel_id=1, source_target_pairs={{0,6},{2,0},{4,2},{6,4},{1,7},{3,1},{5,3},{7,5},{8,14},{10,8},{12,... | collective-permute-start | bytes 221192 | tf_op jit(solution)/shard_map/ppermute | solution.py:550
  381.7 25.0 %collective-permute-start.56 = (f32[144,128]{1,0:T(8,128)S(1)}, f32[144,128]{1,0:T(8,128)S(1)}, u32[]{:S(2)}, u32[]{:S(2)}) collective-permute-start(f32[144,128]{1,0:T(8,128)S(1)} %add_add_fusion.1), channel_id=1, source_target_pairs={{0,4},{2,6},{4,0},{6,2},{1,5},{3,7},{5,1},{7,3},{8,12},{10,14},{12... | collective-permute-start | bytes 221192 | tf_op jit(solution)/shard_map/ppermute | solution.py:550
  382.2 24.4 %collective-permute-start.55 = (f32[144,128]{1,0:T(8,128)S(1)}, f32[144,128]{1,0:T(8,128)S(1)}, u32[]{:S(2)}, u32[]{:S(2)}) collective-permute-start(f32[144,128]{1,0:T(8,128)S(1)} %add_add_fusion.1), channel_id=1, source_target_pairs={{0,2},{2,4},{4,6},{6,0},{1,3},{3,5},{5,7},{7,1},{8,10},{10,12},{12... | collective-permute-start | bytes 221192 | tf_op jit(solution)/shard_map/ppermute | solution.py:550
  390.8 21.9 %collective-permute-start.60 = (bf16[128,1152]{1,0:T(8,128)(2,1)}, bf16[128,1152]{1,0:T(8,128)(2,1)S(1)}, u32[]{:S(2)}, u32[]{:S(2)}) collective-permute-start(bf16[128,1152]{1,0:T(8,128)(2,1)} %get-tuple-element.243), channel_id=1, source_target_pairs={{0,6},{2,0},{4,2},{6,4},{1,7},{3,1},{5,3},{7,5},{8,14},{10,8},{12,... | collective-permute-start | bytes 884744 | tf_op jit(solution)/shard_map/ppermute | solution.py:550
  403.5 19.4 %collective-permute-start.59 = (bf16[128,1152]{1,0:T(8,128)(2,1)S(1)}, bf16[128,1152]{1,0:T(8,128)(2,1)S(1)}, u32[]{:S(2)}, u32[]{:S(2)}) collective-permute-start(bf16[128,1152]{1,0:T(8,128)(2,1)S(1)} %get-tuple-element.242), channel_id=1, source_target_pairs={{0,4},{2,6},{4,0},{6,2},{1,5},{3,7},{5,1},{7,3},{8,12},{10,14},{12... | collective-permute-start | bytes 884744 | tf_op jit(solution)/shard_map/ppermute | solution.py:550
  406.2 16.7 %collective-permute-start.58 = (bf16[128,1152]{1,0:T(8,128)(2,1)S(1)}, bf16[128,1152]{1,0:T(8,128)(2,1)}, u32[]{:S(2)}, u32[]{:S(2)}) collective-permute-start(bf16[128,1152]{1,0:T(8,128)(2,1)S(1)} %get-tuple-element.241), channel_id=1, source_target_pairs={{0,2},{2,4},{4,6},{6,0},{1,3},{3,5},{5,7},{7,1},{8,10},{10,12},{12... | collective-permute-start | bytes 884744 | tf_op jit(solution)/shard_map/ppermute | solution.py:550
  424.1 2.9 collective-permute-start.61
  (70 other events, 753.9 us)

commit v4 on v3

--- a/solution.py
+++ b/solution.py
@@ -414,35 +414,63 @@
 
 def hidden_kernel(lefts, at, *refs):
     left_refs, right_refs = refs[:lefts], refs[lefts:-6]
-    outs, (left_place, right_place) = refs[-6:-2], refs[-2:]
-    left = joined(left_refs, left_place)
-    right = joined(right_refs, right_place)
-    store_turn(pl.program_id(0), contract_rows(left, right), outs)
+    (send_x, send_y, kept, own), (left_place, right_place) = refs[-6:-2], refs[-2:]
+    step = pl.program_id(0)
+
+    @pl.when(step == 0)
+    def _():
+        start = 0
+        for item in left_refs:
+            left_place[start : start + item.shape[0]] = item[...]
+            start += item.shape[0]
+
+    result = contract_rows(left_place[...], joined(right_refs, right_place)).astype(low)
+    half = result.shape[0] // 2
+    first, second = result[:half], result[half:]
+
+    @pl.when(step == 0)
+    def _():
+        send_x[0] = first
+        send_y[0] = second
+
+    @pl.when(step == 1)
+    def _():
+        send_x[0] = first
+        kept[0] = second
+
+    @pl.when(step == 2)
+    def _():
+        kept[0] = first
+        send_y[0] = second
+
+    @pl.when(step == 3)
+    def _():
+        own[0] = first
+        own[1] = second
 
 
 def hidden_weights(at, lefts, pieces, units, part, name):
-    total = len(turns)
     span = lefts[0].shape[0]
     rows = span // 2
     half = units // 2
     depth = len(lefts) * span
 
     def left_of(own):
-        def place(i, s):
-            return (0, s[2 * total] * 2 + s[total + i] if own else s[total + i])
-
-        return pl.BlockSpec((span, half), place)
-
-    def out_of(index):
-        return pl.BlockSpec((1, half, part), lambda i, s: (jnp.clip(i - 2 * index, 0, 1), 0, 0))
-
+        return pl.BlockSpec((span, units), lambda i, s: (0, s[4] if own else 0))
+
+    thin = (1, half, part)
     spec = pltpu.PrefetchScalarGridSpec(
         num_scalar_prefetch=1,
-        grid=(total,),
+        grid=(4,),
         in_specs=[left_of(n == 0) for n in range(len(lefts))]
         + [pl.BlockSpec((rows, part), lambda i, s: (0, s[i])) for _ in pieces],
-        out_specs=[out_of(index) for index in range(4)],
-        scratch_shapes=[pltpu.VMEM((depth, half), low), pltpu.VMEM((depth, part), low)],
+        out_specs=[
+            pl.BlockSpec(thin, lambda i, s: (jnp.clip(i, 0, 1), 0, 0)),
+            pl.BlockSpec(thin, lambda i, s: (i // 2, 0, 0)),
+            pl.BlockSpec(thin, lambda i, s: (i // 2, 0, 0)),
+            pl.BlockSpec((2, half, part), lambda i, s: (0, 0, 0)),
+        ],
+        scratch_shapes=[pltpu.VMEM((depth, units), low), pltpu.VMEM((depth, part), low)],
     )
     return pl.pallas_call(
         functools.partial(hidden_kernel, len(lefts)),
@@ -450,7 +478,7 @@
         out_shape=tuple(jax.ShapeDtypeStruct((2, half, part), low) for _ in range(4)),
         compiler_params=pltpu.CompilerParams(vmem_limit_bytes=60 * 1024 * 1024),
         cost_estimate=pl.CostEstimate(
-            flops=2 * total * depth * half * part,
+            flops=8 * depth * units * part,
             bytes_accessed=4 * depth * (units + 4 * part),
             transcendentals=0,
         ),
@@ -768,8 +796,9 @@
         shared_part(step)
     acts[-1], *last_out = after(acts[-1], *last_out)
     sum_out = dp_join(*first_out[2:], *last_out)[0]
+    hidden_at = jnp.stack([at_dp ^ 3, at_dp ^ 1, at_dp ^ 2, at_dp, at_seq]).astype(jnp.int32)
     downs = hidden_weights(
-        table,
+        hidden_at,
         acts,
         [item for couple in zip(grad_held, grad_far) for item in couple],
         hidden_part,
@@ -781,7 +810,7 @@
     narrow = sum_out.astype(low)
     out_parts = [shift(to_seq(narrow, by, 0), by) for by in range(1, seqs)]
     ups = hidden_weights(
-        table,
+        hidden_at,
         grads,
         [item for couple in zip(held, held_far) for item in couple],
         hidden_part,

time: 434 us -> 430 us (level)
    ppermute x21, waiting for transfers between devices: 36.1 us -> 42.6 us  [shift(): lax.ppermute(item, 'seq', [(i, (i + by) % size) for i in range(size)])]
    ppermute x19, waiting for transfers between devices: 55.1 us -> 49.3 us  [cross(): return lax.ppermute(item, 'dp', [(i, i ^ bits) for i in range(size)])]
  transfers between devices with their start and end apart: 65 -> 65, of which waited for: 23 -> 19; matrix products, arithmetic and copies ran while one was open for 21% -> 21% of each run, Pallas kernels for 23% -> 24%
where the time goes in v4:
time: 430 us; the launch traced here: 424 us
  Pallas kernels  116 us (27%)
  waiting for transfers between devices  111 us (26%)
  starting transfers between devices  83.7 us (19%)
  matrix products  56.3 us (13%)
  other arithmetic  31 us (7%)
  local copies, waits for them, and re-layouts  20 us (5%)
  between operations  5.54 us (1%)
    ppermute x19, waiting for transfers between devices, cross(): return lax.ppermute(item, 'dp', [(i, i ^ bits) for i in range(size)])  49.3 us
    ppermute x21, starting transfers between devices, shift(): lax.ppermute(item, 'seq', [(i, (i + by) % size) for i in range(size)])  45.3 us
    ppermute x21, waiting for transfers between devices, shift(): lax.ppermute(item, 'seq', [(i, (i + by) % size) for i in range(size)])  42.6 us
    dot_general x4, matrix products, contract_cols(): lax.dot_general(left, right, (((1,), (1,)), ((), ())), preferred_element_...  37.5 us
    pallas_call x2, Pallas kernels, hidden_weights(): pl.pallas_call(functools.partial(hidden_kernel, len(lefts)), grid_spec=sp...  32.3 us
    pallas_call x3, Pallas kernels, share(): pl.pallas_call(share_kernel, grid_spec=spec, out_shape=(shape, shape), co...  28.2 us
    ppermute x19, starting transfers between devices, cross(): return lax.ppermute(item, 'dp', [(i, i ^ bits) for i in range(size)])  22.5 us
    pallas_call x1, Pallas kernels, up(): pl.pallas_call(up_kernel, grid=(units // tile,), in_specs=[row, row, pl.B...  19.6 us
  transfers between devices with their start and end apart: 65, of which 19 were waited for; matrix products, arithmetic and copies ran while one was open for 21% of the time, Pallas kernels for 24%

profile of v4, /device:TPU:0, one launch (start us, length us, event | category | flops | bytes accessed | tf_op | source)
XLA Modules:
  0.0 423.8 jit_solution(14073072760251800216)
XLA Ops:
  0.7 1.6 convert_reduce_fusion.1
  2.3 1.6 fusion.24
  5.7 3.0 collective-permute-start.1
  8.6 3.5 collective-permute-start.3
  12.1 3.6 collective-permute-start.4
  20.7 1.6 collective-permute-start.5
  22.3 14.4 %convolution_convert_fusion.g_ref = bf16[512,4096]{1,0:T(8,128)(2,1)} fusion(bf16[4096,2048]{1,0:T(8,128)(2,1)} %down_ref.5, bf16[256,2048]{1,0:T(8,128)(2,1)} %collective-permute-done.2.refs_5_, bf16[256,2048]{1,0:T(8,128)(2,1)} %bitcast.8.refs_4_), kind=kOutput, calls=%fused_computation | convolution fusion | flops 8596226048 | bytes 23068672 | tf_op jit(solution)/shard_map/dot_general | solution.py:27
  38.1 1.9 collective-permute-done.5
  41.1 4.7 %collective-permute-start.7 = (bf16[256,2048]{1,0:T(8,128)(2,1)S(1)}, bf16[256,2048]{1,0:T(8,128)(2,1)S(1)}, u32[]{:S(2)}, u32[]{:S(2)}) collective-permute-start(bf16[256,2048]{1,0:T(8,128)(2,1)S(1)} %collective-permute-done.1.gnear_ref.refs_6_), channel_id=1, source_target_pairs={{0,2},{2,4},{4,6},{6,0},{1,3},{3,5},{5,7},{7,1},{8,10},{10,12},{12... | collective-permute-start | bytes 3145736 | tf_op jit(solution)/shard_map/ppermute | solution.py:578
  45.8 2.4 add_convert_fusion.2.q_ref
  48.3 7.0 %attend.1 = (bf16[512,1024]{1,0:T(8,128)(2,1)S(1)}, f32[8,512]{1,0:T(8,128)S(1)}) custom-call(s32[4]{0:T(128)S(1)} %pad_add_fusion.info, bf16[512,1024]{1,0:T(8,128)(2,1)S(1)} %add_convert_fusion.2.q_ref, bf16[4,256,256]{2,1,0:T(8,128)(2,1)S(1)} %pad_maximum_fusion.2.near_ref, bf16[4,256,256]{2,1,0:T(8,128)(2,1)S(1)} %collective-permute-done.6.far_ref, ...), custom_call_target="tpu_custom_call" | custom-call | flops 8589934592 | bytes 2097152 | tf_op jit(solution)/shard_map/attend/pallas_call | solution.py:223
  55.3 17.1 %collective-permute-done.7.gnear_ref.refs_8_ = bf16[256,2048]{1,0:T(8,128)(2,1)S(1)} collective-permute-done((bf16[256,2048]{1,0:T(8,128)(2,1)S(1)}, bf16[256,2048]{1,0:T(8,128)(2,1)S(1)}, u32[]{:S(2)}, u32[]{:S(2)}) %collective-permute-start.7) | collective-permute-done | bytes 1048608 | tf_op jit(solution)/shard_map/ppermute | solution.py:578
  72.4 2.3 convolution_convert_fusion.1
  75.0 2.6 collective-permute-done.8
  80.7 1.5 collective-permute-done.9.far_ref.refs_5_
  82.2 19.6 %up.1 = (bf16[512,4096]{1,0:T(8,128)(2,1)}, bf16[512,4096]{1,0:T(8,128)(2,1)}, f32[1,4096]{1,0:T(1,128)S(1)}) custom-call(bf16[256,2048]{1,0:T(8,128)(2,1)S(1)} %add_convert_fusion.1.near_ref.refs_4_, bf16[256,2048]{1,0:T(8,128)(2,1)S(1)} %collective-permute-done.9.far_ref.refs_5_, bf16[2048,4096]{1,0:T(8,128)(2,1)} %up_ref.5, f32[1,4096]{1,0:T(1,128)S(1)} %bitcast.227, ...), custom_call_target="tpu_custom_call" | custom-call | flops 8589934592 | bytes 33554432 | tf_op jit(solution)/shard_map/up/pallas_call | solution.py:319
  101.8 5.8 %collective-permute-done.10.gnear_ref.refs_10_ = bf16[256,2048]{1,0:T(8,128)(2,1)} collective-permute-done((bf16[256,2048]{1,0:T(8,128)(2,1)S(1)}, bf16[256,2048]{1,0:T(8,128)(2,1)}, u32[]{:S(2)}, u32[]{:S(2)}) %collective-permute-start.10) | collective-permute-done | bytes 1048608 | tf_op jit(solution)/shard_map/ppermute | solution.py:578
  107.6 13.7 %convolution_convert_fusion.3 = bf16[512,2048]{1,0:T(8,128)(2,1)S(1)} fusion(bf16[512,4096]{1,0:T(8,128)(2,1)} %get-tuple-element.199.refs_0_, bf16[2048,4096]{1,0:T(8,128)(2,1)} %up_ref.5), kind=kOutput, calls=%fused_computation.8 | convolution fusion | flops 8590983168 | bytes 23068672 | tf_op jit(solution)/shard_map/dot_general | solution.py:27
  121.4 13.6 %convolution_convert_fusion.2 = bf16[512,2048]{1,0:T(8,128)(2,1)S(1)} fusion(bf16[512,4096]{1,0:T(8,128)(2,1)} %get-tuple-element.160.refs_0_, bf16[4096,2048]{1,0:T(8,128)(2,1)} %down_ref.5), kind=kOutput, calls=%fused_computation.7 | convolution fusion | flops 8590983168 | bytes 23068672 | tf_op jit(solution)/shard_map/dot_general | solution.py:19
  137.5 1.6 collective-permute-done.13
  139.1 4.4 %convert_reduce_fusion.3 = (f32[2048]{0:T(1024)S(1)}, bf16[256,2048]{1,0:T(8,128)(2,1)}, f32[256,2048]{1,0:T(8,128)}, bf16[1,256,2048]{2,1,0:T(8,128)(2,1)}, f32[2048]{0:T(1024)S(1)}) fusion(f32[256]{0:T(256)S(1)} %get-tuple-element.369, f32[256]{0:T(256)S(1)} %add_rsqrt_fusion, f32[256,2048]{1,0:T(8,128)S(1)} %get-tuple-element.324, ...), kind=kLoop, calls=%fused_computation.48 | loop fusion | flops 9957376 | bytes 11571200 | tf_op jit(solution)/shard_map/reduce_sum | solution.py:740
  144.4 9.0 %share.3 = (bf16[512,1024]{1,0:T(8,128)(2,1)S(1)}, bf16[512,1024]{1,0:T(8,128)(2,1)S(1)}) custom-call(s32[1]{0:T(128)} %bitcast.5.at, bf16[256,2048]{1,0:T(8,128)(2,1)S(1)} %collective-permute-done.12.near_ref.refs_6_, bf16[256,2048]{1,0:T(8,128)(2,1)S(1)} %collective-permute-done.15.far_ref.refs_7_, ...), custom_call_target="tpu_custom_call" | custom-call | flops 4294967296 | bytes 14680064 | tf_op jit(solution)/shard_map/share/pallas_call | solution.py:380
  155.5 7.9 %weight_out.1 = (bf16[2,256,1024]{2,1,0:T(8,128)(2,1)S(1)}, bf16[2,256,1024]{2,1,0:T(8,128)(2,1)S(1)}, bf16[2,256,1024]{2,1,0:T(8,128)(2,1)S(1)}, bf16[2,256,1024]{2,1,0:T(8,128)(2,1)S(1)}) custom-call(s32[18]{0:T(128)S(1)} %stack.76.at, bf16[256,2048]{1,0:T(8,128)(2,1)} %get-tuple-element.319.near_ref, bf16[256,2048]{1,0:T(8,128)(2,1)} %collective-permute-done.14.far_ref, ...), custom_call_target="tpu_custom_call" | custom-call | flops 2147483648 | bytes 4194304 | tf_op jit(solution)/shard_map/weight_out/pallas_call | solution.py:553
  163.5 4.3 %fusion.41.do_ref = bf16[512,1024]{1,0:T(8,128)(2,1)S(1)} fusion(bf16[1024,2048]{1,0:T(8,128)(2,1)S(1)} %copy-done.64, bf16[256,2048]{1,0:T(8,128)(2,1)} %collective-permute-done.14.far_ref, bf16[256,2048]{1,0:T(8,128)(2,1)} %get-tuple-element.319.near_ref), kind=kOutput, calls=%fused_computation.61 | convolution fusion | flops 2152202240 | bytes 7340032 | tf_op jit(solution)/shard_map/dot_general | solution.py:27
  167.8 3.9 collective-permute-done.17.near_ref.refs_8_
  171.7 1.5 collective-permute-start.20
  173.2 1.5 collective-permute-start.19
  174.7 10.0 %attend_back.1 = (bf16[512,1024]{1,0:T(8,128)(2,1)S(1)}, bf16[2,2048,128]{2,1,0:T(8,128)(2,1)S(1)}) custom-call(s32[4]{0:T(128)S(1)} %pad_add_fusion.info, bf16[512,1024]{1,0:T(8,128)(2,1)S(1)} %copy-done.30, bf16[512,1024]{1,0:T(8,128)(2,1)S(1)} %fusion.41.do_ref, bf16[512,1024]{1,0:T(8,128)(2,1)} %copy-done.28, f32[8,512]{1,0:T(8,128)S(1)} %get-tuple-element.171.lse_ref, ...), custom_call_target="tpu_custom_call" | custom-call | flops 21474836480 | bytes 4194304 | tf_op jit(solution)/shard_map/attend_back/pallas_call | solution.py:268
  184.8 12.5 %collective-permute-done.20 = bf16[2,1,256,1024]{3,2,1,0:T(8,128)(2,1)S(1)} collective-permute-done((bf16[2,1,256,1024]{3,2,1,0:T(8,128)(2,1)S(1)}, bf16[2,1,256,1024]{3,2,1,0:T(8,128)(2,1)S(1)}, u32[]{:S(2)}, u32[]{:S(2)}) %collective-permute-start.20) | collective-permute-done | bytes 1048608 | tf_op jit(solution)/shard_map/ppermute | solution.py:573
  198.5 1.4 fusion.68
  201.4 1.5 collective-permute-start.24
  204.2 9.3 %share.5 = (bf16[512,1024]{1,0:T(8,128)(2,1)S(1)}, bf16[512,1024]{1,0:T(8,128)(2,1)S(1)}) custom-call(s32[1]{0:T(128)} %bitcast.5.at, bf16[256,2048]{1,0:T(8,128)(2,1)} %collective-permute-done.17.near_ref.refs_8_, bf16[256,2048]{1,0:T(8,128)(2,1)S(1)} %collective-permute-done.25.far_ref.refs_9_, bf16[256,2048]{1,0:T(8,128)(2,1)S(1)} %copy-done.6, ...), custom_call_target="tpu_custom_call" | custom-call | flops 4294967296 | bytes 14680064 | tf_op jit(solution)/shard_map/share/pallas_call | solution.py:380
  215.5 9.8 %share.4 = (bf16[512,1024]{1,0:T(8,128)(2,1)S(1)}, bf16[512,1024]{1,0:T(8,128)(2,1)S(1)}) custom-call(s32[1]{0:T(128)} %bitcast.5.at, bf16[256,2048]{1,0:T(8,128)(2,1)S(1)} %collective-permute-done.18.near_ref.refs_10_, bf16[256,2048]{1,0:T(8,128)(2,1)} %collective-permute-done.21.far_ref.refs_11_, ...), custom_call_target="tpu_custom_call" | custom-call | flops 4294967296 | bytes 14680064 | tf_op jit(solution)/shard_map/share/pallas_call | solution.py:380
  227.0 16.1 %weight_down.1 = (bf16[2,512,512]{2,1,0:T(8,128)(2,1)}, bf16[2,512,512]{2,1,0:T(8,128)(2,1)}, bf16[2,512,512]{2,1,0:T(8,128)(2,1)}, bf16[2,512,512]{2,1,0:T(8,128)(2,1)}) custom-call(s32[5]{0:T(128)} %stack.77.at, bf16[512,4096]{1,0:T(8,128)(2,1)} %get-tuple-element.160.refs_0_, bf16[512,1024]{1,0:T(8,128)(2,1)} %copy-done.23, bf16[512,1024]{1,0:T(8,128)(2,1)} %copy-done.24, ...), custom_call_target="tpu_custom_call" | custom-call | flops 8589934592 | bytes 25165824 | tf_op jit(solution)/shard_map/weight_down/pallas_call | solution.py:475
  243.1 1.5 collective-permute-start.28
  245.4 10.1 %collective-permute-start.30 = (bf16[128,1024]{1,0:T(8,128)(2,1)S(1)}, bf16[128,1024]{1,0:T(8,128)(2,1)}, u32[]{:S(2)}, u32[]{:S(2)}) collective-permute-start(bf16[128,1024]{1,0:T(8,128)(2,1)S(1)} %get-tuple-element.349), channel_id=1, source_target_pairs={{0,4},{2,6},{4,0},{6,2},{1,5},{3,7},{5,1},{7,3},{8,12},{10,14},{12... | collective-permute-start | bytes 786440 | tf_op jit(solution)/shard_map/ppermute | solution.py:578
  255.5 16.2 %weight_up.1 = (bf16[2,512,512]{2,1,0:T(8,128)(2,1)}, bf16[2,512,512]{2,1,0:T(8,128)(2,1)}, bf16[2,512,512]{2,1,0:T(8,128)(2,1)}, bf16[2,512,512]{2,1,0:T(8,128)(2,1)}) custom-call(s32[5]{0:T(128)} %stack.77.at, bf16[512,4096]{1,0:T(8,128)(2,1)} %get-tuple-element.199.refs_0_, bf16[512,1024]{1,0:T(8,128)(2,1)} %copy-done.20, bf16[512,1024]{1,0:T(8,128)(2,1)} %copy-done.21, ...), custom_call_target="tpu_custom_call" | custom-call | flops 8589934592 | bytes 25165824 | tf_op jit(solution)/shard_map/weight_up/pallas_call | solution.py:475
  271.8 2.6 fusion.64
  276.1 1.6 collective-permute-start.36
  278.3 1.4 add_bitcast_fusion
  285.0 8.7 %collective-permute-done.35 = bf16[512,128]{1,0:T(8,128)(2,1)S(1)} collective-permute-done((bf16[512,128]{1,0:T(8,128)(2,1)S(1)}, bf16[512,128]{1,0:T(8,128)(2,1)S(1)}, u32[]{:S(2)}, u32[]{:S(2)}) %collective-permute-start.35) | collective-permute-done | bytes 131104 | tf_op jit(solution)/shard_map/ppermute | solution.py:588
  294.1 1.7 collective-permute-done.34
  295.8 2.8 collective-permute-start.41
  298.6 5.1 %fusion.4 = bf16[512,2048]{1,0:T(8,128)(2,1)S(1)} fusion(bf16[2048,128]{1,0:T(8,128)(2,1)S(1)} %copy-done.49, bf16[2048,1024]{1,0:T(8,128)(2,1)} %param.26, bf16[512,128]{1,0:T(8,128)(2,1)S(1)} %get-tuple-element.322, bf16[512,1024]{1,0:T(8,128)(2,1)S(1)} %get-tuple-element.208), kind=kOutput, calls=%fused_computation.5 | convolution fusion | flops 2428764160 | bytes 7995392 | tf_op jit(solution)/shard_map/dot_general | solution.py:27
  305.0 1.9 fusion.60
  309.1 8.2 %weight_query.1 = (bf16[2,256,1152]{2,1,0:T(8,128)(2,1)S(1)}, bf16[2,256,1152]{2,1,0:T(8,128)(2,1)S(1)}, bf16[2,256,1152]{2,1,0:T(8,128)(2,1)S(1)}, bf16[2,256,1152]{2,1,0:T(8,128)(2,1)}) custom-call(s32[18]{0:T(128)S(1)} %stack.76.at, bf16[256,2048]{1,0:T(8,128)(2,1)S(1)} %copy-done.10, bf16[256,2048]{1,0:T(8,128)(2,1)S(1)} %copy-done.18, ...), custom_call_target="tpu_custom_call" | custom-call | flops 2415919104 | bytes 4718592 | tf_op jit(solution)/shard_map/weight_query/pallas_call | solution.py:553
  317.8 1.8 collective-permute-done.41
  319.9 2.0 collective-permute-start.46
  323.5 2.0 fusion.70
  326.3 19.8 %collective-permute-done.46 = bf16[2,1,256,1152]{3,2,1,0:T(8,128)(2,1)S(1)} collective-permute-done((bf16[2,1,256,1152]{3,2,1,0:T(8,128)(2,1)S(1)}, bf16[2,1,256,1152]{3,2,1,0:T(8,128)(2,1)S(1)}, u32[]{:S(2)}, u32[]{:S(2)}) %collective-permute-start.46) | collective-permute-done | bytes 1179680 | tf_op jit(solution)/shard_map/ppermute | solution.py:573
  346.1 1.9 collective-permute-start.43
  348.6 9.3 %collective-permute-done.43 = bf16[1,512,512]{2,1,0:T(8,128)(2,1)S(1)} collective-permute-done((bf16[1,512,512]{2,1,0:T(8,128)(2,1)S(1)}, bf16[1,512,512]{2,1,0:T(8,128)(2,1)S(1)}, u32[]{:S(2)}, u32[]{:S(2)}) %collective-permute-start.43) | collective-permute-done | bytes 524320 | tf_op jit(solution)/shard_map/ppermute | solution.py:573
  358.9 1.5 collective-permute-start.52
  365.2 1.3 collective-permute-start.62
  366.5 2.0 collective-permute-start.63
  369.9 2.5 collective-permute-done.53
  373.6 5.5 %collective-permute-start.57 = (f32[144,128]{1,0:T(8,128)S(1)}, f32[144,128]{1,0:T(8,128)S(1)}, u32[]{:S(2)}, u32[]{:S(2)}) collective-permute-start(f32[144,128]{1,0:T(8,128)S(1)} %add_add_fusion.1), channel_id=1, source_target_pairs={{0,6},{2,0},{4,2},{6,4},{1,7},{3,1},{5,3},{7,5},{8,14},{10,8},{12,... | collective-permute-start | bytes 221192 | tf_op jit(solution)/shard_map/ppermute | solution.py:578
  379.9 6.7 %collective-permute-start.55 = (f32[144,128]{1,0:T(8,128)S(1)}, f32[144,128]{1,0:T(8,128)S(1)}, u32[]{:S(2)}, u32[]{:S(2)}) collective-permute-start(f32[144,128]{1,0:T(8,128)S(1)} %add_add_fusion.1), channel_id=1, source_target_pairs={{0,2},{2,4},{4,6},{6,0},{1,3},{3,5},{5,7},{7,1},{8,10},{10,12},{12... | collective-permute-start | bytes 221192 | tf_op jit(solution)/shard_map/ppermute | solution.py:578
  387.4 6.5 %collective-permute-start.60 = (bf16[128,1152]{1,0:T(8,128)(2,1)}, bf16[128,1152]{1,0:T(8,128)(2,1)S(1)}, u32[]{:S(2)}, u32[]{:S(2)}) collective-permute-start(bf16[128,1152]{1,0:T(8,128)(2,1)} %get-tuple-element.243), channel_id=1, source_target_pairs={{0,6},{2,0},{4,2},{6,4},{1,7},{3,1},{5,3},{7,5},{8,14},{10,8},{12,... | collective-permute-start | bytes 884744 | tf_op jit(solution)/shard_map/ppermute | solution.py:578
  393.9 2.6 place.1
  398.4 1.4 reshape.657
  400.4 1.4 constant_dynamic-slice_fusion
  403.1 15.8 %collective-permute-done.59 = bf16[128,1152]{1,0:T(8,128)(2,1)S(1)} collective-permute-done((bf16[128,1152]{1,0:T(8,128)(2,1)S(1)}, bf16[128,1152]{1,0:T(8,128)(2,1)S(1)}, u32[]{:S(2)}, u32[]{:S(2)}) %collective-permute-start.59) | collective-permute-done | bytes 294944 | tf_op jit(solution)/shard_map/ppermute | solution.py:578
  420.8 1.4 copy.41
  (311 shorter events, 54.4 us)
Async XLA Ops:
  5.1 15.7 %collective-permute-start.2 = (bf16[256,2048]{1,0:T(8,128)(2,1)}, bf16[256,2048]{1,0:T(8,128)(2,1)}, u32[]{:S(2)}, u32[]{:S(2)}) collective-permute-start(bf16[256,2048]{1,0:T(8,128)(2,1)} %bitcast.8.refs_4_), channel_id=1, source_target_pairs={{0,1},{1,0},{2,3},{3,2},{4,5},{5,4},{6,7},{7,6},{8,9},{9,8},{10,11... | collective-permute-start | bytes 3145736 | tf_op jit(solution)/shard_map/ppermute | solution.py:568
  5.6 40.2 %collective-permute-start = (bf16[256,2048]{1,0:T(8,128)(2,1)S(1)}, bf16[256,2048]{1,0:T(8,128)(2,1)S(1)}, u32[]{:S(2)}, u32[]{:S(2)}) collective-permute-start(bf16[256,2048]{1,0:T(8,128)(2,1)S(1)} %fusion.17.near_ref), channel_id=1, source_target_pairs={{0,1},{1,0},{2,3},{3,2},{4,5},{5,4},{6,7},{7,6},{8,9},{9,8},{10,11... | collective-permute-start | bytes 3145736 | tf_op jit(solution)/shard_map/ppermute | solution.py:568
  5.7 35.4 %collective-permute-start.1 = (bf16[256,2048]{1,0:T(8,128)(2,1)}, bf16[256,2048]{1,0:T(8,128)(2,1)S(1)}, u32[]{:S(2)}, u32[]{:S(2)}) collective-permute-start(bf16[256,2048]{1,0:T(8,128)(2,1)} %bitcast.8.refs_4_), channel_id=1, source_target_pairs={{0,2},{2,4},{4,6},{6,0},{1,3},{3,5},{5,7},{7,1},{8,10},{10,12},{12... | collective-permute-start | bytes 3145736 | tf_op jit(solution)/shard_map/ppermute | solution.py:578
  8.6 28.1 %collective-permute-start.3 = (bf16[256,256]{1,0:T(8,128)(2,1)S(1)}, bf16[256,256]{1,0:T(8,128)(2,1)S(1)}, u32[]{:S(2)}, u32[]{:S(2)}) collective-permute-start(bf16[256,256]{1,0:T(8,128)(2,1)S(1)} %fusion.48), channel_id=1, source_target_pairs={{0,2},{2,4},{4,6},{1,3},{3,5},{5,7},{8,10},{10,12},{12,14},{9,11},... | collective-permute-start | bytes 393224 | tf_op jit(solution)/shard_map/ppermute | solution.py:583
  12.1 25.9 %collective-permute-start.4 = (bf16[256,256]{1,0:T(8,128)(2,1)S(1)}, bf16[256,256]{1,0:T(8,128)(2,1)}, u32[]{:S(2)}, u32[]{:S(2)}) collective-permute-start(bf16[256,256]{1,0:T(8,128)(2,1)S(1)} %fusion.48), channel_id=1, source_target_pairs={{0,4},{2,6},{1,5},{3,7},{8,12},{10,14},{9,13},{11,15},{16,20},{18,... | collective-permute-start | bytes 393224 | tf_op jit(solution)/shard_map/ppermute | solution.py:583
  20.7 19.3 %collective-permute-start.5 = (bf16[256,256]{1,0:T(8,128)(2,1)S(1)}, bf16[256,256]{1,0:T(8,128)(2,1)S(1)}, u32[]{:S(2)}, u32[]{:S(2)}) collective-permute-start(bf16[256,256]{1,0:T(8,128)(2,1)S(1)} %fusion.48), channel_id=1, source_target_pairs={{0,6},{1,7},{8,14},{9,15},{16,22},{17,23},{24,30},{25,31}} | collective-permute-start | bytes 393224 | tf_op jit(solution)/shard_map/ppermute | solution.py:583
  41.0 7.2 %collective-permute-start.6 = (bf16[4,256,256]{2,1,0:T(8,128)(2,1)S(1)}, bf16[4,256,256]{2,1,0:T(8,128)(2,1)S(1)}, u32[]{:S(2)}, u32[]{:S(2)}) collective-permute-start(bf16[4,256,256]{2,1,0:T(8,128)(2,1)S(1)} %pad_maximum_fusion.2.near_ref), channel_id=1, source_target_pairs={{0,1},{1,0},{2,3},{3,2},{4,5},{5,4},{6,7},{7,6},{8,9},{9,8},{10,11... | collective-permute-start | bytes 1572872 | tf_op jit(solution)/shard_map/ppermute | solution.py:568
  41.1 31.3 %collective-permute-start.7 = (bf16[256,2048]{1,0:T(8,128)(2,1)S(1)}, bf16[256,2048]{1,0:T(8,128)(2,1)S(1)}, u32[]{:S(2)}, u32[]{:S(2)}) collective-permute-start(bf16[256,2048]{1,0:T(8,128)(2,1)S(1)} %collective-permute-done.1.gnear_ref.refs_6_), channel_id=1, source_target_pairs={{0,2},{2,4},{4,6},{6,0},{1,3},{3,5},{5,7},{7,1},{8,10},{10,12},{12... | collective-permute-start | bytes 3145736 | tf_op jit(solution)/shard_map/ppermute | solution.py:578
  74.9 2.7 collective-permute-start.8
  79.5 2.7 collective-permute-start.9
  79.7 27.9 %collective-permute-start.10 = (bf16[256,2048]{1,0:T(8,128)(2,1)S(1)}, bf16[256,2048]{1,0:T(8,128)(2,1)}, u32[]{:S(2)}, u32[]{:S(2)}) collective-permute-start(bf16[256,2048]{1,0:T(8,128)(2,1)S(1)} %collective-permute-done.7.gnear_ref.refs_8_), channel_id=1, source_target_pairs={{0,2},{2,4},{4,6},{6,0},{1,3},{3,5},{5,7},{7,1},{8,10},{10,12},{12... | collective-permute-start | bytes 3145736 | tf_op jit(solution)/shard_map/ppermute | solution.py:578
  79.7 55.7 %collective-permute-start.12 = (bf16[256,2048]{1,0:T(8,128)(2,1)S(1)}, bf16[256,2048]{1,0:T(8,128)(2,1)S(1)}, u32[]{:S(2)}, u32[]{:S(2)}) collective-permute-start(bf16[256,2048]{1,0:T(8,128)(2,1)S(1)} %add_convert_fusion.1.near_ref.refs_4_), channel_id=1, source_target_pairs={{0,2},{2,4},{4,6},{6,0},{1,3},{3,5},{5,7},{7,1},{8,10},{10,12},{12... | collective-permute-start | bytes 3145736 | tf_op jit(solution)/shard_map/ppermute | solution.py:578
  121.4 13.7 %collective-permute-start.11 = (bf16[256,2048]{1,0:T(8,128)(2,1)S(1)}, bf16[256,2048]{1,0:T(8,128)(2,1)S(1)}, u32[]{:S(2)}, u32[]{:S(2)}) collective-permute-start(bf16[256,2048]{1,0:T(8,128)(2,1)S(1)} %slice.276), channel_id=1, source_target_pairs={{0,1},{1,0},{2,3},{3,2},{4,5},{5,4},{6,7},{7,6},{8,9},{9,8},{10,11... | collective-permute-start | bytes 3145736 | tf_op jit(solution)/shard_map/ppermute | solution.py:568
  135.6 3.5 collective-permute-start.13
  136.1 8.3 %collective-permute-start.16 = (bf16[256,2048]{1,0:T(8,128)(2,1)S(1)}, bf16[256,2048]{1,0:T(8,128)(2,1)}, u32[]{:S(2)}, u32[]{:S(2)}) collective-permute-start(bf16[256,2048]{1,0:T(8,128)(2,1)S(1)} %collective-permute-done.1.gnear_ref.refs_6_), channel_id=1, source_target_pairs={{0,1},{1,0},{2,3},{3,2},{4,5},{5,4},{6,7},{7,6},{8,9},{9,8},{10,11... | collective-permute-start | bytes 3145736 | tf_op jit(solution)/shard_map/ppermute | solution.py:568
  136.2 8.2 %collective-permute-start.15 = (bf16[256,2048]{1,0:T(8,128)(2,1)S(1)}, bf16[256,2048]{1,0:T(8,128)(2,1)S(1)}, u32[]{:S(2)}, u32[]{:S(2)}) collective-permute-start(bf16[256,2048]{1,0:T(8,128)(2,1)S(1)} %collective-permute-done.12.near_ref.refs_6_), channel_id=1, source_target_pairs={{0,1},{1,0},{2,3},{3,2},{4,5},{5,4},{6,7},{7,6},{8,9},{9,8},{10,11... | collective-permute-start | bytes 3145736 | tf_op jit(solution)/shard_map/ppermute | solution.py:568
  143.5 11.9 %collective-permute-start.14 = (bf16[256,2048]{1,0:T(8,128)(2,1)}, bf16[256,2048]{1,0:T(8,128)(2,1)}, u32[]{:S(2)}, u32[]{:S(2)}) collective-permute-start(bf16[256,2048]{1,0:T(8,128)(2,1)} %get-tuple-element.319.near_ref), channel_id=1, source_target_pairs={{0,1},{1,0},{2,3},{3,2},{4,5},{5,4},{6,7},{7,6},{8,9},{9,8},{10,11... | collective-permute-start | bytes 3145736 | tf_op jit(solution)/shard_map/ppermute | solution.py:568
  144.0 57.4 %collective-permute-start.26 = (bf16[256,2048]{1,0:T(8,128)(2,1)}, bf16[256,2048]{1,0:T(8,128)(2,1)}, u32[]{:S(2)}, u32[]{:S(2)}) collective-permute-start(bf16[256,2048]{1,0:T(8,128)(2,1)} %copy-done.5), channel_id=1, source_target_pairs={{0,1},{1,0},{2,3},{3,2},{4,5},{5,4},{6,7},{7,6},{8,9},{9,8},{10,11... | collective-permute-start | bytes 3145736 | tf_op jit(solution)/shard_map/ppermute | solution.py:568
  144.2 27.5 %collective-permute-start.17 = (bf16[256,2048]{1,0:T(8,128)(2,1)S(1)}, bf16[256,2048]{1,0:T(8,128)(2,1)}, u32[]{:S(2)}, u32[]{:S(2)}) collective-permute-start(bf16[256,2048]{1,0:T(8,128)(2,1)S(1)} %collective-permute-done.12.near_ref.refs_6_), channel_id=1, source_target_pairs={{0,2},{2,4},{4,6},{6,0},{1,3},{3,5},{5,7},{7,1},{8,10},{10,12},{12... | collective-permute-start | bytes 3145736 | tf_op jit(solution)/shard_map/ppermute | solution.py:578
  171.7 28.2 %collective-permute-start.18 = (bf16[256,2048]{1,0:T(8,128)(2,1)}, bf16[256,2048]{1,0:T(8,128)(2,1)S(1)}, u32[]{:S(2)}, u32[]{:S(2)}) collective-permute-start(bf16[256,2048]{1,0:T(8,128)(2,1)} %collective-permute-done.17.near_ref.refs_8_), channel_id=1, source_target_pairs={{0,2},{2,4},{4,6},{6,0},{1,3},{3,5},{5,7},{7,1},{8,10},{10,12},{12... | collective-permute-start | bytes 3145736 | tf_op jit(solution)/shard_map/ppermute | solution.py:578
  171.7 31.2 %collective-permute-start.25 = (bf16[256,2048]{1,0:T(8,128)(2,1)}, bf16[256,2048]{1,0:T(8,128)(2,1)S(1)}, u32[]{:S(2)}, u32[]{:S(2)}) collective-permute-start(bf16[256,2048]{1,0:T(8,128)(2,1)} %collective-permute-done.17.near_ref.refs_8_), channel_id=1, source_target_pairs={{0,1},{1,0},{2,3},{3,2},{4,5},{5,4},{6,7},{7,6},{8,9},{9,8},{10,11... | collective-permute-start | bytes 3145736 | tf_op jit(solution)/shard_map/ppermute | solution.py:568
  171.7 25.6 %collective-permute-start.20 = (bf16[2,1,256,1024]{3,2,1,0:T(8,128)(2,1)S(1)}, bf16[2,1,256,1024]{3,2,1,0:T(8,128)(2,1)S(1)}, u32[]{:S(2)}, u32[]{:S(2)}) collective-permute-start(bf16[2,1,256,1024]{3,2,1,0:T(8,128)(2,1)S(1)} %bitcast.235), channel_id=1, source_target_pairs={{0,16},{8,24},{16,0},{24,8},{1,17},{9,25},{17,1},{25,9},{2,18},{10... | collective-permute-start | bytes 3145736 | tf_op jit(solution)/shard_map/ppermute | solution.py:573
  173.2 25.3 %collective-permute-start.19 = (bf16[2,1,256,1024]{3,2,1,0:T(8,128)(2,1)S(1)}, bf16[2,1,256,1024]{3,2,1,0:T(8,128)(2,1)S(1)}, u32[]{:S(2)}, u32[]{:S(2)}) collective-permute-start(bf16[2,1,256,1024]{3,2,1,0:T(8,128)(2,1)S(1)} %bitcast.234), channel_id=1, source_target_pairs={{0,8},{8,0},{16,24},{24,16},{1,9},{9,1},{17,25},{25,17},{2,10},{10... | collective-permute-start | bytes 3145736 | tf_op jit(solution)/shard_map/ppermute | solution.py:573
  197.3 18.2 %collective-permute-start.22 = (bf16[256,2048]{1,0:T(8,128)(2,1)}, bf16[256,2048]{1,0:T(8,128)(2,1)}, u32[]{:S(2)}, u32[]{:S(2)}) collective-permute-start(bf16[256,2048]{1,0:T(8,128)(2,1)} %collective-permute-done.10.gnear_ref.refs_10_), channel_id=1, source_target_pairs={{0,1},{1,0},{2,3},{3,2},{4,5},{5,4},{6,7},{7,6},{8,9},{9,8},{10,11... | collective-permute-start | bytes 3145736 | tf_op jit(solution)/shard_map/ppermute | solution.py:568
  200.0 15.6 %collective-permute-start.21 = (bf16[256,2048]{1,0:T(8,128)(2,1)S(1)}, bf16[256,2048]{1,0:T(8,128)(2,1)}, u32[]{:S(2)}, u32[]{:S(2)}) collective-permute-start(bf16[256,2048]{1,0:T(8,128)(2,1)S(1)} %collective-permute-done.18.near_ref.refs_10_), channel_id=1, source_target_pairs={{0,1},{1,0},{2,3},{3,2},{4,5},{5,4},{6,7},{7,6},{8,9},{9,8},{10,11... | collective-permute-start | bytes 3145736 | tf_op jit(solution)/shard_map/ppermute | solution.py:568
  200.8 24.6 %collective-permute-start.23 = (bf16[1,256,1024]{2,1,0:T(8,128)(2,1)}, bf16[1,256,1024]{2,1,0:T(8,128)(2,1)S(1)}, u32[]{:S(2)}, u32[]{:S(2)}) collective-permute-start(bf16[1,256,1024]{2,1,0:T(8,128)(2,1)} %get-tuple-element.184), channel_id=1, source_target_pairs={{0,16},{8,24},{16,0},{24,8},{1,17},{9,25},{17,1},{25,9},{2,18},{10... | collective-permute-start | bytes 1572872 | tf_op jit(solution)/shard_map/ppermute | solution.py:573
  201.4 24.0 %collective-permute-start.24 = (bf16[1,256,1024]{2,1,0:T(8,128)(2,1)}, bf16[1,256,1024]{2,1,0:T(8,128)(2,1)S(1)}, u32[]{:S(2)}, u32[]{:S(2)}) collective-permute-start(bf16[1,256,1024]{2,1,0:T(8,128)(2,1)} %get-tuple-element.185), channel_id=1, source_target_pairs={{0,8},{8,0},{16,24},{24,16},{1,9},{9,1},{17,25},{25,17},{2,10},{10... | collective-permute-start | bytes 1572872 | tf_op jit(solution)/shard_map/ppermute | solution.py:573
  243.1 28.7 %collective-permute-start.28 = (bf16[2,1,512,512]{3,2,1,0:T(8,128)(2,1)}, bf16[2,1,512,512]{3,2,1,0:T(8,128)(2,1)}, u32[]{:S(2)}, u32[]{:S(2)}) collective-permute-start(bf16[2,1,512,512]{3,2,1,0:T(8,128)(2,1)} %bitcast.246), channel_id=1, source_target_pairs={{0,16},{8,24},{16,0},{24,8},{1,17},{9,25},{17,1},{25,9},{2,18},{10... | collective-permute-start | bytes 3145736 | tf_op jit(solution)/shard_map/ppermute | solution.py:573
  244.5 27.2 %collective-permute-start.27 = (bf16[2,1,512,512]{3,2,1,0:T(8,128)(2,1)}, bf16[2,1,512,512]{3,2,1,0:T(8,128)(2,1)}, u32[]{:S(2)}, u32[]{:S(2)}) collective-permute-start(bf16[2,1,512,512]{3,2,1,0:T(8,128)(2,1)} %bitcast.245), channel_id=1, source_target_pairs={{0,8},{8,0},{16,24},{24,16},{1,9},{9,1},{17,25},{25,17},{2,10},{10... | collective-permute-start | bytes 3145736 | tf_op jit(solution)/shard_map/ppermute | solution.py:573
  245.3 29.1 %collective-permute-start.29 = (bf16[128,1024]{1,0:T(8,128)(2,1)S(1)}, bf16[128,1024]{1,0:T(8,128)(2,1)}, u32[]{:S(2)}, u32[]{:S(2)}) collective-permute-start(bf16[128,1024]{1,0:T(8,128)(2,1)S(1)} %get-tuple-element.350), channel_id=1, source_target_pairs={{0,2},{2,4},{4,6},{6,0},{1,3},{3,5},{5,7},{7,1},{8,10},{10,12},{12... | collective-permute-start | bytes 786440 | tf_op jit(solution)/shard_map/ppermute | solution.py:578
  245.4 29.0 %collective-permute-start.30 = (bf16[128,1024]{1,0:T(8,128)(2,1)S(1)}, bf16[128,1024]{1,0:T(8,128)(2,1)}, u32[]{:S(2)}, u32[]{:S(2)}) collective-permute-start(bf16[128,1024]{1,0:T(8,128)(2,1)S(1)} %get-tuple-element.349), channel_id=1, source_target_pairs={{0,4},{2,6},{4,0},{6,2},{1,5},{3,7},{5,1},{7,3},{8,12},{10,14},{12... | collective-permute-start | bytes 786440 | tf_op jit(solution)/shard_map/ppermute | solution.py:578
  255.5 18.9 %collective-permute-start.31 = (bf16[128,1024]{1,0:T(8,128)(2,1)S(1)}, bf16[128,1024]{1,0:T(8,128)(2,1)}, u32[]{:S(2)}, u32[]{:S(2)}) collective-permute-start(bf16[128,1024]{1,0:T(8,128)(2,1)S(1)} %get-tuple-element.348), channel_id=1, source_target_pairs={{0,6},{2,0},{4,2},{6,4},{1,7},{3,1},{5,3},{7,5},{8,14},{10,8},{12,... | collective-permute-start | bytes 786440 | tf_op jit(solution)/shard_map/ppermute | solution.py:578
  275.3 5.4 %collective-permute-start.32 = (bf16[4,2,256,128]{3,2,1,0:T(8,128)(2,1)}, bf16[4,2,256,128]{3,2,1,0:T(8,128)(2,1)S(1)}, u32[]{:S(2)}, u32[]{:S(2)}) collective-permute-start(bf16[4,2,256,128]{3,2,1,0:T(8,128)(2,1)} %dynamic-slice_bitcast_fusion), channel_id=1, source_target_pairs={{0,1},{1,0},{2,3},{3,2},{4,5},{5,4},{6,7},{7,6},{8,9},{9,8},{10,11... | collective-permute-start | bytes 1572872 | tf_op jit(solution)/shard_map/ppermute | solution.py:568
  276.1 27.7 %collective-permute-start.36 = (bf16[1,512,512]{2,1,0:T(8,128)(2,1)}, bf16[1,512,512]{2,1,0:T(8,128)(2,1)}, u32[]{:S(2)}, u32[]{:S(2)}) collective-permute-start(bf16[1,512,512]{2,1,0:T(8,128)(2,1)} %get-tuple-element.210), channel_id=1, source_target_pairs={{0,16},{8,24},{16,0},{24,8},{1,17},{9,25},{17,1},{25,9},{2,18},{10... | collective-permute-start | bytes 1572872 | tf_op jit(solution)/shard_map/ppermute | solution.py:573
  277.8 26.0 %collective-permute-start.37 = (bf16[1,512,512]{2,1,0:T(8,128)(2,1)}, bf16[1,512,512]{2,1,0:T(8,128)(2,1)}, u32[]{:S(2)}, u32[]{:S(2)}) collective-permute-start(bf16[1,512,512]{2,1,0:T(8,128)(2,1)} %get-tuple-element.211), channel_id=1, source_target_pairs={{0,8},{8,0},{16,24},{24,16},{1,9},{9,1},{17,25},{25,17},{2,10},{10... | collective-permute-start | bytes 1572872 | tf_op jit(solution)/shard_map/ppermute | solution.py:573
  280.9 12.8 %collective-permute-start.35 = (bf16[512,128]{1,0:T(8,128)(2,1)S(1)}, bf16[512,128]{1,0:T(8,128)(2,1)S(1)}, u32[]{:S(2)}, u32[]{:S(2)}) collective-permute-start(bf16[512,128]{1,0:T(8,128)(2,1)S(1)} %bitcast.240), channel_id=1, source_target_pairs={{6,0},{7,1},{14,8},{15,9},{22,16},{23,17},{30,24},{31,25}} | collective-permute-start | bytes 393224 | tf_op jit(solution)/shard_map/ppermute | solution.py:588
  282.2 13.6 %collective-permute-start.34 = (bf16[512,128]{1,0:T(8,128)(2,1)S(1)}, bf16[512,128]{1,0:T(8,128)(2,1)S(1)}, u32[]{:S(2)}, u32[]{:S(2)}) collective-permute-start(bf16[512,128]{1,0:T(8,128)(2,1)S(1)} %bitcast.239), channel_id=1, source_target_pairs={{4,0},{6,2},{5,1},{7,3},{12,8},{14,10},{13,9},{15,11},{20,16},{22,... | collective-permute-start | bytes 393224 | tf_op jit(solution)/shard_map/ppermute | solution.py:588
  283.5 15.0 %collective-permute-start.33 = (bf16[512,128]{1,0:T(8,128)(2,1)S(1)}, bf16[512,128]{1,0:T(8,128)(2,1)S(1)}, u32[]{:S(2)}, u32[]{:S(2)}) collective-permute-start(bf16[512,128]{1,0:T(8,128)(2,1)S(1)} %bitcast.238), channel_id=1, source_target_pairs={{2,0},{4,2},{6,4},{3,1},{5,3},{7,5},{10,8},{12,10},{14,12},{11,9},... | collective-permute-start | bytes 393224 | tf_op jit(solution)/shard_map/ppermute | solution.py:588
  293.7 24.1 %collective-permute-start.42 = (bf16[2,1,512,512]{3,2,1,0:T(8,128)(2,1)}, bf16[2,1,512,512]{3,2,1,0:T(8,128)(2,1)S(1)}, u32[]{:S(2)}, u32[]{:S(2)}) collective-permute-start(bf16[2,1,512,512]{3,2,1,0:T(8,128)(2,1)} %bitcast.54), channel_id=1, source_target_pairs={{0,16},{8,24},{16,0},{24,8},{1,17},{9,25},{17,1},{25,9},{2,18},{10... | collective-permute-start | bytes 3145736 | tf_op jit(solution)/shard_map/ppermute | solution.py:573
  295.8 23.8 %collective-permute-start.41 = (bf16[2,1,512,512]{3,2,1,0:T(8,128)(2,1)}, bf16[2,1,512,512]{3,2,1,0:T(8,128)(2,1)S(1)}, u32[]{:S(2)}, u32[]{:S(2)}) collective-permute-start(bf16[2,1,512,512]{3,2,1,0:T(8,128)(2,1)} %bitcast.52), channel_id=1, source_target_pairs={{0,8},{8,0},{16,24},{24,16},{1,9},{9,1},{17,25},{25,17},{2,10},{10... | collective-permute-start | bytes 3145736 | tf_op jit(solution)/shard_map/ppermute | solution.py:573
  303.9 18.2 %collective-permute-start.38 = (bf16[256,2048]{1,0:T(8,128)(2,1)S(1)}, bf16[256,2048]{1,0:T(8,128)(2,1)S(1)}, u32[]{:S(2)}, u32[]{:S(2)}) collective-permute-start(bf16[256,2048]{1,0:T(8,128)(2,1)S(1)} %slice.240), channel_id=1, source_target_pairs={{0,1},{1,0},{2,3},{3,2},{4,5},{5,4},{6,7},{7,6},{8,9},{9,8},{10,11... | collective-permute-start | bytes 3145736 | tf_op jit(solution)/shard_map/ppermute | solution.py:568
  304.0 13.3 %collective-permute-start.40 = (f32[1,128]{1,0:T(1,128)S(1)}, f32[1,128]{1,0:T(1,128)S(1)}, u32[]{:S(2)}, u32[]{:S(2)}) collective-permute-start(f32[1,128]{1,0:T(1,128)S(1)} %fusion.87), channel_id=1, source_target_pairs={{0,1},{1,0},{2,3},{3,2},{4,5},{5,4},{6,7},{7,6},{8,9},{9,8},{10,11... | collective-permute-start | bytes 1544 | tf_op jit(solution)/shard_map/ppermute | solution.py:568
  308.3 40.3 %collective-permute-start.47 = (bf16[1,1024,128]{2,1,0:T(8,128)(2,1)S(1)}, bf16[1,1024,128]{2,1,0:T(8,128)(2,1)S(1)}, u32[]{:S(2)}, u32[]{:S(2)}) collective-permute-start(bf16[1,1024,128]{2,1,0:T(8,128)(2,1)S(1)} %get-tuple-element.231), channel_id=1, source_target_pairs={{0,2},{2,4},{4,6},{6,0},{1,3},{3,5},{5,7},{7,1},{8,10},{10,12},{12... | collective-permute-start | bytes 786440 | tf_op jit(solution)/shard_map/ppermute | solution.py:578
  317.3 31.3 %collective-permute-start.48 = (bf16[1,1024,128]{2,1,0:T(8,128)(2,1)S(1)}, bf16[1,1024,128]{2,1,0:T(8,128)(2,1)S(1)}, u32[]{:S(2)}, u32[]{:S(2)}) collective-permute-start(bf16[1,1024,128]{2,1,0:T(8,128)(2,1)S(1)} %get-tuple-element.232), channel_id=1, source_target_pairs={{0,4},{2,6},{4,0},{6,2},{1,5},{3,7},{5,1},{7,3},{8,12},{10,14},{12... | collective-permute-start | bytes 786440 | tf_op jit(solution)/shard_map/ppermute | solution.py:578
  319.9 26.2 %collective-permute-start.46 = (bf16[2,1,256,1152]{3,2,1,0:T(8,128)(2,1)S(1)}, bf16[2,1,256,1152]{3,2,1,0:T(8,128)(2,1)S(1)}, u32[]{:S(2)}, u32[]{:S(2)}) collective-permute-start(bf16[2,1,256,1152]{3,2,1,0:T(8,128)(2,1)S(1)} %bitcast.233), channel_id=1, source_target_pairs={{0,16},{8,24},{16,0},{24,8},{1,17},{9,25},{17,1},{25,9},{2,18},{10... | collective-permute-start | bytes 3538952 | tf_op jit(solution)/shard_map/ppermute | solution.py:573
  321.9 26.1 %collective-permute-start.45 = (bf16[2,1,256,1152]{3,2,1,0:T(8,128)(2,1)S(1)}, bf16[2,1,256,1152]{3,2,1,0:T(8,128)(2,1)S(1)}, u32[]{:S(2)}, u32[]{:S(2)}) collective-permute-start(bf16[2,1,256,1152]{3,2,1,0:T(8,128)(2,1)S(1)} %bitcast.232), channel_id=1, source_target_pairs={{0,8},{8,0},{16,24},{24,16},{1,9},{9,1},{17,25},{25,17},{2,10},{10... | collective-permute-start | bytes 3538952 | tf_op jit(solution)/shard_map/ppermute | solution.py:573
  325.5 23.1 %collective-permute-start.49 = (bf16[1,1024,128]{2,1,0:T(8,128)(2,1)S(1)}, bf16[1,1024,128]{2,1,0:T(8,128)(2,1)S(1)}, u32[]{:S(2)}, u32[]{:S(2)}) collective-permute-start(bf16[1,1024,128]{2,1,0:T(8,128)(2,1)S(1)} %get-tuple-element.233), channel_id=1, source_target_pairs={{0,6},{2,0},{4,2},{6,4},{1,7},{3,1},{5,3},{7,5},{8,14},{10,8},{12,... | collective-permute-start | bytes 786440 | tf_op jit(solution)/shard_map/ppermute | solution.py:578
  346.1 11.9 %collective-permute-start.43 = (bf16[1,512,512]{2,1,0:T(8,128)(2,1)S(1)}, bf16[1,512,512]{2,1,0:T(8,128)(2,1)S(1)}, u32[]{:S(2)}, u32[]{:S(2)}) collective-permute-start(bf16[1,512,512]{2,1,0:T(8,128)(2,1)S(1)} %get-tuple-element.225), channel_id=1, source_target_pairs={{0,16},{8,24},{16,0},{24,8},{1,17},{9,25},{17,1},{25,9},{2,18},{10... | collective-permute-start | bytes 1572872 | tf_op jit(solution)/shard_map/ppermute | solution.py:573
  348.0 10.9 %collective-permute-start.44 = (bf16[1,512,512]{2,1,0:T(8,128)(2,1)S(1)}, bf16[1,512,512]{2,1,0:T(8,128)(2,1)S(1)}, u32[]{:S(2)}, u32[]{:S(2)}) collective-permute-start(bf16[1,512,512]{2,1,0:T(8,128)(2,1)S(1)} %get-tuple-element.226), channel_id=1, source_target_pairs={{0,8},{8,0},{16,24},{24,16},{1,9},{9,1},{17,25},{25,17},{2,10},{10... | collective-permute-start | bytes 1572872 | tf_op jit(solution)/shard_map/ppermute | solution.py:573
  358.9 6.2 %collective-permute-start.52 = (f32[144,128]{1,0:T(8,128)S(1)}, f32[144,128]{1,0:T(8,128)S(1)}, u32[]{:S(2)}, u32[]{:S(2)}) collective-permute-start(f32[144,128]{1,0:T(8,128)S(1)} %pad_maximum_fusion.3), channel_id=1, source_target_pairs={{0,24},{8,16},{16,8},{24,0},{1,25},{9,17},{17,9},{25,1},{2,26},{10... | collective-permute-start | bytes 221192 | tf_op jit(solution)/shard_map/ppermute | solution.py:573
  360.5 6.1 %collective-permute-start.51 = (f32[144,128]{1,0:T(8,128)S(1)}, f32[144,128]{1,0:T(8,128)S(1)}, u32[]{:S(2)}, u32[]{:S(2)}) collective-permute-start(f32[144,128]{1,0:T(8,128)S(1)} %pad_maximum_fusion.3), channel_id=1, source_target_pairs={{0,16},{8,24},{16,0},{24,8},{1,17},{9,25},{17,1},{25,9},{2,18},{10... | collective-permute-start | bytes 221192 | tf_op jit(solution)/shard_map/ppermute | solution.py:573
  361.8 6.8 %collective-permute-start.50 = (f32[144,128]{1,0:T(8,128)S(1)}, f32[144,128]{1,0:T(8,128)S(1)}, u32[]{:S(2)}, u32[]{:S(2)}) collective-permute-start(f32[144,128]{1,0:T(8,128)S(1)} %pad_maximum_fusion.3), channel_id=1, source_target_pairs={{0,8},{8,0},{16,24},{24,16},{1,9},{9,1},{17,25},{25,17},{2,10},{10... | collective-permute-start | bytes 221192 | tf_op jit(solution)/shard_map/ppermute | solution.py:573
  362.4 10.0 %collective-permute-start.53 = (bf16[1,256,1152]{2,1,0:T(8,128)(2,1)S(1)}, bf16[1,256,1152]{2,1,0:T(8,128)(2,1)S(1)}, u32[]{:S(2)}, u32[]{:S(2)}) collective-permute-start(bf16[1,256,1152]{2,1,0:T(8,128)(2,1)S(1)} %get-tuple-element.235), channel_id=1, source_target_pairs={{0,16},{8,24},{16,0},{24,8},{1,17},{9,25},{17,1},{25,9},{2,18},{10... | collective-permute-start | bytes 1769480 | tf_op jit(solution)/shard_map/ppermute | solution.py:573
  363.7 9.9 %collective-permute-start.54 = (bf16[1,256,1152]{2,1,0:T(8,128)(2,1)S(1)}, bf16[1,256,1152]{2,1,0:T(8,128)(2,1)S(1)}, u32[]{:S(2)}, u32[]{:S(2)}) collective-permute-start(bf16[1,256,1152]{2,1,0:T(8,128)(2,1)S(1)} %get-tuple-element.236), channel_id=1, source_target_pairs={{0,8},{8,0},{16,24},{24,16},{1,9},{9,1},{17,25},{25,17},{2,10},{10... | collective-permute-start | bytes 1769480 | tf_op jit(solution)/shard_map/ppermute | solution.py:573
  365.2 14.6 %collective-permute-start.62 = (bf16[1,1024,128]{2,1,0:T(8,128)(2,1)S(1)}, bf16[1,1024,128]{2,1,0:T(8,128)(2,1)S(1)}, u32[]{:S(2)}, u32[]{:S(2)}) collective-permute-start(bf16[1,1024,128]{2,1,0:T(8,128)(2,1)S(1)} %get-tuple-element.335), channel_id=1, source_target_pairs={{0,2},{2,4},{4,6},{6,0},{1,3},{3,5},{5,7},{7,1},{8,10},{10,12},{12... | collective-permute-start | bytes 786440 | tf_op jit(solution)/shard_map/ppermute | solution.py:578
  366.5 20.8 %collective-permute-start.63 = (bf16[1,1024,128]{2,1,0:T(8,128)(2,1)S(1)}, bf16[1,1024,128]{2,1,0:T(8,128)(2,1)S(1)}, u32[]{:S(2)}, u32[]{:S(2)}) collective-permute-start(bf16[1,1024,128]{2,1,0:T(8,128)(2,1)S(1)} %get-tuple-element.336), channel_id=1, source_target_pairs={{0,4},{2,6},{4,0},{6,2},{1,5},{3,7},{5,1},{7,3},{8,12},{10,14},{12... | collective-permute-start | bytes 786440 | tf_op jit(solution)/shard_map/ppermute | solution.py:578
  368.6 25.3 %collective-permute-start.64 = (bf16[1,1024,128]{2,1,0:T(8,128)(2,1)S(1)}, bf16[1,1024,128]{2,1,0:T(8,128)(2,1)S(1)}, u32[]{:S(2)}, u32[]{:S(2)}) collective-permute-start(bf16[1,1024,128]{2,1,0:T(8,128)(2,1)S(1)} %get-tuple-element.333), channel_id=1, source_target_pairs={{0,6},{2,0},{4,2},{6,4},{1,7},{3,1},{5,3},{7,5},{8,14},{10,8},{12,... | collective-permute-start | bytes 786440 | tf_op jit(solution)/shard_map/ppermute | solution.py:578
  373.6 23.0 %collective-permute-start.57 = (f32[144,128]{1,0:T(8,128)S(1)}, f32[144,128]{1,0:T(8,128)S(1)}, u32[]{:S(2)}, u32[]{:S(2)}) collective-permute-start(f32[144,128]{1,0:T(8,128)S(1)} %add_add_fusion.1), channel_id=1, source_target_pairs={{0,6},{2,0},{4,2},{6,4},{1,7},{3,1},{5,3},{7,5},{8,14},{10,8},{12,... | collective-permute-start | bytes 221192 | tf_op jit(solution)/shard_map/ppermute | solution.py:578
  379.1 18.0 %collective-permute-start.56 = (f32[144,128]{1,0:T(8,128)S(1)}, f32[144,128]{1,0:T(8,128)S(1)}, u32[]{:S(2)}, u32[]{:S(2)}) collective-permute-start(f32[144,128]{1,0:T(8,128)S(1)} %add_add_fusion.1), channel_id=1, source_target_pairs={{0,4},{2,6},{4,0},{6,2},{1,5},{3,7},{5,1},{7,3},{8,12},{10,14},{12... | collective-permute-start | bytes 221192 | tf_op jit(solution)/shard_map/ppermute | solution.py:578
  379.9 17.2 %collective-permute-start.55 = (f32[144,128]{1,0:T(8,128)S(1)}, f32[144,128]{1,0:T(8,128)S(1)}, u32[]{:S(2)}, u32[]{:S(2)}) collective-permute-start(f32[144,128]{1,0:T(8,128)S(1)} %add_add_fusion.1), channel_id=1, source_target_pairs={{0,2},{2,4},{4,6},{6,0},{1,3},{3,5},{5,7},{7,1},{8,10},{10,12},{12... | collective-permute-start | bytes 221192 | tf_op jit(solution)/shard_map/ppermute | solution.py:578
  387.4 15.8 %collective-permute-start.60 = (bf16[128,1152]{1,0:T(8,128)(2,1)}, bf16[128,1152]{1,0:T(8,128)(2,1)S(1)}, u32[]{:S(2)}, u32[]{:S(2)}) collective-permute-start(bf16[128,1152]{1,0:T(8,128)(2,1)} %get-tuple-element.243), channel_id=1, source_target_pairs={{0,6},{2,0},{4,2},{6,4},{1,7},{3,1},{5,3},{7,5},{8,14},{10,8},{12,... | collective-permute-start | bytes 884744 | tf_op jit(solution)/shard_map/ppermute | solution.py:578
  393.9 25.0 %collective-permute-start.59 = (bf16[128,1152]{1,0:T(8,128)(2,1)S(1)}, bf16[128,1152]{1,0:T(8,128)(2,1)S(1)}, u32[]{:S(2)}, u32[]{:S(2)}) collective-permute-start(bf16[128,1152]{1,0:T(8,128)(2,1)S(1)} %get-tuple-element.242), channel_id=1, source_target_pairs={{0,4},{2,6},{4,0},{6,2},{1,5},{3,7},{5,1},{7,3},{8,12},{10,14},{12... | collective-permute-start | bytes 884744 | tf_op jit(solution)/shard_map/ppermute | solution.py:578
  396.5 22.4 %collective-permute-start.58 = (bf16[128,1152]{1,0:T(8,128)(2,1)S(1)}, bf16[128,1152]{1,0:T(8,128)(2,1)}, u32[]{:S(2)}, u32[]{:S(2)}) collective-permute-start(bf16[128,1152]{1,0:T(8,128)(2,1)S(1)} %get-tuple-element.241), channel_id=1, source_target_pairs={{0,2},{2,4},{4,6},{6,0},{1,3},{3,5},{5,7},{7,1},{8,10},{10,12},{12... | collective-permute-start | bytes 884744 | tf_op jit(solution)/shard_map/ppermute | solution.py:578
  420.1 2.9 collective-permute-start.61
  (70 other events, 687.6 us)
